TPU v7x, 256 devices: a whole 4x4x8 slice. The times are simulated.
256 devices in a mesh: enc: 8 (over y, core), exp: 32 (over x, z).
Axes of the slice: x: 4, y: 4, z: 8, core: 2. Of those that a mesh axis runs over, the one named last changes fastest.
Arguments:
- tokens: bfloat16 [4096, 4096], P('exp'), may hold values from -61 to 61
- norm_gain: bfloat16 [4096], replicated, may hold values from 0.099609375 to 1.8984375
- router: bfloat16 [64, 4096], replicated, may hold values from -0.09375 to 0.09375
- routes: int32 [4096, 8], P('exp'), may hold values from 0 to 63, all different within a row; in each aligned block of 128 rows (0 to 127, 128 to 255, ...) at most 32 rows name the same one
- w_gate: bfloat16 [64, 1536, 4096], P('exp', 'enc'), may hold values from -0.09375 to 0.09375
- w_up: bfloat16 [64, 1536, 4096], P('exp', 'enc'), may hold values from -0.09375 to 0.09375
- w_down: bfloat16 [64, 1536, 4096], P('exp', None, 'enc'), may hold values from -0.15625 to 0.15625
Outputs:
- mixed: bfloat16 [4096, 4096], P('exp', 'enc')
Inputs may be any that keep to these rules, and one draw needn't show every extreme that they name: `routes`: each row names 8 different experts. In the rows of one owner (128 rows, aligned), no expert is named more than 32 times, a bound that some block reaches.
All inputs are finite; a program needn't handle non-finite values.
Results may differ from a plain program's by a relative error of at most 0.024.
Values may be sent and summed in bfloat16 or wider, within the bound.
No kernel may reach another device: no remote copies, remote signals or barrier semaphores. Data moves between devices by JAX's collectives and lax.ppermute only.
A program may use at most 128 MiB of HBM per device.

v0:
```python
import jax
import jax.numpy as jnp
from jax import lax
from jax.sharding import PartitionSpec as P

EPS = 1e-06


def by_rows(left, right):
    return lax.dot_general(
        left, right, (((1,), (1,)), ((), ())), preferred_element_type=jnp.float32
    )


def body(tokens, norm_gain, router, routes, w_gate, w_up, w_down):
    tok_rows, width = tokens.shape
    experts = router.shape[0]
    top_count = routes.shape[1]
    exp_local = w_gate.shape[0]
    out_cols = w_down.shape[2]
    capacity = 2 * tok_rows * top_count // experts
    values = tokens.astype(jnp.float32)
    scaled = (values * norm_gain.astype(jnp.float32)).astype(jnp.bfloat16)
    squares = jnp.sum(values * values, axis=1, keepdims=True)
    inverse = lax.rsqrt(squares / width + EPS)
    logits = by_rows(scaled, router) * inverse
    normed = (scaled.astype(jnp.float32) * inverse).astype(jnp.bfloat16)
    labels = lax.broadcasted_iota(jnp.int32, (1, 1, experts), 2)
    chosen_mask = routes[:, :, None] == labels
    chosen = jnp.sum(jnp.where(chosen_mask, logits[:, None, :], 0.0), axis=2)
    raised = jnp.exp(chosen)
    weights = raised / jnp.sum(raised, axis=1, keepdims=True)
    hit_count = jnp.sum(chosen_mask.astype(jnp.int32), axis=1)
    before = jnp.cumsum(hit_count, axis=0) - hit_count
    position = jnp.take_along_axis(before, routes, axis=1)
    slot_index = routes * capacity + position
    outgoing = jnp.zeros((experts * capacity, width), jnp.bfloat16)
    outgoing = outgoing.at[slot_index.reshape(-1)].set(jnp.repeat(normed, top_count, axis=0))
    outgoing = outgoing.reshape(experts // exp_local, exp_local, capacity, width)
    received = lax.all_to_all(outgoing, "exp", split_axis=0, concat_axis=0, tiled=True)
    results = []
    for member in range(exp_local):
        slot_rows = received[:, member].reshape(-1, width)
        gate_part = by_rows(slot_rows, w_gate[member])
        up_part = by_rows(slot_rows, w_up[member])
        hidden = (jax.nn.silu(gate_part) * up_part).astype(jnp.bfloat16)
        down_rows = w_down[member]

        def add_segment(running, segment, offset, down_rows=down_rows):
            return jnp.dot(segment, down_rows, preferred_element_type=jnp.float32)

        starting = jnp.zeros((hidden.shape[0], out_cols), jnp.float32)
        result = add_segment(
            starting, lax.all_gather(hidden, "enc", axis=1, tiled=True), jnp.int32(0)
        )
        results.append(result.astype(jnp.bfloat16).reshape(received.shape[0], -1, out_cols))
    processed = jnp.stack(results, axis=1)
    returned = lax.all_to_all(processed, "exp", split_axis=0, concat_axis=0, tiled=True)
    back_rows = returned.reshape(-1, out_cols)
    gathered = back_rows[slot_index].astype(jnp.float32)
    mixed = jnp.sum(weights[:, :, None] * gathered, axis=1)
    return mixed.astype(jnp.bfloat16)


def solution(mesh):
    return jax.shard_map(
        body,
        mesh=mesh,
        in_specs=(
            P("exp", None),
            P(),
            P(),
            P("exp", None),
            P("exp", "enc", None),
            P("exp", "enc", None),
            P("exp", None, "enc"),
        ),
        out_specs=P("exp", "enc"),
        check_vma=False,
    )
```

profile of v0, /device:TPU:1, one launch (start us, length us, event | category | flops | bytes accessed | tf_op | source)
XLA Modules:
  0.0 564.4 jit_solution(4604874824618915482)
XLA Ops:
  6.5 0.8 convert_reduce_fusion
  7.3 0.7 bitcast_or_fusion
  8.5 7.1 %gather_fusion.1 = s32[1024]{0:T(1024)S(1)} fusion(s32[128,64]{1,0:T(8,128)S(1)} %sub.3, s32[1024]{0:T(1024)S(1)} %reshape.92), kind=kCustom, calls=%fused_computation.1 | custom fusion | bytes 16384 | tf_op jit(solution)/shard_map/jit(take_along_axis)/gather | solution.py:35
  16.0 0.3 fusion.5
  16.3 0.3 multiply_convert_fusion
  16.6 20.3 %scatter_custom_fusion = bf16[2048,4096]{1,0:T(8,128)(2,1)} fusion(s32[1024]{0:T(1024)S(1)} %bitcast.66, bf16[]{:T(256)} %constant.15.clone.1, bf16[128,4096]{1,0:T(8,128)(2,1)S(1)} %multiply_convert_fusion), kind=kCustom, calls=%fused_computation.3 | custom fusion | bytes 17825794 | tf_op jit(solution)/shard_map/scatter | solution.py:38
  37.0 373.5 %all_to_all.10 = bf16[32,2,32,4096]{3,2,1,0:T(8,128)(2,1)S(1)} all-to-all(bf16[32,2,32,4096]{3,2,1,0:T(8,128)(2,1)} %bitcast.58), channel_id=1, replica_groups=mesh['enc'=8,'exp'=32] {'exp'}, dimensions={0} | all-to-all | bytes 33554432 | tf_op jit(solution)/shard_map/all_to_all | solution.py:40
  410.5 4.3 fusion.44
  414.8 2.9 fusion.17
  417.7 3.8 fusion.40
  421.6 0.3 all-gather.5.cloned.1.call-start
  421.9 6.8 %fusion.11 = f32[1024,192]{0,1:T(8,128)S(1)} fusion(bf16[1024,4096]{1,0:T(8,128)(2,1)} %bitcast.60, bf16[2,192,4096]{2,1,0:T(8,128)(2,1)} %param.11), kind=kOutput, calls=%fused_computation.19 | convolution fusion | flops 1610612736 | bytes 10747904 | tf_op jit(solution)/shard_map/dot_general | solution.py:10
  428.7 0.2 copy-done.7
  429.0 3.7 fusion.37
  432.6 20.9 %all-gather.3.cloned.1.call-done = bf16[1024,1536]{0,1:T(8,128)(2,1)} async-done(((bf16[1024,192]{0,1:T(8,128)(2,1)}), bf16[1024,1536]{0,1:T(8,128)(2,1)}) %all-gather.3.cloned.1.call-update) | async-done | bytes 3145744 | tf_op jit(solution)/shard_map/all_gather | solution.py:54
  453.5 4.2 fusion.25
  457.7 28.1 %all-gather.5.cloned.1.call-done = bf16[1024,1536]{0,1:T(8,128)(2,1)} async-done(((bf16[1024,192]{0,1:T(8,128)(2,1)}), bf16[1024,1536]{0,1:T(8,128)(2,1)}) %all-gather.5.cloned.1.call-update) | async-done | bytes 3145744 | tf_op jit(solution)/shard_map/all_gather | solution.py:54
  485.7 4.2 fusion.28
  489.9 1.6 pad_maximum_fusion
  491.5 9.5 %all-to-all-start.1 = ((bf16[32,2,32,512]{3,2,1,0:T(8,128)(2,1)}), bf16[32,2,32,512]{3,2,1,0:T(8,128)(2,1)S(1)}, u32[]{:S(2)}, u32[]{:S(2)}) async-start(bf16[32,2,32,512]{3,2,1,0:T(8,128)(2,1)} %pad_maximum_fusion), calls=%async_computation.1 | async-start | bytes 4194304 | tf_op jit(solution)/shard_map/all_to_all | solution.py:58
  501.2 1.7 convolution_multiply_fusion
  503.1 46.8 %all-to-all-done.1 = bf16[32,2,32,512]{3,2,1,0:T(8,128)(2,1)S(1)} async-done(((bf16[32,2,32,512]{3,2,1,0:T(8,128)(2,1)}), bf16[32,2,32,512]{3,2,1,0:T(8,128)(2,1)S(1)}, u32[]{:S(2)}, u32[]{:S(2)}) %all-to-all-start.1) | async-done | bytes 2097184 | tf_op jit(solution)/shard_map/all_to_all | solution.py:58
  549.9 5.1 gather_fusion
  555.0 2.6 fusion.6
  (38 shorter events, 1.3 us)
Async XLA Ops:
  6.5 494.7 %copy-start = (bf16[64,4096]{1,0:T(8,128)(2,1)S(1)}, bf16[64,4096]{1,0:T(8,128)(2,1)}, u32[]{:S(2)}) copy-start(bf16[64,4096]{1,0:T(8,128)(2,1)} %param.9) | copy-start | bytes 1572868
  6.5 447.0 %all-gather.3.cloned.1.call-start = ((), (), s32[]{:S(2)}) async-start(), calls=%async_computation.2 | async-start | bytes 3538944 | tf_op jit(solution)/shard_map/all_gather | solution.py:54
  8.5 7.3 %copy-start.3 = (s32[128,8]{0,1:T(8,128)S(1)}, s32[128,8]{0,1:T(8,128)}, u32[]{:S(2)}) copy-start(s32[128,8]{0,1:T(8,128)} %param.10) | copy-start | bytes 12292
  8.5 7.5 %copy-start.4 = (bf16[4096]{0:T(1024)(128)(2,1)S(1)}, bf16[4096]{0:T(1024)(128)(2,1)}, u32[]{:S(2)}) copy-start(bf16[4096]{0:T(1024)(128)(2,1)} %param.8) | copy-start | bytes 24580
  8.5 7.5 %copy-start.2 = (bf16[128,4096]{1,0:T(8,128)(2,1)S(1)}, bf16[128,4096]{1,0:T(8,128)(2,1)}, u32[]{:S(2)}) copy-start(bf16[128,4096]{1,0:T(8,128)(2,1)} %param.7) | copy-start | bytes 3145732
  410.5 4.3 copy-start.5
  414.8 2.9 copy-start.6
  421.6 64.2 %all-gather.5.cloned.1.call-start = ((), (), s32[]{:S(2)}) async-start(), calls=%async_computation.3 | async-start | bytes 3538944 | tf_op jit(solution)/shard_map/all_gather | solution.py:54
  421.8 6.9 %copy-start.1 = (bf16[32,1,32,4096]{3,2,1,0:T(8,128)(2,1)S(1)}, bf16[32,1,32,4096]{3,2,1,0:T(8,128)(2,1)}, u32[]{:S(2)}) copy-start(bf16[32,1,32,4096]{3,2,1,0:T(8,128)(2,1)} %get-tuple-element.8) | copy-start | bytes 25165828
  421.8 7.1 %copy-start.7 = (bf16[2,192,4096]{2,1,0:T(8,128)(2,1)S(1)}, bf16[2,192,4096]{2,1,0:T(8,128)(2,1)}, u32[]{:S(2)}) copy-start(bf16[2,192,4096]{2,1,0:T(8,128)(2,1)} %param.12) | copy-start | bytes 9437188
  491.5 58.5 %all-to-all-start.1 = ((bf16[32,2,32,512]{3,2,1,0:T(8,128)(2,1)}), bf16[32,2,32,512]{3,2,1,0:T(8,128)(2,1)S(1)}, u32[]{:S(2)}, u32[]{:S(2)}) async-start(bf16[32,2,32,512]{3,2,1,0:T(8,128)(2,1)} %pad_maximum_fusion), calls=%async_computation.1 | async-start | bytes 4194304 | tf_op jit(solution)/shard_map/all_to_all | solution.py:58
Sparse Core Ops, SparseCore 0:
  421.7 31.7 all-gather.2
  455.3 30.3 all-gather.4
where the time goes:
time: 565 us; the launch traced here: 564 us
  blocking collectives  374 us (66%)
  waiting for transfers between devices  95.7 us (17%)
  local copies, waits for them, and re-layouts  38 us (7%)
  matrix products  27.3 us (5%)
  between operations  13.6 us (2%)
  starting transfers between devices  9.79 us (2%)
  other arithmetic  6.51 us (1%)
    all_to_all x1, blocking collectives, body(): lax.all_to_all(outgoing, 'exp', split_axis=0, concat_axis=0, tiled=True)  374 us
    all_gather x2, waiting for transfers between devices, body(): lax.all_gather(hidden, 'enc', axis=1, tiled=True)  48.9 us
    all_to_all x1, waiting for transfers between devices, body(): lax.all_to_all(processed, 'exp', split_axis=0, concat_axis=0, tiled=True)  46.8 us
    scatter x1, local copies, waits for them, and re-layouts, body(): outgoing.at[slot_index.reshape(-1)]  20.3 us
    dot_general x5, matrix products, by_rows(): lax.dot_general(left, right, (((1,), (1,)), ((), ())), preferred_element_...  18.9 us
  transfers between devices with their start and end apart: 3, of which 3 were waited for; matrix products, arithmetic and copies ran while one was open for 3% of the time, Pallas kernels for 0%

commit v1 on v0

v1 whole, which is shorter than its diff:
```python
import jax
import jax.numpy as jnp
from jax import lax
from jax.sharding import PartitionSpec as P

EPS = 1e-06


def by_rows(left, right):
    return lax.dot_general(
        left, right, (((1,), (1,)), ((), ())), preferred_element_type=jnp.float32
    )


def body(tokens, norm_gain, router, routes, w_gate, w_up, w_down):
    tok_rows, width = tokens.shape
    experts = router.shape[0]
    top_count = routes.shape[1]
    exp_local = w_gate.shape[0]
    out_cols = w_down.shape[2]
    n_exp = experts // exp_local
    capacity = 2 * tok_rows * top_count // experts
    values = tokens.astype(jnp.float32)
    scaled = (values * norm_gain.astype(jnp.float32)).astype(jnp.bfloat16)
    squares = jnp.sum(values * values, axis=1, keepdims=True)
    inverse = lax.rsqrt(squares / width + EPS)
    start = lax.axis_index("enc") * out_cols
    part = lax.dynamic_slice(scaled, (0, start), (tok_rows, out_cols))
    normed = (part.astype(jnp.float32) * inverse).astype(jnp.bfloat16)

    routes_t = routes.T
    labels = lax.broadcasted_iota(jnp.int32, (experts, 1, 1), 0)
    chosen_t = routes_t[None] == labels
    mask_t = jnp.any(chosen_t, axis=1)
    row = lax.broadcasted_iota(jnp.int32, (tok_rows, tok_rows), 0)
    col = lax.broadcasted_iota(jnp.int32, (tok_rows, tok_rows), 1)
    earlier = (row < col).astype(jnp.bfloat16)
    before = jnp.dot(
        mask_t.astype(jnp.bfloat16), earlier, preferred_element_type=jnp.float32
    ).astype(jnp.int32)
    place = jnp.where(mask_t, before, -1)
    slots = lax.broadcasted_iota(jnp.int32, (1, capacity, 1), 1)
    select = place[:, None, :] == slots
    pick = select.astype(jnp.bfloat16).reshape(n_exp, exp_local, capacity, tok_rows)

    received = []
    for member in range(exp_local):
        rows = jnp.dot(
            pick[:, member].reshape(n_exp * capacity, tok_rows),
            normed,
            preferred_element_type=jnp.float32,
        ).astype(jnp.bfloat16)
        received.append(
            lax.all_to_all(rows, "exp", split_axis=0, concat_axis=0, tiled=True)
        )

    logits = by_rows(scaled, router) * inverse
    logits_t = logits.T
    chosen = jnp.sum(jnp.where(chosen_t, logits_t[:, None, :], 0.0), axis=0)
    raised = jnp.exp(chosen)
    weights = raised / jnp.sum(raised, axis=0, keepdims=True)
    dense = jnp.sum(jnp.where(chosen_t, weights[None], 0.0), axis=1)
    mix = jnp.where(select, dense[:, None, :], 0.0).astype(jnp.bfloat16)
    mix = mix.reshape(n_exp, exp_local, capacity, tok_rows)

    total = None
    for member in range(exp_local):
        slot_rows = lax.all_gather(received[member], "enc", axis=1, tiled=True)
        gate_part = by_rows(slot_rows, w_gate[member])
        up_part = by_rows(slot_rows, w_up[member])
        hidden = (jax.nn.silu(gate_part) * up_part).astype(jnp.bfloat16)
        full = lax.all_gather(hidden, "enc", axis=1, tiled=True)
        result = jnp.dot(full, w_down[member], preferred_element_type=jnp.float32)
        back = lax.all_to_all(
            result.astype(jnp.bfloat16), "exp", split_axis=0, concat_axis=0, tiled=True
        )
        share = lax.dot_general(
            mix[:, member].reshape(n_exp * capacity, tok_rows),
            back,
            (((0,), (0,)), ((), ())),
            preferred_element_type=jnp.float32,
        )
        total = share if total is None else total + share
    return total.astype(jnp.bfloat16)


def solution(mesh):
    return jax.shard_map(
        body,
        mesh=mesh,
        in_specs=(
            P("exp", None),
            P(),
            P(),
            P("exp", None),
            P("exp", "enc", None),
            P("exp", "enc", None),
            P("exp", None, "enc"),
        ),
        out_specs=P("exp", "enc"),
        check_vma=False,
    )
```

time: 565 us -> 273 us (0.48)
  blocking collectives: 374 us -> 69.7 us
  local copies, waits for them, and re-layouts: 38 us -> 0.58 us
  waiting for transfers between devices: 95.7 us -> 128 us
  starting transfers between devices: 9.79 us -> 18.1 us
  matrix products: 27.3 us -> 35.6 us
    all_to_all x1 -> x2, blocking collectives: 374 us -> 69.7 us  [body(): lax.all_to_all(rows, 'exp', split_axis=0, concat_axis=0, tiled=True)]
    all_gather x2 -> x4, waiting for transfers between devices: 48.9 us -> 102 us  [the longest x2 63.3 us: body(): slot_rows = lax.all_gather(received[member], 'enc', axis=1, tiled=True)]
    all_to_all x1 -> x2, waiting for transfers between devices: 46.8 us -> 26.1 us  [body(): lax.all_to_all(result.astype(jnp.bfloat16), 'exp', split_axis=0, concat_a...]
    scatter x1 -> x0, local copies, waits for them, and re-layouts: 20.3 us -> none  [body(): outgoing.at[slot_index.reshape(-1)]]
    gather x6 -> x0, local copies, waits for them, and re-layouts: 12.5 us -> none  [the longest x5 7.39 us: body(): position = jnp.take_along_axis(before, routes, axis=1)]
    all_to_all x1 -> x2, starting transfers between devices: 9.53 us -> 17.8 us  [body(): lax.all_to_all(result.astype(jnp.bfloat16), 'exp', split_axis=0, concat_a...]
    dot_general x2 -> x7, matrix products: 8.35 us -> 14 us  [the longest x2 10.3 us: body(): result = jnp.dot(full, w_down[member], preferred_element_type=jnp.float32)]
  transfers between devices with their start and end apart: 3 -> 6, of which waited for: 3 -> 6; matrix products, arithmetic and copies ran while one was open for 3% -> 12% of each run, Pallas kernels for 0% -> 0%
where the time goes in v1:
time: 273 us; the launch traced here: 269 us
  waiting for transfers between devices  128 us (47%)
  blocking collectives  69.7 us (26%)
  matrix products  35.6 us (13%)
  starting transfers between devices  18.1 us (7%)
  between operations  13.3 us (5%)
  other arithmetic  3.73 us (1%)
    all_to_all x2, blocking collectives, body(): lax.all_to_all(rows, 'exp', split_axis=0, concat_axis=0, tiled=True)  69.7 us
    all_gather x2, waiting for transfers between devices, body(): slot_rows = lax.all_gather(received[member], 'enc', axis=1, tiled=True)  63.3 us
    all_gather x2, waiting for transfers between devices, body(): full = lax.all_gather(hidden, 'enc', axis=1, tiled=True)  38.9 us
    all_to_all x2, waiting for transfers between devices, body(): lax.all_to_all(result.astype(jnp.bfloat16), 'exp', split_axis=0, concat_a...  26.1 us
    dot_general x5, matrix products, by_rows(): lax.dot_general(left, right, (((1,), (1,)), ((), ())), preferred_element_...  21.6 us
    all_to_all x2, starting transfers between devices, body(): lax.all_to_all(result.astype(jnp.bfloat16), 'exp', split_axis=0, concat_a...  17.8 us
    dot_general x2, matrix products, body(): result = jnp.dot(full, w_down[member], preferred_element_type=jnp.float32)  10.3 us
  transfers between devices with their start and end apart: 6, of which 6 were waited for; matrix products, arithmetic and copies ran while one was open for 12% of the time, Pallas kernels for 0%

profile of v1, /device:TPU:1, one launch (start us, length us, event | category | flops | bytes accessed | tf_op | source)
XLA Modules:
  0.0 269.3 jit_solution(16162365168234129186)
XLA Ops:
  6.5 0.8 fusion.41
  7.7 0.7 convert_element_type.48
  8.4 1.6 fusion.1
  10.1 0.5 convolution_convert_fusion.1
  10.6 36.4 %all_to_all.48 = bf16[32,32,512]{2,1,0:T(8,128)(2,1)} all-to-all(bf16[32,32,512]{2,1,0:T(8,128)(2,1)S(1)} %bitcast.66), channel_id=1, replica_groups=mesh['enc'=8,'exp'=32] {'exp'}, dimensions={0} | all-to-all | bytes 2097152 | tf_op jit(solution)/shard_map/all_to_all | solution.py:54
  47.1 0.5 convolution_convert_fusion
  47.6 33.3 %all_to_all.49 = bf16[32,32,512]{2,1,0:T(8,128)(2,1)} all-to-all(bf16[32,32,512]{2,1,0:T(8,128)(2,1)S(1)} %bitcast.65), channel_id=1, replica_groups=mesh['enc'=8,'exp'=32] {'exp'}, dimensions={0} | all-to-all | bytes 2097152 | tf_op jit(solution)/shard_map/all_to_all | solution.py:54
  80.9 20.0 %all-gather.5.cloned.1.call-done = bf16[1024,4096]{1,0:T(8,128)(2,1)} async-done(((bf16[1024,512]{1,0:T(8,128)(2,1)}), bf16[1024,4096]{1,0:T(8,128)(2,1)}) %all-gather.5.cloned.1.call-update) | async-done | bytes 8388624 | tf_op jit(solution)/shard_map/all_gather | solution.py:68
  100.9 6.8 %fusion.12 = f32[1024,192]{0,1:T(8,128)S(1)} fusion(bf16[1024,4096]{1,0:T(8,128)(2,1)} %all-gather.5.cloned.1.call-done, bf16[2,192,4096]{2,1,0:T(8,128)(2,1)} %param.11), kind=kOutput, calls=%fused_computation.14 | convolution fusion | flops 1610612736 | bytes 10747904 | tf_op jit(solution)/shard_map/dot_general | solution.py:10
  108.0 3.7 %fusion.35 = bf16[1024,192]{0,1:T(8,128)(2,1)} fusion(bf16[1024,4096]{1,0:T(8,128)(2,1)S(1)} %copy-done.3, bf16[2,192,4096]{2,1,0:T(8,128)(2,1)S(1)} %copy-done.4, f32[1024,192]{0,1:T(8,128)S(1)} %fusion.12), kind=kOutput, calls=%fused_computation.29 | convolution fusion | flops 1611792384 | bytes 11141120 | tf_op jit(solution)/shard_map/dot_general | solution.py:10
  112.0 43.3 %all-gather.9.cloned.1.call-done = bf16[1024,4096]{1,0:T(8,128)(2,1)} async-done(((bf16[1024,512]{1,0:T(8,128)(2,1)}), bf16[1024,4096]{1,0:T(8,128)(2,1)}) %all-gather.9.cloned.1.call-update) | async-done | bytes 8388624 | tf_op jit(solution)/shard_map/all_gather | solution.py:68
  155.3 6.8 %fusion.6 = f32[1024,192]{0,1:T(8,128)S(1)} fusion(bf16[1024,4096]{1,0:T(8,128)(2,1)} %all-gather.9.cloned.1.call-done, bf16[2,192,4096]{2,1,0:T(8,128)(2,1)} %param.11), kind=kOutput, calls=%fused_computation.8 | convolution fusion | flops 1610612736 | bytes 10747904 | tf_op jit(solution)/shard_map/dot_general | solution.py:10
  162.4 3.7 %fusion.32 = bf16[1024,192]{0,1:T(8,128)(2,1)} fusion(bf16[1024,4096]{1,0:T(8,128)(2,1)S(1)} %copy-done.2, bf16[2,192,4096]{2,1,0:T(8,128)(2,1)S(1)} %copy-done.5, f32[1024,192]{0,1:T(8,128)S(1)} %fusion.6), kind=kOutput, calls=%fused_computation.28 | convolution fusion | flops 1611792384 | bytes 11141120 | tf_op jit(solution)/shard_map/dot_general | solution.py:10
  166.1 21.6 %all-gather.7.cloned.1.call-done = bf16[1024,1536]{0,1:T(8,128)(2,1)} async-done(((bf16[1024,192]{0,1:T(8,128)(2,1)}), bf16[1024,1536]{0,1:T(8,128)(2,1)}) %all-gather.7.cloned.1.call-update) | async-done | bytes 3145744 | tf_op jit(solution)/shard_map/all_gather | solution.py:72
  187.6 5.2 %fusion.20 = bf16[1024,512]{1,0:T(8,128)(2,1)} fusion(bf16[1024,1536]{0,1:T(8,128)(2,1)} %all-gather.7.cloned.1.call-done, bf16[2,1536,512]{2,1,0:T(8,128)(2,1)} %param.13), kind=kOutput, calls=%fused_computation.22 | convolution fusion | flops 1611137024 | bytes 5767168 | tf_op jit(solution)/shard_map/dot_general | solution.py:73
  192.8 9.5 %all-to-all-start.1 = ((bf16[32,32,512]{2,1,0:T(8,128)(2,1)}), bf16[32,32,512]{2,1,0:T(8,128)(2,1)S(1)}, u32[]{:S(2)}, u32[]{:S(2)}) async-start(bf16[32,32,512]{2,1,0:T(8,128)(2,1)} %bitcast.68), calls=%async_computation.1 | async-start | bytes 2097152 | tf_op jit(solution)/shard_map/all_to_all | solution.py:74
  202.4 17.4 %all-gather.11.cloned.1.call-done = bf16[1024,1536]{0,1:T(8,128)(2,1)} async-done(((bf16[1024,192]{0,1:T(8,128)(2,1)}), bf16[1024,1536]{0,1:T(8,128)(2,1)}) %all-gather.11.cloned.1.call-update) | async-done | bytes 3145744 | tf_op jit(solution)/shard_map/all_gather | solution.py:72
  219.7 5.1 %fusion.23 = bf16[1024,512]{1,0:T(8,128)(2,1)} fusion(bf16[1024,1536]{0,1:T(8,128)(2,1)} %all-gather.11.cloned.1.call-done, bf16[2,1536,512]{2,1,0:T(8,128)(2,1)} %param.13), kind=kOutput, calls=%fused_computation.23 | convolution fusion | flops 1611137024 | bytes 5767168 | tf_op jit(solution)/shard_map/dot_general | solution.py:73
  224.9 2.7 all-to-all-done.1
  227.5 8.2 %all-to-all-start.3 = ((bf16[32,32,512]{2,1,0:T(8,128)(2,1)}), bf16[32,32,512]{2,1,0:T(8,128)(2,1)}, u32[]{:S(2)}, u32[]{:S(2)}) async-start(bf16[32,32,512]{2,1,0:T(8,128)(2,1)} %bitcast.67), calls=%async_computation.3 | async-start | bytes 2097152 | tf_op jit(solution)/shard_map/all_to_all | solution.py:74
  235.8 0.5 fusion.39
  236.7 0.3 fusion.46
  237.1 23.5 %all-to-all-done.3 = bf16[32,32,512]{2,1,0:T(8,128)(2,1)} async-done(((bf16[32,32,512]{2,1,0:T(8,128)(2,1)}), bf16[32,32,512]{2,1,0:T(8,128)(2,1)}, u32[]{:S(2)}, u32[]{:S(2)}) %all-to-all-start.3) | async-done | bytes 1048608 | tf_op jit(solution)/shard_map/all_to_all | solution.py:74
  260.6 2.2 fusion.38
  (30 shorter events, 1.7 us)
Async XLA Ops:
  6.5 229.2 %copy-start = (bf16[64,4096]{1,0:T(8,128)(2,1)S(1)}, bf16[64,4096]{1,0:T(8,128)(2,1)}, u32[]{:S(2)}) copy-start(bf16[64,4096]{1,0:T(8,128)(2,1)} %param.9) | copy-start | bytes 1572868
  6.5 94.4 %all-gather.5.cloned.1.call-start = ((), (), s32[]{:S(2)}) async-start(), calls=%async_computation.4 | async-start | bytes 9437184 | tf_op jit(solution)/shard_map/all_gather | solution.py:68
  47.0 108.3 %all-gather.9.cloned.1.call-start = ((), (), s32[]{:S(2)}) async-start(), calls=%async_computation.6 | async-start | bytes 9437184 | tf_op jit(solution)/shard_map/all_gather | solution.py:68
  80.9 106.8 %all-gather.7.cloned.1.call-start = ((), (), s32[]{:S(2)}) async-start(), calls=%async_computation.5 | async-start | bytes 3538944 | tf_op jit(solution)/shard_map/all_gather | solution.py:72
  100.9 6.9 %copy-start.3 = (bf16[1024,4096]{1,0:T(8,128)(2,1)S(1)}, bf16[1024,4096]{1,0:T(8,128)(2,1)}, u32[]{:S(2)}) copy-start(bf16[1024,4096]{1,0:T(8,128)(2,1)} %all-gather.5.cloned.1.call-done) | copy-start | bytes 25165828
  100.9 7.1 %copy-start.4 = (bf16[2,192,4096]{2,1,0:T(8,128)(2,1)S(1)}, bf16[2,192,4096]{2,1,0:T(8,128)(2,1)}, u32[]{:S(2)}) copy-start(bf16[2,192,4096]{2,1,0:T(8,128)(2,1)} %param.12) | copy-start | bytes 9437188
  111.7 108.0 %all-gather.11.cloned.1.call-start = ((), (), s32[]{:S(2)}) async-start(), calls=%async_computation.7 | async-start | bytes 3538944 | tf_op jit(solution)/shard_map/all_gather | solution.py:72
  155.3 6.9 %copy-start.2 = (bf16[1024,4096]{1,0:T(8,128)(2,1)S(1)}, bf16[1024,4096]{1,0:T(8,128)(2,1)}, u32[]{:S(2)}) copy-start(bf16[1024,4096]{1,0:T(8,128)(2,1)} %all-gather.9.cloned.1.call-done) | copy-start | bytes 25165828
  155.3 7.1 %copy-start.5 = (bf16[2,192,4096]{2,1,0:T(8,128)(2,1)S(1)}, bf16[2,192,4096]{2,1,0:T(8,128)(2,1)}, u32[]{:S(2)}) copy-start(bf16[2,192,4096]{2,1,0:T(8,128)(2,1)} %param.12) | copy-start | bytes 9437188
  192.8 34.7 %all-to-all-start.1 = ((bf16[32,32,512]{2,1,0:T(8,128)(2,1)}), bf16[32,32,512]{2,1,0:T(8,128)(2,1)S(1)}, u32[]{:S(2)}, u32[]{:S(2)}) async-start(bf16[32,32,512]{2,1,0:T(8,128)(2,1)} %bitcast.68), calls=%async_computation.1 | async-start | bytes 2097152 | tf_op jit(solution)/shard_map/all_to_all | solution.py:74
  224.9 11.4 %copy-start.1 = (s32[128,8]{0,1:T(8,128)S(1)}, s32[128,8]{0,1:T(8,128)}, u32[]{:S(2)}) copy-start(s32[128,8]{0,1:T(8,128)} %param.10) | copy-start | bytes 12292
  227.5 33.0 %all-to-all-start.3 = ((bf16[32,32,512]{2,1,0:T(8,128)(2,1)}), bf16[32,32,512]{2,1,0:T(8,128)(2,1)}, u32[]{:S(2)}, u32[]{:S(2)}) async-start(bf16[32,32,512]{2,1,0:T(8,128)(2,1)} %bitcast.67), calls=%async_computation.3 | async-start | bytes 2097152 | tf_op jit(solution)/shard_map/all_to_all | solution.py:74
Sparse Core Ops, SparseCore 0:
  47.1 53.7 all-gather.4
  102.7 52.4 all-gather.8
  157.1 30.4 all-gather.6
  189.3 30.3 all-gather.10

commit v2 on v0

v2 whole, which is shorter than its diff:
```python
import functools

import jax
import jax.numpy as jnp
from jax import lax
from jax.experimental import pallas as pl
from jax.experimental.pallas import tpu as pltpu
from jax.sharding import Mesh, PartitionSpec as P

EPS = 1e-06
F32 = jnp.float32
BF16 = jnp.bfloat16
NY, NC, NX, NZ = 4, 2, 4, 8
N_EXP = NX * NZ
CHUNKS = ((0, 8), (8, 16), (24, 8))
PIECE = 256

VMEM = pl.BlockSpec(memory_space=pltpu.VMEM)
SMEM = pl.BlockSpec(memory_space=pltpu.SMEM)


def by_rows(left, right):
    return lax.dot_general(
        left, right, (((1,), (1,)), ((), ())), preferred_element_type=F32
    )


def times(left, right):
    return jnp.dot(left, right, preferred_element_type=F32)


def params(mib):
    return pltpu.CompilerParams(vmem_limit_bytes=mib << 20)


def cost(flops, moved):
    return pl.CostEstimate(flops=flops, bytes_accessed=moved, transcendentals=0)


def places(names, core):
    tokens = names.shape[1]
    expert = core.astype(F32) + 2.0 * lax.broadcasted_iota(
        jnp.int32, (N_EXP, tokens), 0
    ).astype(F32)
    hits = [names[k : k + 1, :] == expert for k in range(8)]
    named = hits[0]
    for hit in hits[1:]:
        named = named | hit
    row = lax.broadcasted_iota(jnp.int32, (tokens, tokens), 0)
    col = lax.broadcasted_iota(jnp.int32, (tokens, tokens), 1)
    earlier = jnp.where(row < col, 1.0, 0.0).astype(BF16)
    before = times(jnp.where(named, 1.0, 0.0).astype(BF16), earlier)
    return hits, jnp.where(named, before, -1.0)


def spread(place, values, first, size):
    tokens = place.shape[1]
    slot = lax.broadcasted_iota(jnp.int32, (size, tokens), 0) + first
    slot = slot.astype(F32)
    return jnp.concatenate(
        [
            jnp.where(place[d : d + 1, :] == slot, values[d : d + 1, :], 0.0)
            for d in range(N_EXP)
        ],
        axis=0,
    )


def pick(names, part, chunk, core):
    _, place = places(names, core)
    picks = spread(place, jnp.ones_like(place), *chunk).astype(BF16)
    return times(picks, part).astype(BF16)


def first_kernel(pos, tokens, gain, routes, part_out, rows_out):
    values = tokens[...].astype(F32)
    count, width = values.shape
    squares = jnp.sum(values * values, axis=1, keepdims=True)
    inverse = lax.rsqrt(squares / width + EPS)
    quarter = width // NY
    cols = pl.ds(pl.multiple_of(pos[0] * quarter, quarter), quarter)
    mine = (tokens[:, cols].astype(F32) * gain[:, cols].astype(F32)).astype(BF16)
    part = (mine.astype(F32) * inverse).astype(BF16)
    part_out[...] = part
    rows_out[...] = pick(routes[...].astype(F32), part, CHUNKS[0], pos[1])


def later_kernel(pos, part, routes, *rows_out):
    for chunk, out in zip(CHUNKS[1:], rows_out):
        out[...] = pick(routes[...].astype(F32), part[...], chunk, pos[1])


def mix_kernel(pos, tokens, gain, router, routes, *mix_out):
    values = tokens[...].astype(F32)
    count, width = values.shape
    scaled = (values * gain[...].astype(F32)).astype(BF16)
    squares = jnp.sum(values * values, axis=1, keepdims=True)
    inverse = lax.rsqrt(squares / width + EPS)
    turned = jnp.transpose(jnp.broadcast_to(inverse, (count, 128)))
    logits = by_rows(router[...], scaled) * turned[0:1, :]
    expert = lax.broadcasted_iota(jnp.int32, logits.shape, 0).astype(F32)
    names = routes[...].astype(F32)
    chosen = [
        jnp.sum(jnp.where(names[k : k + 1, :] == expert, logits, 0.0), axis=0, keepdims=True)
        for k in range(8)
    ]
    raised = jnp.exp(jnp.concatenate(chosen, axis=0))
    weights = raised / jnp.sum(raised, axis=0, keepdims=True)
    hits, place = places(names, pos[1])
    dense = jnp.zeros_like(place)
    for k in range(8):
        dense = dense + jnp.where(hits[k], weights[k : k + 1, :], 0.0)
    for (first, size), out in zip(CHUNKS, mix_out):
        out[...] = jnp.transpose(spread(place, dense, first, size)).astype(BF16)


def hidden_kernel(pos, blocks, gate_own, gate_other, up_own, up_other, out):
    quarter = blocks.shape[2]
    sums = [None] * 4
    for index in range(NY):
        block = blocks[index]
        cols = slice(index * quarter, (index + 1) * quarter)
        for which, rows in enumerate(
            (gate_own[0, :, cols], up_own[0, :, cols], gate_other[:, cols], up_other[:, cols])
        ):
            step = by_rows(block, rows)
            sums[which] = step if sums[which] is None else sums[which] + step
    own, other = [
        gate / (1.0 + jnp.exp(-gate)) * up for gate, up in (sums[0:2], sums[2:4])
    ]
    low = jnp.where(pos[1] == 0, own, other)
    high = jnp.where(pos[1] == 0, other, own)
    out[...] = jnp.concatenate([low, high], axis=1).astype(BF16)


def down_kernel(pos, down_own, down_other, *refs):
    out = refs[-1]
    cols = down_other.shape[1]
    for index, blocks in enumerate(refs[:-1]):
        rows, units = blocks.shape[1:]
        at = slice(index * rows, (index + 1) * rows)
        own = other = None
        for y in range(NY):
            span = slice(y * units, (y + 1) * units)
            own_step = times(blocks[y], down_own[0, span, :])
            other_step = times(blocks[y], down_other[span, :])
            own = own_step if own is None else own + own_step
            other = other_step if other is None else other + other_step
        for core, total in ((pos[1], own), (1 - pos[1], other)):
            out[at, pl.ds(pl.multiple_of(core * cols, cols), cols)] = total.astype(BF16)


def combine_kernel(pos, *refs):
    keep_out, give_out = refs[-2:]
    cols = keep_out.shape[1]
    pairs = len(refs) // 2 - 1
    for out, core in ((give_out, 1 - pos[1]), (keep_out, pos[1])):
        at = pl.ds(pl.multiple_of(core * cols, cols), cols)
        total = None
        for index in range(pairs):
            step = times(refs[2 * index][...], refs[2 * index + 1][:, at])
            total = step if total is None else total + step
        out[...] = total.astype(out.dtype)


def body(tokens, norm_gain, router, routes, w_gate, w_up, w_down):
    count, width = tokens.shape
    quarter = width // NY
    units = 2 * w_gate.shape[1]
    ff = w_down.shape[1]
    cols = w_down.shape[2]
    sds = jax.ShapeDtypeStruct
    pos = jnp.stack([lax.axis_index("y"), lax.axis_index("c")]).astype(jnp.int32)
    turned = routes.T
    sizes = [N_EXP * size for _, size in CHUNKS]

    gain = norm_gain[None, :]
    part, first_rows = pl.pallas_call(
        first_kernel,
        out_shape=(sds((count, quarter), BF16), sds((sizes[0], quarter), BF16)),
        in_specs=[SMEM] + [VMEM] * 3,
        out_specs=(VMEM, VMEM),
        compiler_params=params(16),
        cost_estimate=cost(2 * count * sizes[0] * quarter, count * width * 2),
    )(pos, tokens, gain, turned)
    received = [lax.all_to_all(first_rows, ("x", "z"), 0, 0, tiled=True)]
    later_rows = pl.pallas_call(
        later_kernel,
        out_shape=tuple(sds((size, quarter), BF16) for size in sizes[1:]),
        in_specs=[SMEM] + [VMEM] * 2,
        out_specs=(VMEM,) * (len(CHUNKS) - 1),
        compiler_params=params(16),
        cost_estimate=cost(2 * count * sum(sizes) * quarter, sum(sizes) * quarter * 2),
    )(pos, part, turned)
    sent = [
        lax.dynamic_index_in_dim(array, 1 - pos[1], 0, keepdims=False)
        for array in (w_gate, w_up, w_down)
    ]
    *sent, received[0] = lax.optimization_barrier((*sent, received[0]))
    others = [lax.ppermute(array, "c", [(0, 1), (1, 0)]) for array in sent]
    for rows in later_rows:
        rows, received[-1] = lax.optimization_barrier((rows, received[-1]))
        received.append(lax.all_to_all(rows, ("x", "z"), 0, 0, tiled=True))
    tokens, router, received[0] = lax.optimization_barrier((tokens, router, received[0]))
    mixes = pl.pallas_call(
        mix_kernel,
        out_shape=tuple(sds((count, size), BF16) for size in sizes),
        in_specs=[SMEM] + [VMEM] * 4,
        out_specs=(VMEM,) * len(CHUNKS),
        compiler_params=params(16),
        cost_estimate=cost(2 * count * width * 64, count * width * 2),
    )(pos, tokens, gain, router, turned)

    returned = []
    done = []
    for index, size in enumerate(sizes):
        mine = received[index]
        if index:
            before = [done[i][j] for i, j in ((index - 1, 0), (index - 2, 1)) if i >= 0]
            mine, *before = lax.optimization_barrier((mine, *before))
        blocks = lax.all_gather(mine, "y", axis=0)
        pieces = []
        for half in range(size // PIECE):
            hidden = pl.pallas_call(
                hidden_kernel,
                grid_spec=pltpu.PrefetchScalarGridSpec(
                    num_scalar_prefetch=1,
                    grid=(1,),
                    in_specs=[
                        pl.BlockSpec(
                            (NY, PIECE, quarter), lambda step, pos, half=half: (0, half, 0)
                        ),
                        pl.BlockSpec((1, units // 2, width), lambda step, pos: (pos[1], 0, 0)),
                        pl.BlockSpec((units // 2, width), lambda step, pos: (0, 0)),
                        pl.BlockSpec((1, units // 2, width), lambda step, pos: (pos[1], 0, 0)),
                        pl.BlockSpec((units // 2, width), lambda step, pos: (0, 0)),
                    ],
                    out_specs=pl.BlockSpec((PIECE, units), lambda step, pos: (0, 0)),
                ),
                out_shape=sds((PIECE, units), BF16),
                compiler_params=params(32),
                cost_estimate=cost(
                    4 * PIECE * width * units, 4 * units * width + 2 * PIECE * width
                ),
            )(pos, blocks, w_gate, others[0], w_up, others[1])
            pieces.append(lax.all_gather(hidden, "y", axis=0))
        result = pl.pallas_call(
            down_kernel,
            grid_spec=pltpu.PrefetchScalarGridSpec(
                num_scalar_prefetch=1,
                grid=(1,),
                in_specs=[
                    pl.BlockSpec((1, ff, cols), lambda step, pos: (pos[1], 0, 0)),
                    pl.BlockSpec((ff, cols), lambda step, pos: (0, 0)),
                ]
                + [pl.BlockSpec((NY, PIECE, units), lambda step, pos: (0, 0, 0))] * len(pieces),
                out_specs=pl.BlockSpec((size, NC * cols), lambda step, pos: (0, 0)),
            ),
            out_shape=sds((size, NC * cols), BF16),
            compiler_params=params(24),
            cost_estimate=cost(
                2 * size * ff * NC * cols, 2 * ff * NC * cols + 2 * size * NC * cols
            ),
        )(pos, w_down, others[2], *pieces)
        done.append((blocks, result))
        returned.append(lax.all_to_all(result, ("x", "z"), 0, 0, tiled=True))

    total = None
    last = len(CHUNKS) - 1
    for group in (range(last), range(last, last + 1)):
        keep, give = pl.pallas_call(
            combine_kernel,
            out_shape=(sds((count, cols), F32), sds((count, cols), BF16)),
            in_specs=[SMEM] + [VMEM] * (2 * len(group)),
            out_specs=(VMEM, VMEM),
            compiler_params=params(16),
            cost_estimate=cost(4 * count * cols * 512, 1 << 20),
        )(pos, *[item for i in group for item in (mixes[i], returned[i])])
        give = lax.ppermute(give, "c", [(0, 1), (1, 0)])
        share = keep + give.astype(F32)
        total = share if total is None else total + share
    return total.astype(BF16)


def solution(mesh):
    grid = Mesh(mesh.devices.reshape(NY, NC, NX, NZ), ("y", "c", "x", "z"))
    enc, exp = ("y", "c"), ("x", "z")
    return jax.shard_map(
        body,
        mesh=grid,
        in_specs=(
            P(exp, None),
            P(),
            P(),
            P(exp, None),
            P(exp, enc, None),
            P(exp, enc, None),
            P(exp, None, enc),
        ),
        out_specs=P(exp, enc),
        check_vma=False,
    )
```

time: 565 us -> 261 us (0.46)
  blocking collectives: 374 us -> 89.4 us
  waiting for transfers between devices: 95.7 us -> 26.8 us
  starting transfers between devices: 9.79 us -> 66.1 us
  Pallas kernels: 0 us -> 39.8 us
  matrix products: 27.3 us -> 0 us
  local copies, waits for them, and re-layouts: 38 us -> 23.7 us
  other arithmetic: 6.51 us -> 0.8 us
    all_to_all x1, blocking collectives: 374 us -> 32.3 us  [body(): received.append(lax.all_to_all(rows, ('x', 'z'), 0, 0, tiled=True))]
    all_gather x0 -> x4, blocking collectives: none -> 57.1 us  [body(): pieces.append(lax.all_gather(hidden, 'y', axis=0))]
    all_to_all x1 -> x5, waiting for transfers between devices: 46.8 us -> 6.6 us  [the longest x1 4.9 us: body(): received = [lax.all_to_all(first_rows, ('x', 'z'), 0, 0, tiled=True)]]
    pallas_call x0 -> x12, Pallas kernels: none -> 39.8 us  [the longest x4 21.1 us: body(): pl.pallas_call(hidden_kernel, grid_spec=pltpu.PrefetchScalarGridSpec(num_...]
    all_to_all x1 -> x5, starting transfers between devices: 9.53 us -> 46.9 us  [the longest x3 28.4 us: body(): returned.append(lax.all_to_all(result, ('x', 'z'), 0, 0, tiled=True))]
    all_gather x2 -> x3, waiting for transfers between devices: 48.9 us -> 19.1 us  [body(): blocks = lax.all_gather(mine, 'y', axis=0)]
    dot_general x7 -> x0, matrix products: 27.3 us -> none  [the longest x5 18.9 us: by_rows(): lax.dot_general(left, right, (((1,), (1,)), ((), ())), preferred_element_...]
    scatter x1 -> x0, local copies, waits for them, and re-layouts: 20.3 us -> none  [body(): outgoing.at[slot_index.reshape(-1)]]
  transfers between devices with their start and end apart: 3 -> 13, of which waited for: 3 -> 5; matrix products, arithmetic and copies ran while one was open for 3% -> 2% of each run, Pallas kernels for 0% -> 15%
where the time goes in v2:
time: 261 us; the launch traced here: 260 us
  blocking collectives  89.4 us (34%)
  starting transfers between devices  66.1 us (25%)
  Pallas kernels  39.8 us (15%)
  waiting for transfers between devices  26.8 us (10%)
  local copies, waits for them, and re-layouts  23.7 us (9%)
  between operations  13.4 us (5%)
    all_gather x4, blocking collectives, body(): pieces.append(lax.all_gather(hidden, 'y', axis=0))  57.1 us
    all_to_all x1, blocking collectives, body(): received.append(lax.all_to_all(rows, ('x', 'z'), 0, 0, tiled=True))  32.3 us
    all_to_all x3, starting transfers between devices, body(): returned.append(lax.all_to_all(result, ('x', 'z'), 0, 0, tiled=True))  28.4 us
    pallas_call x4, Pallas kernels, body(): pl.pallas_call(hidden_kernel, grid_spec=pltpu.PrefetchScalarGridSpec(num_...  21.1 us
    all_gather x3, waiting for transfers between devices, body(): blocks = lax.all_gather(mine, 'y', axis=0)  19.1 us
    unnamed x38, local copies, waits for them, and re-layouts  16.8 us
    ppermute x2, starting transfers between devices, body(): give = lax.ppermute(give, 'c', [(0, 1), (1, 0)])  14.6 us
    all_to_all x1, starting transfers between devices, body(): received = [lax.all_to_all(first_rows, ('x', 'z'), 0, 0, tiled=True)]  12 us
  transfers between devices with their start and end apart: 13, of which 5 were waited for; matrix products, arithmetic and copies ran while one was open for 2% of the time, Pallas kernels for 15%

profile of v2, /device:TPU:1, one launch (start us, length us, event | category | flops | bytes accessed | tf_op | source)
XLA Modules:
  0.0 259.8 jit_solution(5754379184349395747)
XLA Ops:
  11.2 12.0 %all-to-all-start = ((bf16[32,8,1024]{2,1,0:T(8,128)(2,1)}), bf16[32,8,1024]{2,1,0:T(8,128)(2,1)}, u32[]{:S(2)}, u32[]{:S(2)}) async-start(bf16[32,8,1024]{2,1,0:T(8,128)(2,1)} %bitcast.6), calls=%async_computation | async-start | bytes 1048576 | tf_op jit(solution)/shard_map/all_to_all | solution.py:186
  26.5 2.8 %dynamic-slice_bitcast_fusion = bf16[1536,512]{1,0:T(8,128)(2,1)} fusion(bf16[2,1536,512]{2,1,0:T(8,128)(2,1)} %down_own.5, s32[]{:T(128)S(6)} %select_n.7), kind=kLoop, calls=%fused_computation | loop fusion | bytes 3145732 | tf_op jit(solution)/shard_map/jit(dynamic_index_in_dim)/squeeze | solution.py:196
  29.2 3.4 %dynamic-slice_bitcast_fusion.1 = (bf16[192,4096]{1,0:T(8,128)(2,1)}, bf16[192,4096]{1,0:T(8,128)(2,1)}) fusion(bf16[2,192,4096]{2,1,0:T(8,128)(2,1)} %up_own.7, s32[]{:T(128)S(6)} %select_n.7, bf16[2,192,4096]{2,1,0:T(8,128)(2,1)S(1)} %copy-done), kind=kLoop, calls=%fused_computation.1 | loop fusion | bytes 6291460 | tf_op jit(solution)/shard_map/jit(dynamic_index_in_dim)/squeeze | solution.py:196
  32.6 4.9 %all-to-all-done = bf16[32,8,1024]{2,1,0:T(8,128)(2,1)} async-done(((bf16[32,8,1024]{2,1,0:T(8,128)(2,1)}), bf16[32,8,1024]{2,1,0:T(8,128)(2,1)}, u32[]{:S(2)}, u32[]{:S(2)}) %all-to-all-start) | async-done | bytes 524320 | tf_op jit(solution)/shard_map/all_to_all | solution.py:186
  37.6 32.3 %all_to_all.69 = bf16[32,16,1024]{2,1,0:T(8,128)(2,1)} all-to-all(bf16[32,16,1024]{2,1,0:T(8,128)(2,1)} %bitcast.39), channel_id=1, replica_groups=mesh['y'=4,'c'=2,'x'=4,'z'=8] {'x','z'}, dimensions={0} | all-to-all | bytes 2097152 | tf_op jit(solution)/shard_map/all_to_all | solution.py:203
  71.2 3.8 %collective-permute-start.1 = (bf16[192,4096]{1,0:T(8,128)(2,1)}, bf16[192,4096]{1,0:T(8,128)(2,1)}, u32[]{:S(2)}, u32[]{:S(2)}) collective-permute-start(bf16[192,4096]{1,0:T(8,128)(2,1)} %get-tuple-element.39), channel_id=1, source_target_pairs={{0,32},{32,0},{1,33},{33,1},{2,34},{34,2},{3,35},{35,3},{4,36},{36... | collective-permute-start | bytes 4718600 | tf_op jit(solution)/shard_map/ppermute | solution.py:200
  75.6 6.6 %all-to-all-start.4 = ((bf16[32,8,1024]{2,1,0:T(8,128)(2,1)}), bf16[32,8,1024]{2,1,0:T(8,128)(2,1)}, u32[]{:S(2)}, u32[]{:S(2)}) async-start(bf16[32,8,1024]{2,1,0:T(8,128)(2,1)} %bitcast.40), calls=%async_computation.4 | async-start | bytes 1048576 | tf_op jit(solution)/shard_map/all_to_all | solution.py:203
  86.0 5.5 %shard_map.76 = bf16[256,384]{1,0:T(8,128)(2,1)S(1)} custom-call(s32[2]{0:T(128)S(1)} %pad_add_fusion.pos, bf16[4,256,1024]{2,1,0:T(8,128)(2,1)S(1)} %bitcast.37, bf16[2,192,4096]{2,1,0:T(8,128)(2,1)S(1)} %copy-done, bf16[192,4096]{1,0:T(8,128)(2,1)} %collective-permute-done.1.gate_other, bf16[2,192,4096]{2,1,0:T(8,128)(2,1)S(1)} %copy-done.1, ...), custom_call_target="tpu_custom_call" | custom-call | flops 1610612736 | bytes 8388608 | tf_op jit(solution)/shard_map/pallas_call | solution.py:224
  91.5 17.0 %all-gather.1 = bf16[1024,384]{1,0:T(8,128)(2,1)S(1)} all-gather(bf16[256,384]{1,0:T(8,128)(2,1)S(1)} %shard_map.76), channel_id=3, replica_groups=mesh['y'=4,'c'=2,'x'=4,'z'=8] {'y'}, dimensions={0}, use_global_device_ids=true | all-gather | bytes 983040 | tf_op jit(solution)/shard_map/all_gather | solution.py:246
  108.5 3.2 %shard_map.77 = bf16[256,1024]{1,0:T(8,128)(2,1)S(1)} custom-call(s32[2]{0:T(128)S(1)} %pad_add_fusion.pos, bf16[2,1536,512]{2,1,0:T(8,128)(2,1)S(1)} %copy-done.4, bf16[1536,512]{1,0:T(8,128)(2,1)} %collective-permute-done.down_other, bf16[4,256,384]{2,1,0:T(8,128)(2,1)S(1)} %bitcast.31), custom_call_target="tpu_custom_call" | custom-call | flops 805306368 | bytes 3670016 | tf_op jit(solution)/shard_map/pallas_call | solution.py:247
  112.5 17.7 %all-gather.13.cloned.1.call-done = bf16[2048,1024]{1,0:T(8,128)(2,1)} async-done(((bf16[512,1024]{1,0:T(8,128)(2,1)}), bf16[2048,1024]{1,0:T(8,128)(2,1)}) %all-gather.13.cloned.1.call-update) | async-done | bytes 4194320 | tf_op jit(solution)/shard_map/all_gather | solution.py:221
  130.3 9.9 %all-to-all-start.1 = ((bf16[32,8,1024]{2,1,0:T(8,128)(2,1)}), bf16[32,8,1024]{2,1,0:T(8,128)(2,1)}, u32[]{:S(2)}, u32[]{:S(2)}) async-start(bf16[32,8,1024]{2,1,0:T(8,128)(2,1)} %bitcast.35), calls=%async_computation.1 | async-start | bytes 1048576 | tf_op jit(solution)/shard_map/all_to_all | solution.py:266
  144.3 5.2 %shard_map.79 = bf16[256,384]{1,0:T(8,128)(2,1)S(1)} custom-call(s32[2]{0:T(128)S(1)} %pad_add_fusion.pos, bf16[4,512,1024]{2,1,0:T(8,128)(2,1)S(1)} %bitcast.28, bf16[2,192,4096]{2,1,0:T(8,128)(2,1)S(1)} %copy-done, bf16[192,4096]{1,0:T(8,128)(2,1)} %collective-permute-done.1.gate_other, bf16[2,192,4096]{2,1,0:T(8,128)(2,1)S(1)} %copy-done.2, ...), custom_call_target="tpu_custom_call" | custom-call | flops 1610612736 | bytes 8388608 | tf_op jit(solution)/shard_map/pallas_call | solution.py:224
  149.5 5.3 %shard_map.78 = bf16[256,384]{1,0:T(8,128)(2,1)S(1)} custom-call(s32[2]{0:T(128)S(1)} %pad_add_fusion.pos, bf16[4,512,1024]{2,1,0:T(8,128)(2,1)S(1)} %bitcast.29, bf16[2,192,4096]{2,1,0:T(8,128)(2,1)S(1)} %copy-done, bf16[192,4096]{1,0:T(8,128)(2,1)} %collective-permute-done.1.gate_other, bf16[2,192,4096]{2,1,0:T(8,128)(2,1)S(1)} %copy-done.2, ...), custom_call_target="tpu_custom_call" | custom-call | flops 1610612736 | bytes 8388608 | tf_op jit(solution)/shard_map/pallas_call | solution.py:224
  154.8 16.7 %all-gather.3 = bf16[1024,384]{1,0:T(8,128)(2,1)S(1)} all-gather(bf16[256,384]{1,0:T(8,128)(2,1)S(1)} %shard_map.78), channel_id=5, replica_groups=mesh['y'=4,'c'=2,'x'=4,'z'=8] {'y'}, dimensions={0}, use_global_device_ids=true | all-gather | bytes 983040 | tf_op jit(solution)/shard_map/all_gather | solution.py:246
  171.5 11.7 %all-gather.4 = bf16[1024,384]{1,0:T(8,128)(2,1)S(1)} all-gather(bf16[256,384]{1,0:T(8,128)(2,1)S(1)} %shard_map.79), channel_id=6, replica_groups=mesh['y'=4,'c'=2,'x'=4,'z'=8] {'y'}, dimensions={0}, use_global_device_ids=true | all-gather | bytes 983040 | tf_op jit(solution)/shard_map/all_gather | solution.py:246
  183.3 4.3 %shard_map.80 = bf16[512,1024]{1,0:T(8,128)(2,1)S(1)} custom-call(s32[2]{0:T(128)S(1)} %pad_add_fusion.pos, bf16[2,1536,512]{2,1,0:T(8,128)(2,1)S(1)} %copy-done.5, bf16[1536,512]{1,0:T(8,128)(2,1)} %collective-permute-done.down_other, bf16[4,256,384]{2,1,0:T(8,128)(2,1)S(1)} %bitcast.33, bf16[4,256,384]{2,1,0:T(8,128)(2,1)S(1)} %bitcast.34), custom_call_target="tpu_custom_call" | custom-call | flops 1610612736 | bytes 4194304 | tf_op jit(solution)/shard_map/pallas_call | solution.py:247
  188.6 9.2 %all-to-all-start.3 = ((bf16[32,16,1024]{2,1,0:T(8,128)(2,1)}), bf16[32,16,1024]{2,1,0:T(8,128)(2,1)}, u32[]{:S(2)}, u32[]{:S(2)}) async-start(bf16[32,16,1024]{2,1,0:T(8,128)(2,1)} %bitcast.30), calls=%async_computation.3 | async-start | bytes 2097152 | tf_op jit(solution)/shard_map/all_to_all | solution.py:266
  201.3 5.1 %shard_map.82 = bf16[256,384]{1,0:T(8,128)(2,1)S(1)} custom-call(s32[2]{0:T(128)S(1)} %pad_add_fusion.pos, bf16[4,256,1024]{2,1,0:T(8,128)(2,1)S(1)} %bitcast.38, bf16[2,192,4096]{2,1,0:T(8,128)(2,1)S(1)} %copy-done, bf16[192,4096]{1,0:T(8,128)(2,1)} %collective-permute-done.1.gate_other, bf16[2,192,4096]{2,1,0:T(8,128)(2,1)S(1)} %copy-done.3, ...), custom_call_target="tpu_custom_call" | custom-call | flops 1610612736 | bytes 8388608 | tf_op jit(solution)/shard_map/pallas_call | solution.py:224
  206.4 11.6 %all-gather.6 = bf16[1024,384]{1,0:T(8,128)(2,1)S(1)} all-gather(bf16[256,384]{1,0:T(8,128)(2,1)S(1)} %shard_map.82), channel_id=8, replica_groups=mesh['y'=4,'c'=2,'x'=4,'z'=8] {'y'}, dimensions={0}, use_global_device_ids=true | all-gather | bytes 983040 | tf_op jit(solution)/shard_map/all_gather | solution.py:246
  218.1 4.0 %shard_map.83 = bf16[256,1024]{1,0:T(8,128)(2,1)} custom-call(s32[2]{0:T(128)S(1)} %pad_add_fusion.pos, bf16[2,1536,512]{2,1,0:T(8,128)(2,1)S(1)} %copy-done.6, bf16[1536,512]{1,0:T(8,128)(2,1)} %collective-permute-done.down_other, bf16[4,256,384]{2,1,0:T(8,128)(2,1)S(1)} %bitcast.32), custom_call_target="tpu_custom_call" | custom-call | flops 805306368 | bytes 3670016 | tf_op jit(solution)/shard_map/pallas_call | solution.py:247
  222.1 9.3 %all-to-all-start.5 = ((bf16[32,8,1024]{2,1,0:T(8,128)(2,1)}), bf16[32,8,1024]{2,1,0:T(8,128)(2,1)S(1)}, u32[]{:S(2)}, u32[]{:S(2)}) async-start(bf16[32,8,1024]{2,1,0:T(8,128)(2,1)} %bitcast.23), calls=%async_computation.5 | async-start | bytes 1048576 | tf_op jit(solution)/shard_map/all_to_all | solution.py:266
  234.5 6.6 %collective-permute-start.3 = (bf16[128,512]{1,0:T(8,128)(2,1)S(1)}, bf16[128,512]{1,0:T(8,128)(2,1)S(1)}, u32[]{:S(2)}, u32[]{:S(2)}) collective-permute-start(bf16[128,512]{1,0:T(8,128)(2,1)S(1)} %get-tuple-element.47), channel_id=1, source_target_pairs={{0,32},{32,0},{1,33},{33,1},{2,34},{34,2},{3,35},{35,3},{4,36},{36... | collective-permute-start | bytes 393224 | tf_op jit(solution)/shard_map/ppermute | solution.py:279
  243.5 8.1 %collective-permute-start.4 = (bf16[128,512]{1,0:T(8,128)(2,1)S(1)}, bf16[128,512]{1,0:T(8,128)(2,1)S(1)}, u32[]{:S(2)}, u32[]{:S(2)}) collective-permute-start(bf16[128,512]{1,0:T(8,128)(2,1)S(1)} %get-tuple-element.52), channel_id=1, source_target_pairs={{0,32},{32,0},{1,33},{33,1},{2,34},{34,2},{3,35},{35,3},{4,36},{36... | collective-permute-start | bytes 393224 | tf_op jit(solution)/shard_map/ppermute | solution.py:279
  (65 shorter events, 30.3 us)
Async XLA Ops:
  6.5 16.8 %copy-start.18 = (s32[128,8]{0,1:T(8,128)S(1)}, s32[128,8]{0,1:T(8,128)}, u32[]{:S(2)}) copy-start(s32[128,8]{0,1:T(8,128)} %param.10) | copy-start | bytes 12292
  11.2 26.3 %all-to-all-start = ((bf16[32,8,1024]{2,1,0:T(8,128)(2,1)}), bf16[32,8,1024]{2,1,0:T(8,128)(2,1)}, u32[]{:S(2)}, u32[]{:S(2)}) async-start(bf16[32,8,1024]{2,1,0:T(8,128)(2,1)} %bitcast.6), calls=%async_computation | async-start | bytes 1048576 | tf_op jit(solution)/shard_map/all_to_all | solution.py:186
  23.2 6.0 %copy-start = (bf16[2,192,4096]{2,1,0:T(8,128)(2,1)S(1)}, bf16[2,192,4096]{2,1,0:T(8,128)(2,1)}, u32[]{:S(2)}) copy-start(bf16[2,192,4096]{2,1,0:T(8,128)(2,1)} %gate_own.7) | copy-start | bytes 9437188
  23.2 48.0 %all-gather.11.cloned.1.call-start = ((), (), s32[]{:S(2)}) async-start(), calls=%async_computation.6 | async-start | bytes 2621440 | tf_op jit(solution)/shard_map/all_gather | solution.py:221
  37.5 92.7 %all-gather.13.cloned.1.call-start = ((), (), s32[]{:S(2)}) async-start(), calls=%async_computation.7 | async-start | bytes 5242880 | tf_op jit(solution)/shard_map/all_gather | solution.py:221
  71.2 11.0 %collective-permute-start.1 = (bf16[192,4096]{1,0:T(8,128)(2,1)}, bf16[192,4096]{1,0:T(8,128)(2,1)}, u32[]{:S(2)}, u32[]{:S(2)}) collective-permute-start(bf16[192,4096]{1,0:T(8,128)(2,1)} %get-tuple-element.39), channel_id=1, source_target_pairs={{0,32},{32,0},{1,33},{33,1},{2,34},{34,2},{3,35},{35,3},{4,36},{36... | collective-permute-start | bytes 4718600 | tf_op jit(solution)/shard_map/ppermute | solution.py:200
  75.1 7.2 %collective-permute-start.2 = (bf16[192,4096]{1,0:T(8,128)(2,1)}, bf16[192,4096]{1,0:T(8,128)(2,1)}, u32[]{:S(2)}, u32[]{:S(2)}) collective-permute-start(bf16[192,4096]{1,0:T(8,128)(2,1)} %get-tuple-element.40), channel_id=1, source_target_pairs={{0,32},{32,0},{1,33},{33,1},{2,34},{34,2},{3,35},{35,3},{4,36},{36... | collective-permute-start | bytes 4718600 | tf_op jit(solution)/shard_map/ppermute | solution.py:200
  75.2 33.3 %collective-permute-start = (bf16[1536,512]{1,0:T(8,128)(2,1)}, bf16[1536,512]{1,0:T(8,128)(2,1)}, u32[]{:S(2)}, u32[]{:S(2)}) collective-permute-start(bf16[1536,512]{1,0:T(8,128)(2,1)} %dynamic-slice_bitcast_fusion), channel_id=1, source_target_pairs={{0,32},{32,0},{1,33},{33,1},{2,34},{34,2},{3,35},{35,3},{4,36},{36... | collective-permute-start | bytes 4718600 | tf_op jit(solution)/shard_map/ppermute | solution.py:200
  75.6 36.9 %all-to-all-start.4 = ((bf16[32,8,1024]{2,1,0:T(8,128)(2,1)}), bf16[32,8,1024]{2,1,0:T(8,128)(2,1)}, u32[]{:S(2)}, u32[]{:S(2)}) async-start(bf16[32,8,1024]{2,1,0:T(8,128)(2,1)} %bitcast.40), calls=%async_computation.4 | async-start | bytes 1048576 | tf_op jit(solution)/shard_map/all_to_all | solution.py:203
  82.2 115.6 %all-gather.15.cloned.1.call-start = ((), (), s32[]{:S(2)}) async-start(), calls=%async_computation.8 | async-start | bytes 2621440 | tf_op jit(solution)/shard_map/all_gather | solution.py:221
  82.3 1.9 copy-start.1
  86.0 22.6 %copy-start.4 = (bf16[2,1536,512]{2,1,0:T(8,128)(2,1)S(1)}, bf16[2,1536,512]{2,1,0:T(8,128)(2,1)}, u32[]{:S(2)}) copy-start(bf16[2,1536,512]{2,1,0:T(8,128)(2,1)} %down_own.5) | copy-start | bytes 9437188
  130.3 58.3 %all-to-all-start.1 = ((bf16[32,8,1024]{2,1,0:T(8,128)(2,1)}), bf16[32,8,1024]{2,1,0:T(8,128)(2,1)}, u32[]{:S(2)}, u32[]{:S(2)}) async-start(bf16[32,8,1024]{2,1,0:T(8,128)(2,1)} %bitcast.35), calls=%async_computation.1 | async-start | bytes 1048576 | tf_op jit(solution)/shard_map/all_to_all | solution.py:266
  140.1 1.9 copy-start.2
  142.0 2.3 copy-start.7
  149.5 33.8 %copy-start.5 = (bf16[2,1536,512]{2,1,0:T(8,128)(2,1)S(1)}, bf16[2,1536,512]{2,1,0:T(8,128)(2,1)}, u32[]{:S(2)}) copy-start(bf16[2,1536,512]{2,1,0:T(8,128)(2,1)} %down_own.5) | copy-start | bytes 9437188
  188.6 33.5 %all-to-all-start.3 = ((bf16[32,16,1024]{2,1,0:T(8,128)(2,1)}), bf16[32,16,1024]{2,1,0:T(8,128)(2,1)}, u32[]{:S(2)}, u32[]{:S(2)}) async-start(bf16[32,16,1024]{2,1,0:T(8,128)(2,1)} %bitcast.30), calls=%async_computation.3 | async-start | bytes 2097152 | tf_op jit(solution)/shard_map/all_to_all | solution.py:266
  197.8 1.9 copy-start.3
  201.3 16.8 %copy-start.6 = (bf16[2,1536,512]{2,1,0:T(8,128)(2,1)S(1)}, bf16[2,1536,512]{2,1,0:T(8,128)(2,1)}, u32[]{:S(2)}) copy-start(bf16[2,1536,512]{2,1,0:T(8,128)(2,1)} %down_own.5) | copy-start | bytes 9437188
  218.1 13.3 %copy-start.9 = (bf16[128,4096]{1,0:T(8,128)(2,1)S(1)}, bf16[128,4096]{1,0:T(8,128)(2,1)}, u32[]{:S(2)}) copy-start(bf16[128,4096]{1,0:T(8,128)(2,1)} %tokens.2) | copy-start | bytes 3145732
  218.1 13.3 %copy-start.15 = (bf16[64,4096]{1,0:T(8,128)(2,1)S(1)}, bf16[64,4096]{1,0:T(8,128)(2,1)}, u32[]{:S(2)}) copy-start(bf16[64,4096]{1,0:T(8,128)(2,1)} %router) | copy-start | bytes 1572868
  222.1 20.7 %all-to-all-start.5 = ((bf16[32,8,1024]{2,1,0:T(8,128)(2,1)}), bf16[32,8,1024]{2,1,0:T(8,128)(2,1)S(1)}, u32[]{:S(2)}, u32[]{:S(2)}) async-start(bf16[32,8,1024]{2,1,0:T(8,128)(2,1)} %bitcast.23), calls=%async_computation.5 | async-start | bytes 1048576 | tf_op jit(solution)/shard_map/all_to_all | solution.py:266
  234.5 17.1 %collective-permute-start.3 = (bf16[128,512]{1,0:T(8,128)(2,1)S(1)}, bf16[128,512]{1,0:T(8,128)(2,1)S(1)}, u32[]{:S(2)}, u32[]{:S(2)}) collective-permute-start(bf16[128,512]{1,0:T(8,128)(2,1)S(1)} %get-tuple-element.47), channel_id=1, source_target_pairs={{0,32},{32,0},{1,33},{33,1},{2,34},{34,2},{3,35},{35,3},{4,36},{36... | collective-permute-start | bytes 393224 | tf_op jit(solution)/shard_map/ppermute | solution.py:279
  243.5 9.1 %collective-permute-start.4 = (bf16[128,512]{1,0:T(8,128)(2,1)S(1)}, bf16[128,512]{1,0:T(8,128)(2,1)S(1)}, u32[]{:S(2)}, u32[]{:S(2)}) collective-permute-start(bf16[128,512]{1,0:T(8,128)(2,1)S(1)} %get-tuple-element.52), channel_id=1, source_target_pairs={{0,32},{32,0},{1,33},{33,1},{2,34},{34,2},{3,35},{35,3},{4,36},{36... | collective-permute-start | bytes 393224 | tf_op jit(solution)/shard_map/ppermute | solution.py:279
  (8 other events, 8.9 us)
Sparse Core Ops, SparseCore 0:
  37.7 33.5 all-gather.10
  73.0 57.1 all-gather.12
  132.1 39.4 all-gather.14

commit v3 on v2

--- a/solution.py
+++ b/solution.py
@@ -114,40 +114,69 @@
         out[...] = jnp.transpose(spread(place, dense, first, size)).astype(BF16)
 
 
-def hidden_kernel(pos, blocks, gate_own, gate_other, up_own, up_other, out):
-    quarter = blocks.shape[2]
-    sums = [None] * 4
-    for index in range(NY):
-        block = blocks[index]
-        cols = slice(index * quarter, (index + 1) * quarter)
-        for which, rows in enumerate(
-            (gate_own[0, :, cols], up_own[0, :, cols], gate_other[:, cols], up_other[:, cols])
-        ):
-            step = by_rows(block, rows)
-            sums[which] = step if sums[which] is None else sums[which] + step
-    own, other = [
-        gate / (1.0 + jnp.exp(-gate)) * up for gate, up in (sums[0:2], sums[2:4])
-    ]
-    low = jnp.where(pos[1] == 0, own, other)
-    high = jnp.where(pos[1] == 0, other, own)
-    out[...] = jnp.concatenate([low, high], axis=1).astype(BF16)
-
-
-def down_kernel(pos, down_own, down_other, *refs):
-    out = refs[-1]
-    cols = down_other.shape[1]
-    for index, blocks in enumerate(refs[:-1]):
-        rows, units = blocks.shape[1:]
-        at = slice(index * rows, (index + 1) * rows)
-        own = other = None
-        for y in range(NY):
-            span = slice(y * units, (y + 1) * units)
-            own_step = times(blocks[y], down_own[0, span, :])
-            other_step = times(blocks[y], down_other[span, :])
-            own = own_step if own is None else own + own_step
-            other = other_step if other is None else other + other_step
-        for core, total in ((pos[1], own), (1 - pos[1], other)):
-            out[at, pl.ds(pl.multiple_of(core * cols, cols), cols)] = total.astype(BF16)
+def hidden_kernel(pos, blocks, gate_own, gate_other, up_own, up_other, out, *sums):
+    step = pl.program_id(0)
+    block = blocks[0]
+    for total, rows in zip(
+        sums, (gate_own[0], up_own[0], gate_other[...], up_other[...])
+    ):
+        term = by_rows(block, rows)
+
+        @pl.when(step == 0)
+        def _(total=total, term=term):
+            total[...] = term
+
+        @pl.when(step > 0)
+        def _(total=total, term=term):
+            total[...] += term
+
+    @pl.when(step == NY - 1)
+    def _():
+        own, other = [
+            gate[...] / (1.0 + jnp.exp(-gate[...])) * up[...]
+            for gate, up in (sums[0:2], sums[2:4])
+        ]
+        low = jnp.where(pos[1] == 0, own, other)
+        high = jnp.where(pos[1] == 0, other, own)
+        out[...] = jnp.concatenate([low, high], axis=1).astype(BF16)
+
+
+def store_columns(pos, out, own, other):
+    cols = own.shape[1]
+    for core, total in ((pos[1], own), (1 - pos[1], other)):
+        out[:, pl.ds(pl.multiple_of(core * cols, cols), cols)] = total.astype(BF16)
+
+
+def down_kernel(pos, blocks, down_own, down_other, out, *sums):
+    step = pl.program_id(0)
+    for total, part in zip(sums, (down_own[0], down_other[...])):
+        term = times(blocks[0], part)
+
+        @pl.when(step == 0)
+        def _(total=total, term=term):
+            total[...] = term
+
+        @pl.when(step > 0)
+        def _(total=total, term=term):
+            total[...] += term
+
+    @pl.when(step == NY - 1)
+    def _():
+        store_columns(pos, out, sums[0][...], sums[1][...])
+
+
+def down_ring_kernel(pos, down_own, down_other, own, low, high, far_top, far_bottom, out):
+    units = own.shape[1]
+    far = jnp.concatenate([far_top[...], far_bottom[...]], axis=0)
+    mine = theirs = None
+    for block, shift in ((own[...], 0), (low[...], 3), (high[...], 1), (far, 2)):
+        index = lax.rem(pos[0] + shift, NY)
+        rows = pl.ds(pl.multiple_of(index * units, units), units)
+        mine_step = times(block, down_own[0, rows, :])
+        theirs_step = times(block, down_other[rows, :])
+        mine = mine_step if mine is None else mine + mine_step
+        theirs = theirs_step if theirs is None else theirs + theirs_step
+    store_columns(pos, out, mine, theirs)
 
 
 def combine_kernel(pos, *refs):
@@ -161,6 +190,17 @@
             step = times(refs[2 * index][...], refs[2 * index + 1][:, at])
             total = step if total is None else total + step
         out[...] = total.astype(out.dtype)
+
+
+def turn(array, step):
+    return lax.ppermute(array, "y", [(i, (i + step) % NY) for i in range(NY)])
+
+
+def ring(block):
+    half = block.shape[0] // 2
+    low = turn(block, 1)
+    high = turn(block, -1)
+    return block, low, high, turn(low[:half], 1), turn(high[half:], -1)
 
 
 def body(tokens, norm_gain, router, routes, w_gate, w_up, w_down):
@@ -219,49 +259,75 @@
             before = [done[i][j] for i, j in ((index - 1, 0), (index - 2, 1)) if i >= 0]
             mine, *before = lax.optimization_barrier((mine, *before))
         blocks = lax.all_gather(mine, "y", axis=0)
-        pieces = []
-        for half in range(size // PIECE):
-            hidden = pl.pallas_call(
-                hidden_kernel,
+        if index == 1:
+            blocks, returned[0] = lax.optimization_barrier((blocks, returned[0]))
+        own_weight = pl.BlockSpec((1, units // 2, quarter), lambda y, pos: (pos[1], 0, y))
+        other_weight = pl.BlockSpec((units // 2, quarter), lambda y, pos: (0, y))
+        hidden = pl.pallas_call(
+            hidden_kernel,
+            grid_spec=pltpu.PrefetchScalarGridSpec(
+                num_scalar_prefetch=1,
+                grid=(NY,),
+                in_specs=[
+                    pl.BlockSpec((1, size, quarter), lambda y, pos: (y, 0, 0)),
+                    own_weight,
+                    other_weight,
+                    own_weight,
+                    other_weight,
+                ],
+                out_specs=pl.BlockSpec((size, units), lambda y, pos: (0, 0)),
+                scratch_shapes=[pltpu.VMEM((size, units // 2), F32)] * 4,
+            ),
+            out_shape=sds((size, units), BF16),
+            compiler_params=params(56),
+            cost_estimate=cost(4 * size * width * units, 4 * units * width + 2 * size * width),
+        )(pos, blocks, w_gate, others[0], w_up, others[1])
+        down_cost = cost(
+            2 * size * ff * NC * cols, 2 * ff * NC * cols + 2 * size * NC * cols
+        )
+        if size > PIECE:
+            whole = pl.BlockSpec((size, units), lambda step, pos: (0, 0))
+            half = pl.BlockSpec((size // 2, units), lambda step, pos: (0, 0))
+            result = pl.pallas_call(
+                down_ring_kernel,
                 grid_spec=pltpu.PrefetchScalarGridSpec(
                     num_scalar_prefetch=1,
                     grid=(1,),
                     in_specs=[
-                        pl.BlockSpec(
-                            (NY, PIECE, quarter), lambda step, pos, half=half: (0, half, 0)
-                        ),
-                        pl.BlockSpec((1, units // 2, width), lambda step, pos: (pos[1], 0, 0)),
-                        pl.BlockSpec((units // 2, width), lambda step, pos: (0, 0)),
-                        pl.BlockSpec((1, units // 2, width), lambda step, pos: (pos[1], 0, 0)),
-                        pl.BlockSpec((units // 2, width), lambda step, pos: (0, 0)),
+                        pl.BlockSpec((1, ff, cols), lambda step, pos: (pos[1], 0, 0)),
+                        pl.BlockSpec((ff, cols), lambda step, pos: (0, 0)),
+                        whole,
+                        whole,
+                        whole,
+                        half,
+                        half,
                     ],
-                    out_specs=pl.BlockSpec((PIECE, units), lambda step, pos: (0, 0)),
+                    out_specs=pl.BlockSpec((size, NC * cols), lambda step, pos: (0, 0)),
                 ),
-                out_shape=sds((PIECE, units), BF16),
-                compiler_params=params(32),
-                cost_estimate=cost(
-                    4 * PIECE * width * units, 4 * units * width + 2 * PIECE * width
+                out_shape=sds((size, NC * cols), BF16),
+                compiler_params=params(56),
+                cost_estimate=down_cost,
+            )(pos, w_down, others[2], *ring(hidden))
+        else:
+            result = pl.pallas_call(
+                down_kernel,
+                grid_spec=pltpu.PrefetchScalarGridSpec(
+                    num_scalar_prefetch=1,
+                    grid=(NY,),
+                    in_specs=[
+                        pl.BlockSpec((1, size, units), lambda y, pos: (y, 0, 0)),
+                        pl.BlockSpec((1, units, cols), lambda y, pos: (pos[1], y, 0)),
+                        pl.BlockSpec((units, cols), lambda y, pos: (y, 0)),
+                    ],
+                    out_specs=pl.BlockSpec((size, NC * cols), lambda y, pos: (0, 0)),
+                    scratch_shapes=[pltpu.VMEM((size, cols), F32)] * 2,
                 ),
-            )(pos, blocks, w_gate, others[0], w_up, others[1])
-            pieces.append(lax.all_gather(hidden, "y", axis=0))
-        result = pl.pallas_call(
-            down_kernel,
-            grid_spec=pltpu.PrefetchScalarGridSpec(
-                num_scalar_prefetch=1,
-                grid=(1,),
-                in_specs=[
-                    pl.BlockSpec((1, ff, cols), lambda step, pos: (pos[1], 0, 0)),
-                    pl.BlockSpec((ff, cols), lambda step, pos: (0, 0)),
-                ]
-                + [pl.BlockSpec((NY, PIECE, units), lambda step, pos: (0, 0, 0))] * len(pieces),
-                out_specs=pl.BlockSpec((size, NC * cols), lambda step, pos: (0, 0)),
-            ),
-            out_shape=sds((size, NC * cols), BF16),
-            compiler_params=params(24),
-            cost_estimate=cost(
-                2 * size * ff * NC * cols, 2 * ff * NC * cols + 2 * size * NC * cols
-            ),
-        )(pos, w_down, others[2], *pieces)
+                out_shape=sds((size, NC * cols), BF16),
+                compiler_params=params(56),
+                cost_estimate=down_cost,
+            )(pos, lax.all_gather(hidden, "y", axis=0), w_down, others[2])
+        if index == 0:
+            result, received[-1] = lax.optimization_barrier((result, received[-1]))
         done.append((blocks, result))
         returned.append(lax.all_to_all(result, ("x", "z"), 0, 0, tiled=True))
 

time: 261 us -> 270 us (1.034)
  Pallas kernels: 39.8 us -> 63.5 us
  local copies, waits for them, and re-layouts: 23.7 us -> 13.6 us
  waiting for transfers between devices: 26.8 us -> 33.7 us
  blocking collectives: 89.4 us -> 83.4 us
  starting transfers between devices: 66.1 us -> 61.1 us
    all_gather x4 -> x2, blocking collectives: 57.1 us -> 32.1 us  [body(): lax.all_gather(hidden, 'y', axis=0)]
    ppermute x0 -> x4, waiting for transfers between devices: none -> 22.5 us  [turn(): return lax.ppermute(array, 'y', [(i, (i + step) % NY) for i in range(NY)])]
    all_to_all x0 -> x1, blocking collectives: none -> 19.3 us  [body(): returned.append(lax.all_to_all(result, ('x', 'z'), 0, 0, tiled=True))]
    all_gather x3, waiting for transfers between devices: 19.1 us -> 1.61 us  [body(): blocks = lax.all_gather(mine, 'y', axis=0)]
    pallas_call x4 -> x3, Pallas kernels: 21.1 us -> 37.6 us  [body(): pl.pallas_call(hidden_kernel, grid_spec=pltpu.PrefetchScalarGridSpec(num_...]
    unnamed x38 -> x28, local copies, waits for them, and re-layouts: 16.8 us -> 6.23 us
    all_to_all x3 -> x2, starting transfers between devices: 28.4 us -> 18.9 us  [body(): returned.append(lax.all_to_all(result, ('x', 'z'), 0, 0, tiled=True))]
    pallas_call x0 -> x1, Pallas kernels: none -> 6.31 us  [body(): pl.pallas_call(down_ring_kernel, grid_spec=pltpu.PrefetchScalarGridSpec(n...]
  transfers between devices with their start and end apart: 13 -> 16, of which waited for: 5 -> 7; matrix products, arithmetic and copies ran while one was open for 2% -> 2% of each run, Pallas kernels for 15% -> 23%
where the time goes in v3:
time: 270 us; the launch traced here: 269 us
  blocking collectives  83.4 us (31%)
  Pallas kernels  63.5 us (24%)
  starting transfers between devices  61.1 us (23%)
  waiting for transfers between devices  33.7 us (12%)
  local copies, waits for them, and re-layouts  13.6 us (5%)
  between operations  13.3 us (5%)
    pallas_call x3, Pallas kernels, body(): pl.pallas_call(hidden_kernel, grid_spec=pltpu.PrefetchScalarGridSpec(num_...  37.6 us
    all_gather x2, blocking collectives, body(): lax.all_gather(hidden, 'y', axis=0)  32.1 us
    all_to_all x1, blocking collectives, body(): received.append(lax.all_to_all(rows, ('x', 'z'), 0, 0, tiled=True))  32 us
    ppermute x4, waiting for transfers between devices, turn(): return lax.ppermute(array, 'y', [(i, (i + step) % NY) for i in range(NY)])  22.5 us
    all_to_all x1, blocking collectives, body(): returned.append(lax.all_to_all(result, ('x', 'z'), 0, 0, tiled=True))  19.3 us
    all_to_all x2, starting transfers between devices, body(): returned.append(lax.all_to_all(result, ('x', 'z'), 0, 0, tiled=True))  18.9 us
    ppermute x2, starting transfers between devices, body(): give = lax.ppermute(give, 'c', [(0, 1), (1, 0)])  13.7 us
    pallas_call x2, Pallas kernels, body(): pl.pallas_call(down_kernel, grid_spec=pltpu.PrefetchScalarGridSpec(num_sc...  12.4 us
  transfers between devices with their start and end apart: 16, of which 7 were waited for; matrix products, arithmetic and copies ran while one was open for 2% of the time, Pallas kernels for 23%

profile of v3, /device:TPU:1, one launch (start us, length us, event | category | flops | bytes accessed | tf_op | source)
XLA Modules:
  0.0 269.3 jit_solution(11244527721464121472)
XLA Ops:
  11.2 11.9 %all-to-all-start = ((bf16[32,8,1024]{2,1,0:T(8,128)(2,1)}), bf16[32,8,1024]{2,1,0:T(8,128)(2,1)S(1)}, u32[]{:S(2)}, u32[]{:S(2)}) async-start(bf16[32,8,1024]{2,1,0:T(8,128)(2,1)} %bitcast.6), calls=%async_computation | async-start | bytes 1048576 | tf_op jit(solution)/shard_map/all_to_all | solution.py:226
  25.3 2.7 dynamic-slice_bitcast_fusion
  28.0 4.0 %dynamic-slice_bitcast_fusion.1 = (bf16[192,4096]{1,0:T(8,128)(2,1)}, bf16[192,4096]{1,0:T(8,128)(2,1)}) fusion(bf16[2,192,4096]{2,1,0:T(8,128)(2,1)} %up_own.5, s32[]{:T(128)S(6)} %select_n.7, bf16[2,192,4096]{2,1,0:T(8,128)(2,1)} %gate_own.5), kind=kLoop, calls=%fused_computation.1 | loop fusion | bytes 6291460 | tf_op jit(solution)/shard_map/jit(dynamic_index_in_dim)/squeeze | solution.py:236
  31.9 5.4 %all-to-all-done = bf16[32,8,1024]{2,1,0:T(8,128)(2,1)S(1)} async-done(((bf16[32,8,1024]{2,1,0:T(8,128)(2,1)}), bf16[32,8,1024]{2,1,0:T(8,128)(2,1)S(1)}, u32[]{:S(2)}, u32[]{:S(2)}) %all-to-all-start) | async-done | bytes 524320 | tf_op jit(solution)/shard_map/all_to_all | solution.py:226
  38.2 32.0 %all_to_all.70 = bf16[32,16,1024]{2,1,0:T(8,128)(2,1)} all-to-all(bf16[32,16,1024]{2,1,0:T(8,128)(2,1)S(1)} %bitcast.29), channel_id=1, replica_groups=mesh['y'=4,'c'=2,'x'=4,'z'=8] {'x','z'}, dimensions={0} | all-to-all | bytes 2097152 | tf_op jit(solution)/shard_map/all_to_all | solution.py:243
  71.9 3.6 %collective-permute-start = (bf16[192,4096]{1,0:T(8,128)(2,1)}, bf16[192,4096]{1,0:T(8,128)(2,1)}, u32[]{:S(2)}, u32[]{:S(2)}) collective-permute-start(bf16[192,4096]{1,0:T(8,128)(2,1)} %get-tuple-element.46), channel_id=1, source_target_pairs={{0,32},{32,0},{1,33},{33,1},{2,34},{34,2},{3,35},{35,3},{4,36},{36... | collective-permute-start | bytes 4718600 | tf_op jit(solution)/shard_map/ppermute | solution.py:240
  76.0 6.7 %all-to-all-start.2 = ((bf16[32,8,1024]{2,1,0:T(8,128)(2,1)}), bf16[32,8,1024]{2,1,0:T(8,128)(2,1)S(1)}, u32[]{:S(2)}, u32[]{:S(2)}) async-start(bf16[32,8,1024]{2,1,0:T(8,128)(2,1)} %bitcast.13), calls=%async_computation.2 | async-start | bytes 1048576 | tf_op jit(solution)/shard_map/all_to_all | solution.py:243
  83.4 11.0 %shard_map.76 = bf16[256,384]{1,0:T(8,128)(2,1)} custom-call(s32[2]{0:T(128)} %copy-done.3, bf16[4,256,1024]{2,1,0:T(8,128)(2,1)} %bitcast.43, bf16[2,192,4096]{2,1,0:T(8,128)(2,1)} %gate_own.5, bf16[192,4096]{1,0:T(8,128)(2,1)} %collective-permute-done.gate_other, bf16[2,192,4096]{2,1,0:T(8,128)(2,1)} %up_own.5, ...), custom_call_target="tpu_custom_call" | custom-call | flops 1610612736 | bytes 8388608 | tf_op jit(solution)/shard_map/pallas_call | solution.py:266
  94.4 18.8 %all-gather.2 = bf16[1024,384]{1,0:T(8,128)(2,1)} all-gather(bf16[256,384]{1,0:T(8,128)(2,1)} %shard_map.76), channel_id=4, replica_groups=mesh['y'=4,'c'=2,'x'=4,'z'=8] {'y'}, dimensions={0}, use_global_device_ids=true | all-gather | bytes 983040 | tf_op jit(solution)/shard_map/all_gather | solution.py:328
  114.3 6.2 %shard_map.77 = bf16[256,1024]{1,0:T(8,128)(2,1)} custom-call(s32[2]{0:T(128)} %copy-done.3, bf16[4,256,384]{2,1,0:T(8,128)(2,1)} %bitcast.36, bf16[2,1536,512]{2,1,0:T(8,128)(2,1)} %down_own.5, bf16[1536,512]{1,0:T(8,128)(2,1)} %copy-done.7), custom_call_target="tpu_custom_call" | custom-call | flops 805306368 | bytes 3670016 | tf_op jit(solution)/shard_map/pallas_call | solution.py:312
  120.5 19.3 %all_to_all.71 = bf16[32,8,1024]{2,1,0:T(8,128)(2,1)S(1)} all-to-all(bf16[32,8,1024]{2,1,0:T(8,128)(2,1)} %bitcast.39), channel_id=1, replica_groups=mesh['y'=4,'c'=2,'x'=4,'z'=8] {'x','z'}, dimensions={0} | all-to-all | bytes 1048576 | tf_op jit(solution)/shard_map/all_to_all | solution.py:332
  139.8 15.9 %shard_map.78.own = bf16[512,384]{1,0:T(8,128)(2,1)} custom-call(s32[2]{0:T(128)} %copy-done.3, bf16[4,512,1024]{2,1,0:T(8,128)(2,1)} %bitcast.34, bf16[2,192,4096]{2,1,0:T(8,128)(2,1)} %gate_own.5, bf16[192,4096]{1,0:T(8,128)(2,1)} %collective-permute-done.gate_other, bf16[2,192,4096]{2,1,0:T(8,128)(2,1)} %up_own.5, ...), custom_call_target="tpu_custom_call" | custom-call | flops 3221225472 | bytes 10485760 | tf_op jit(solution)/shard_map/pallas_call | solution.py:266
  158.4 16.5 %collective-permute-done.3.low = bf16[512,384]{1,0:T(8,128)(2,1)S(1)} collective-permute-done((bf16[512,384]{1,0:T(8,128)(2,1)}, bf16[512,384]{1,0:T(8,128)(2,1)S(1)}, u32[]{:S(2)}, u32[]{:S(2)}) %collective-permute-start.3) | collective-permute-done | bytes 393248 | tf_op jit(solution)/shard_map/ppermute | solution.py:196
  175.0 2.9 %collective-permute-start.6 = (bf16[256,384]{1,0:T(8,128)(2,1)S(1)}, bf16[256,384]{1,0:T(8,128)(2,1)S(1)}, u32[]{:S(2)}, u32[]{:S(2)}) collective-permute-start(bf16[256,384]{1,0:T(8,128)(2,1)S(1)} %slice.9), channel_id=1, source_target_pairs={{0,192},{64,0},{128,64},{192,128},{1,193},{65,1},{129,65},{193,129... | collective-permute-start | bytes 589832 | tf_op jit(solution)/shard_map/ppermute | solution.py:196
  177.9 6.0 %collective-permute-done.5.far_top = bf16[256,384]{1,0:T(8,128)(2,1)S(1)} collective-permute-done((bf16[256,384]{1,0:T(8,128)(2,1)S(1)}, bf16[256,384]{1,0:T(8,128)(2,1)S(1)}, u32[]{:S(2)}, u32[]{:S(2)}) %collective-permute-start.5) | collective-permute-done | bytes 196640 | tf_op jit(solution)/shard_map/ppermute | solution.py:196
  185.3 6.3 %shard_map.79 = bf16[512,1024]{1,0:T(8,128)(2,1)} custom-call(s32[2]{0:T(128)} %copy-done.3, bf16[2,1536,512]{2,1,0:T(8,128)(2,1)} %down_own.5, bf16[1536,512]{1,0:T(8,128)(2,1)} %copy-done.7, bf16[512,384]{1,0:T(8,128)(2,1)} %shard_map.78.own, bf16[512,384]{1,0:T(8,128)(2,1)} %copy-done.10, bf16[512,384]{1,0:T(8,128)(2,1)} %copy-done.11, ...), custom_call_target="tpu_custom_call" | custom-call | flops 1610612736 | bytes 4194304 | tf_op jit(solution)/shard_map/pallas_call | solution.py:291
  191.6 10.0 %all-to-all-start.4 = ((bf16[32,16,1024]{2,1,0:T(8,128)(2,1)}), bf16[32,16,1024]{2,1,0:T(8,128)(2,1)S(1)}, u32[]{:S(2)}, u32[]{:S(2)}) async-start(bf16[32,16,1024]{2,1,0:T(8,128)(2,1)} %bitcast.35), calls=%async_computation.4 | async-start | bytes 2097152 | tf_op jit(solution)/shard_map/all_to_all | solution.py:332
  201.6 10.8 %shard_map.81 = bf16[256,384]{1,0:T(8,128)(2,1)} custom-call(s32[2]{0:T(128)} %copy-done.3, bf16[4,256,1024]{2,1,0:T(8,128)(2,1)} %bitcast.42, bf16[2,192,4096]{2,1,0:T(8,128)(2,1)} %gate_own.5, bf16[192,4096]{1,0:T(8,128)(2,1)} %collective-permute-done.gate_other, bf16[2,192,4096]{2,1,0:T(8,128)(2,1)} %up_own.5, ...), custom_call_target="tpu_custom_call" | custom-call | flops 1610612736 | bytes 8388608 | tf_op jit(solution)/shard_map/pallas_call | solution.py:266
  212.4 13.2 %all-gather.4 = bf16[1024,384]{1,0:T(8,128)(2,1)} all-gather(bf16[256,384]{1,0:T(8,128)(2,1)} %shard_map.81), channel_id=6, replica_groups=mesh['y'=4,'c'=2,'x'=4,'z'=8] {'y'}, dimensions={0}, use_global_device_ids=true | all-gather | bytes 983040 | tf_op jit(solution)/shard_map/all_gather | solution.py:328
  225.6 6.3 %shard_map.82 = bf16[256,1024]{1,0:T(8,128)(2,1)} custom-call(s32[2]{0:T(128)} %copy-done.3, bf16[4,256,384]{2,1,0:T(8,128)(2,1)} %bitcast.37, bf16[2,1536,512]{2,1,0:T(8,128)(2,1)} %down_own.5, bf16[1536,512]{1,0:T(8,128)(2,1)} %copy-done.7), custom_call_target="tpu_custom_call" | custom-call | flops 805306368 | bytes 3670016 | tf_op jit(solution)/shard_map/pallas_call | solution.py:312
  231.9 8.9 %all-to-all-start.5 = ((bf16[32,8,1024]{2,1,0:T(8,128)(2,1)}), bf16[32,8,1024]{2,1,0:T(8,128)(2,1)S(1)}, u32[]{:S(2)}, u32[]{:S(2)}) async-start(bf16[32,8,1024]{2,1,0:T(8,128)(2,1)} %bitcast.38), calls=%async_computation.5 | async-start | bytes 1048576 | tf_op jit(solution)/shard_map/all_to_all | solution.py:332
  244.1 5.6 %collective-permute-start.7 = (bf16[128,512]{1,0:T(8,128)(2,1)S(1)}, bf16[128,512]{1,0:T(8,128)(2,1)S(1)}, u32[]{:S(2)}, u32[]{:S(2)}) collective-permute-start(bf16[128,512]{1,0:T(8,128)(2,1)S(1)} %get-tuple-element.55), channel_id=1, source_target_pairs={{0,32},{32,0},{1,33},{33,1},{2,34},{34,2},{3,35},{35,3},{4,36},{36... | collective-permute-start | bytes 393224 | tf_op jit(solution)/shard_map/ppermute | solution.py:345
  249.7 2.5 all-to-all-done.5
  253.0 8.1 %collective-permute-start.8 = (bf16[128,512]{1,0:T(8,128)(2,1)S(1)}, bf16[128,512]{1,0:T(8,128)(2,1)S(1)}, u32[]{:S(2)}, u32[]{:S(2)}) collective-permute-start(bf16[128,512]{1,0:T(8,128)(2,1)S(1)} %get-tuple-element.60), channel_id=1, source_target_pairs={{0,32},{32,0},{1,33},{33,1},{2,34},{34,2},{3,35},{35,3},{4,36},{36... | collective-permute-start | bytes 393224 | tf_op jit(solution)/shard_map/ppermute | solution.py:345
  (61 shorter events, 21.6 us)
Async XLA Ops:
  6.5 16.6 %copy-start.6 = (s32[128,8]{0,1:T(8,128)S(1)}, s32[128,8]{0,1:T(8,128)}, u32[]{:S(2)}) copy-start(s32[128,8]{0,1:T(8,128)} %param.10) | copy-start | bytes 12292
  7.3 20.6 %copy-start.3 = (s32[2]{0:T(128)}, s32[2]{0:T(128)S(1)}, u32[]{:S(2)}) copy-start(s32[2]{0:T(128)S(1)} %pad_add_fusion.pos) | copy-start | bytes 28
  7.3 1.2 copy-start
  11.2 26.2 %all-to-all-start = ((bf16[32,8,1024]{2,1,0:T(8,128)(2,1)}), bf16[32,8,1024]{2,1,0:T(8,128)(2,1)S(1)}, u32[]{:S(2)}, u32[]{:S(2)}) async-start(bf16[32,8,1024]{2,1,0:T(8,128)(2,1)} %bitcast.6), calls=%async_computation | async-start | bytes 1048576 | tf_op jit(solution)/shard_map/all_to_all | solution.py:226
  23.1 48.8 %all-gather.9.cloned.1.call-start = ((), (), s32[]{:S(2)}) async-start(), calls=%async_computation.6 | async-start | bytes 2621440 | tf_op jit(solution)/shard_map/all_gather | solution.py:261
  38.2 101.6 %all-gather.11.cloned.1.call-start = ((), (), s32[]{:S(2)}) async-start(), calls=%async_computation.7 | async-start | bytes 5242880 | tf_op jit(solution)/shard_map/all_gather | solution.py:261
  71.9 10.9 %collective-permute-start = (bf16[192,4096]{1,0:T(8,128)(2,1)}, bf16[192,4096]{1,0:T(8,128)(2,1)}, u32[]{:S(2)}, u32[]{:S(2)}) collective-permute-start(bf16[192,4096]{1,0:T(8,128)(2,1)} %get-tuple-element.46), channel_id=1, source_target_pairs={{0,32},{32,0},{1,33},{33,1},{2,34},{34,2},{3,35},{35,3},{4,36},{36... | collective-permute-start | bytes 4718600 | tf_op jit(solution)/shard_map/ppermute | solution.py:240
  75.5 7.9 %collective-permute-start.1 = (bf16[192,4096]{1,0:T(8,128)(2,1)}, bf16[192,4096]{1,0:T(8,128)(2,1)}, u32[]{:S(2)}, u32[]{:S(2)}) collective-permute-start(bf16[192,4096]{1,0:T(8,128)(2,1)} %get-tuple-element.47), channel_id=1, source_target_pairs={{0,32},{32,0},{1,33},{33,1},{2,34},{34,2},{3,35},{35,3},{4,36},{36... | collective-permute-start | bytes 4718600 | tf_op jit(solution)/shard_map/ppermute | solution.py:240
  75.6 37.6 %collective-permute-start.2 = (bf16[1536,512]{1,0:T(8,128)(2,1)}, bf16[1536,512]{1,0:T(8,128)(2,1)S(1)}, u32[]{:S(2)}, u32[]{:S(2)}) collective-permute-start(bf16[1536,512]{1,0:T(8,128)(2,1)} %dynamic-slice_bitcast_fusion), channel_id=1, source_target_pairs={{0,32},{32,0},{1,33},{33,1},{2,34},{34,2},{3,35},{35,3},{4,36},{36... | collective-permute-start | bytes 4718600 | tf_op jit(solution)/shard_map/ppermute | solution.py:240
  76.0 44.5 %all-to-all-start.2 = ((bf16[32,8,1024]{2,1,0:T(8,128)(2,1)}), bf16[32,8,1024]{2,1,0:T(8,128)(2,1)S(1)}, u32[]{:S(2)}, u32[]{:S(2)}) async-start(bf16[32,8,1024]{2,1,0:T(8,128)(2,1)} %bitcast.13), calls=%async_computation.2 | async-start | bytes 1048576 | tf_op jit(solution)/shard_map/all_to_all | solution.py:243
  82.7 118.9 %all-gather.13.cloned.1.call-start = ((), (), s32[]{:S(2)}) async-start(), calls=%async_computation.8 | async-start | bytes 2621440 | tf_op jit(solution)/shard_map/all_gather | solution.py:261
  120.5 19.3 %copy-start.8 = (bf16[32,8,1024]{2,1,0:T(8,128)(2,1)}, bf16[32,8,1024]{2,1,0:T(8,128)(2,1)S(1)}, u32[]{:S(2)}) copy-start(bf16[32,8,1024]{2,1,0:T(8,128)(2,1)S(1)} %all-to-all-done.2) | copy-start | bytes 1572868
  155.7 19.2 %collective-permute-start.3 = (bf16[512,384]{1,0:T(8,128)(2,1)}, bf16[512,384]{1,0:T(8,128)(2,1)S(1)}, u32[]{:S(2)}, u32[]{:S(2)}) collective-permute-start(bf16[512,384]{1,0:T(8,128)(2,1)} %shard_map.78.own), channel_id=1, source_target_pairs={{0,64},{64,128},{128,192},{192,0},{1,65},{65,129},{129,193},{193,1... | collective-permute-start | bytes 1179656 | tf_op jit(solution)/shard_map/ppermute | solution.py:196
  156.2 18.7 %collective-permute-start.4 = (bf16[512,384]{1,0:T(8,128)(2,1)}, bf16[512,384]{1,0:T(8,128)(2,1)S(1)}, u32[]{:S(2)}, u32[]{:S(2)}) collective-permute-start(bf16[512,384]{1,0:T(8,128)(2,1)} %shard_map.78.own), channel_id=1, source_target_pairs={{0,192},{64,0},{128,64},{192,128},{1,193},{65,1},{129,65},{193,129... | collective-permute-start | bytes 1179656 | tf_op jit(solution)/shard_map/ppermute | solution.py:196
  174.8 9.1 %copy-start.10 = (bf16[512,384]{1,0:T(8,128)(2,1)}, bf16[512,384]{1,0:T(8,128)(2,1)S(1)}, u32[]{:S(2)}) copy-start(bf16[512,384]{1,0:T(8,128)(2,1)S(1)} %collective-permute-done.3.low) | copy-start | bytes 1179652
  174.9 9.1 %collective-permute-start.5 = (bf16[256,384]{1,0:T(8,128)(2,1)S(1)}, bf16[256,384]{1,0:T(8,128)(2,1)S(1)}, u32[]{:S(2)}, u32[]{:S(2)}) collective-permute-start(bf16[256,384]{1,0:T(8,128)(2,1)S(1)} %slice.8), channel_id=1, source_target_pairs={{0,64},{64,128},{128,192},{192,0},{1,65},{65,129},{129,193},{193,1... | collective-permute-start | bytes 589832 | tf_op jit(solution)/shard_map/ppermute | solution.py:196
  175.0 9.0 %copy-start.11 = (bf16[512,384]{1,0:T(8,128)(2,1)}, bf16[512,384]{1,0:T(8,128)(2,1)S(1)}, u32[]{:S(2)}) copy-start(bf16[512,384]{1,0:T(8,128)(2,1)S(1)} %collective-permute-done.4.high) | copy-start | bytes 1179652
  175.0 9.0 %collective-permute-start.6 = (bf16[256,384]{1,0:T(8,128)(2,1)S(1)}, bf16[256,384]{1,0:T(8,128)(2,1)S(1)}, u32[]{:S(2)}, u32[]{:S(2)}) collective-permute-start(bf16[256,384]{1,0:T(8,128)(2,1)S(1)} %slice.9), channel_id=1, source_target_pairs={{0,192},{64,0},{128,64},{192,128},{1,193},{65,1},{129,65},{193,129... | collective-permute-start | bytes 589832 | tf_op jit(solution)/shard_map/ppermute | solution.py:196
  191.6 40.3 %all-to-all-start.4 = ((bf16[32,16,1024]{2,1,0:T(8,128)(2,1)}), bf16[32,16,1024]{2,1,0:T(8,128)(2,1)S(1)}, u32[]{:S(2)}, u32[]{:S(2)}) async-start(bf16[32,16,1024]{2,1,0:T(8,128)(2,1)} %bitcast.35), calls=%async_computation.4 | async-start | bytes 2097152 | tf_op jit(solution)/shard_map/all_to_all | solution.py:332
  225.6 15.2 %copy-start.1 = (bf16[128,4096]{1,0:T(8,128)(2,1)S(1)}, bf16[128,4096]{1,0:T(8,128)(2,1)}, u32[]{:S(2)}) copy-start(bf16[128,4096]{1,0:T(8,128)(2,1)} %tokens.2) | copy-start | bytes 3145732
  225.6 15.2 %copy-start.4 = (s32[2]{0:T(128)S(1)}, s32[2]{0:T(128)}, u32[]{:S(2)}) copy-start(s32[2]{0:T(128)} %copy-done.3) | copy-start | bytes 28
  231.9 20.3 %all-to-all-start.5 = ((bf16[32,8,1024]{2,1,0:T(8,128)(2,1)}), bf16[32,8,1024]{2,1,0:T(8,128)(2,1)S(1)}, u32[]{:S(2)}, u32[]{:S(2)}) async-start(bf16[32,8,1024]{2,1,0:T(8,128)(2,1)} %bitcast.38), calls=%async_computation.5 | async-start | bytes 1048576 | tf_op jit(solution)/shard_map/all_to_all | solution.py:332
  244.1 17.0 %collective-permute-start.7 = (bf16[128,512]{1,0:T(8,128)(2,1)S(1)}, bf16[128,512]{1,0:T(8,128)(2,1)S(1)}, u32[]{:S(2)}, u32[]{:S(2)}) collective-permute-start(bf16[128,512]{1,0:T(8,128)(2,1)S(1)} %get-tuple-element.55), channel_id=1, source_target_pairs={{0,32},{32,0},{1,33},{33,1},{2,34},{34,2},{3,35},{35,3},{4,36},{36... | collective-permute-start | bytes 393224 | tf_op jit(solution)/shard_map/ppermute | solution.py:345
  253.0 9.1 %collective-permute-start.8 = (bf16[128,512]{1,0:T(8,128)(2,1)S(1)}, bf16[128,512]{1,0:T(8,128)(2,1)S(1)}, u32[]{:S(2)}, u32[]{:S(2)}) collective-permute-start(bf16[128,512]{1,0:T(8,128)(2,1)S(1)} %get-tuple-element.60), channel_id=1, source_target_pairs={{0,32},{32,0},{1,33},{33,1},{2,34},{34,2},{3,35},{35,3},{4,36},{36... | collective-permute-start | bytes 393224 | tf_op jit(solution)/shard_map/ppermute | solution.py:345
  (6 other events, 5.0 us)
Sparse Core Ops, SparseCore 0:
  38.3 33.5 all-gather.8
  73.7 57.1 all-gather.10
  139.9 43.5 all-gather.12

commit v4 on v2

--- a/solution.py
+++ b/solution.py
@@ -117,20 +117,18 @@
 def hidden_kernel(pos, blocks, gate_own, gate_other, up_own, up_other, out):
     quarter = blocks.shape[2]
     sums = [None] * 4
-    for index in range(NY):
-        block = blocks[index]
-        cols = slice(index * quarter, (index + 1) * quarter)
-        for which, rows in enumerate(
-            (gate_own[0, :, cols], up_own[0, :, cols], gate_other[:, cols], up_other[:, cols])
-        ):
-            step = by_rows(block, rows)
-            sums[which] = step if sums[which] is None else sums[which] + step
+    for y in range(NY):
+        block = blocks[y]
+        cols = slice(y * quarter, (y + 1) * quarter)
+        for which, weight in enumerate((gate_own, up_own, gate_other, up_other)):
+            term = by_rows(weight[:, cols], block)
+            sums[which] = term if y == 0 else sums[which] + term
     own, other = [
         gate / (1.0 + jnp.exp(-gate)) * up for gate, up in (sums[0:2], sums[2:4])
     ]
     low = jnp.where(pos[1] == 0, own, other)
     high = jnp.where(pos[1] == 0, other, own)
-    out[...] = jnp.concatenate([low, high], axis=1).astype(BF16)
+    out[...] = jnp.transpose(jnp.concatenate([low, high], axis=0)).astype(BF16)
 
 
 def down_kernel(pos, down_own, down_other, *refs):
@@ -142,10 +140,10 @@
         own = other = None
         for y in range(NY):
             span = slice(y * units, (y + 1) * units)
-            own_step = times(blocks[y], down_own[0, span, :])
-            other_step = times(blocks[y], down_other[span, :])
-            own = own_step if own is None else own + own_step
-            other = other_step if other is None else other + other_step
+            own_term = times(blocks[y], down_own[span, :])
+            other_term = times(blocks[y], down_other[span, :])
+            own = own_term if y == 0 else own + own_term
+            other = other_term if y == 0 else other + other_term
         for core, total in ((pos[1], own), (1 - pos[1], other)):
             out[at, pl.ds(pl.multiple_of(core * cols, cols), cols)] = total.astype(BF16)
 
@@ -192,11 +190,13 @@
         compiler_params=params(16),
         cost_estimate=cost(2 * count * sum(sizes) * quarter, sum(sizes) * quarter * 2),
     )(pos, part, turned)
-    sent = [
-        lax.dynamic_index_in_dim(array, 1 - pos[1], 0, keepdims=False)
-        for array in (w_gate, w_up, w_down)
+    arrays = (w_gate, w_up, w_down)
+    sent, own = [
+        [lax.dynamic_index_in_dim(array, core, 0, keepdims=False) for array in arrays]
+        for core in (1 - pos[1], pos[1])
     ]
     *sent, received[0] = lax.optimization_barrier((*sent, received[0]))
+    *own, received[0] = lax.optimization_barrier((*own, received[0]))
     others = [lax.ppermute(array, "c", [(0, 1), (1, 0)]) for array in sent]
     for rows in later_rows:
         rows, received[-1] = lax.optimization_barrier((rows, received[-1]))
@@ -219,6 +219,8 @@
             before = [done[i][j] for i, j in ((index - 1, 0), (index - 2, 1)) if i >= 0]
             mine, *before = lax.optimization_barrier((mine, *before))
         blocks = lax.all_gather(mine, "y", axis=0)
+        if index == 1:
+            blocks, returned[0] = lax.optimization_barrier((blocks, returned[0]))
         pieces = []
         for half in range(size // PIECE):
             hidden = pl.pallas_call(
@@ -229,30 +231,24 @@
                     in_specs=[
                         pl.BlockSpec(
                             (NY, PIECE, quarter), lambda step, pos, half=half: (0, half, 0)
-                        ),
-                        pl.BlockSpec((1, units // 2, width), lambda step, pos: (pos[1], 0, 0)),
-                        pl.BlockSpec((units // 2, width), lambda step, pos: (0, 0)),
-                        pl.BlockSpec((1, units // 2, width), lambda step, pos: (pos[1], 0, 0)),
-                        pl.BlockSpec((units // 2, width), lambda step, pos: (0, 0)),
-                    ],
+                        )
+                    ]
+                    + [pl.BlockSpec((units // 2, width), lambda step, pos: (0, 0))] * 4,
                     out_specs=pl.BlockSpec((PIECE, units), lambda step, pos: (0, 0)),
                 ),
                 out_shape=sds((PIECE, units), BF16),
-                compiler_params=params(32),
+                compiler_params=params(24),
                 cost_estimate=cost(
                     4 * PIECE * width * units, 4 * units * width + 2 * PIECE * width
                 ),
-            )(pos, blocks, w_gate, others[0], w_up, others[1])
+            )(pos, blocks, own[0], others[0], own[1], others[1])
             pieces.append(lax.all_gather(hidden, "y", axis=0))
         result = pl.pallas_call(
             down_kernel,
             grid_spec=pltpu.PrefetchScalarGridSpec(
                 num_scalar_prefetch=1,
                 grid=(1,),
-                in_specs=[
-                    pl.BlockSpec((1, ff, cols), lambda step, pos: (pos[1], 0, 0)),
-                    pl.BlockSpec((ff, cols), lambda step, pos: (0, 0)),
-                ]
+                in_specs=[pl.BlockSpec((ff, cols), lambda step, pos: (0, 0))] * 2
                 + [pl.BlockSpec((NY, PIECE, units), lambda step, pos: (0, 0, 0))] * len(pieces),
                 out_specs=pl.BlockSpec((size, NC * cols), lambda step, pos: (0, 0)),
             ),
@@ -261,7 +257,9 @@
             cost_estimate=cost(
                 2 * size * ff * NC * cols, 2 * ff * NC * cols + 2 * size * NC * cols
             ),
-        )(pos, w_down, others[2], *pieces)
+        )(pos, own[2], others[2], *pieces)
+        if index == 0:
+            result, received[-1] = lax.optimization_barrier((result, received[-1]))
         done.append((blocks, result))
         returned.append(lax.all_to_all(result, ("x", "z"), 0, 0, tiled=True))
 

time: 261 us -> 253 us (0.969)
  blocking collectives: 89.4 us -> 113 us
  waiting for transfers between devices: 26.8 us -> 6.48 us
  starting transfers between devices: 66.1 us -> 56.9 us
  local copies, waits for them, and re-layouts: 23.7 us -> 20.6 us
    all_to_all x0 -> x1, blocking collectives: none -> 22.1 us  [body(): returned.append(lax.all_to_all(result, ('x', 'z'), 0, 0, tiled=True))]
    all_gather x3, waiting for transfers between devices: 19.1 us -> 1.37 us  [body(): blocks = lax.all_gather(mine, 'y', axis=0)]
    all_to_all x3 -> x2, starting transfers between devices: 28.4 us -> 19.6 us  [body(): returned.append(lax.all_to_all(result, ('x', 'z'), 0, 0, tiled=True))]
    unnamed x38 -> x36, local copies, waits for them, and re-layouts: 16.8 us -> 13.9 us
  transfers between devices with their start and end apart: 13 -> 12, of which waited for: 5 -> 3; matrix products, arithmetic and copies ran while one was open for 2% -> 2% of each run, Pallas kernels for 15% -> 15%
where the time goes in v4:
time: 253 us; the launch traced here: 252 us
  blocking collectives  113 us (45%)
  starting transfers between devices  56.9 us (22%)
  Pallas kernels  40.7 us (16%)
  local copies, waits for them, and re-layouts  20.6 us (8%)
  between operations  13.3 us (5%)
  waiting for transfers between devices  6.48 us (3%)
    all_gather x4, blocking collectives, body(): pieces.append(lax.all_gather(hidden, 'y', axis=0))  59 us
    all_to_all x1, blocking collectives, body(): received.append(lax.all_to_all(rows, ('x', 'z'), 0, 0, tiled=True))  32.3 us
    pallas_call x4, Pallas kernels, body(): pl.pallas_call(hidden_kernel, grid_spec=pltpu.PrefetchScalarGridSpec(num_...  22.2 us
    all_to_all x1, blocking collectives, body(): returned.append(lax.all_to_all(result, ('x', 'z'), 0, 0, tiled=True))  22.1 us
    all_to_all x2, starting transfers between devices, body(): returned.append(lax.all_to_all(result, ('x', 'z'), 0, 0, tiled=True))  19.6 us
    ppermute x2, starting transfers between devices, body(): give = lax.ppermute(give, 'c', [(0, 1), (1, 0)])  14.2 us
    unnamed x36, local copies, waits for them, and re-layouts  13.9 us
    all_to_all x1, starting transfers between devices, body(): received = [lax.all_to_all(first_rows, ('x', 'z'), 0, 0, tiled=True)]  12 us
  transfers between devices with their start and end apart: 12, of which 3 were waited for; matrix products, arithmetic and copies ran while one was open for 2% of the time, Pallas kernels for 15%

profile of v4, /device:TPU:1, one launch (start us, length us, event | category | flops | bytes accessed | tf_op | source)
XLA Modules:
  0.0 252.2 jit_solution(2855239113310780623)
XLA Ops:
  11.2 12.0 %all-to-all-start = ((bf16[32,8,1024]{2,1,0:T(8,128)(2,1)}), bf16[32,8,1024]{2,1,0:T(8,128)(2,1)}, u32[]{:S(2)}, u32[]{:S(2)}) async-start(bf16[32,8,1024]{2,1,0:T(8,128)(2,1)} %bitcast.9), calls=%async_computation | async-start | bytes 1048576 | tf_op jit(solution)/shard_map/all_to_all | solution.py:184
  26.4 3.9 %dynamic-slice_bitcast_fusion = (bf16[1536,512]{1,0:T(8,128)(2,1)}, bf16[1536,512]{1,0:T(8,128)(2,1)}) fusion(bf16[2,1536,512]{2,1,0:T(8,128)(2,1)} %param.13, s32[]{:T(128)S(6)} %select_n.13, s32[]{:T(128)S(6)} %select_n.12), kind=kLoop, calls=%fused_computation | loop fusion | bytes 6291464 | tf_op jit(solution)/shard_map/jit(dynamic_index_in_dim)/squeeze | solution.py:195
  31.4 2.1 dynamic-slice_bitcast_fusion.1
  33.4 4.1 %all-to-all-done = bf16[32,8,1024]{2,1,0:T(8,128)(2,1)} async-done(((bf16[32,8,1024]{2,1,0:T(8,128)(2,1)}), bf16[32,8,1024]{2,1,0:T(8,128)(2,1)}, u32[]{:S(2)}, u32[]{:S(2)}) %all-to-all-start) | async-done | bytes 524320 | tf_op jit(solution)/shard_map/all_to_all | solution.py:184
  37.6 32.3 %all_to_all.70 = bf16[32,16,1024]{2,1,0:T(8,128)(2,1)} all-to-all(bf16[32,16,1024]{2,1,0:T(8,128)(2,1)} %bitcast.43), channel_id=1, replica_groups=mesh['y'=4,'c'=2,'x'=4,'z'=8] {'x','z'}, dimensions={0} | all-to-all | bytes 2097152 | tf_op jit(solution)/shard_map/all_to_all | solution.py:203
  71.2 3.9 %collective-permute-start.1 = (bf16[192,4096]{1,0:T(8,128)(2,1)}, bf16[192,4096]{1,0:T(8,128)(2,1)}, u32[]{:S(2)}, u32[]{:S(2)}) collective-permute-start(bf16[192,4096]{1,0:T(8,128)(2,1)} %get-tuple-element.54), channel_id=1, source_target_pairs={{0,32},{32,0},{1,33},{33,1},{2,34},{34,2},{3,35},{35,3},{4,36},{36... | collective-permute-start | bytes 4718600 | tf_op jit(solution)/shard_map/ppermute | solution.py:200
  75.6 6.6 %all-to-all-start.2 = ((bf16[32,8,1024]{2,1,0:T(8,128)(2,1)}), bf16[32,8,1024]{2,1,0:T(8,128)(2,1)}, u32[]{:S(2)}, u32[]{:S(2)}) async-start(bf16[32,8,1024]{2,1,0:T(8,128)(2,1)} %bitcast.47), calls=%async_computation.2 | async-start | bytes 1048576 | tf_op jit(solution)/shard_map/all_to_all | solution.py:203
  83.9 5.8 %shard_map.76 = bf16[256,384]{1,0:T(8,128)(2,1)S(1)} custom-call(s32[2]{0:T(128)S(1)} %pad_add_fusion.pos, bf16[4,256,1024]{2,1,0:T(8,128)(2,1)S(1)} %bitcast.41, bf16[192,4096]{1,0:T(8,128)(2,1)S(1)} %get-tuple-element.53.gate_own, bf16[192,4096]{1,0:T(8,128)(2,1)} %collective-permute-done.1.gate_other, bf16[192,4096]{1,0:T(8,128)(2,1)S(1)} %get-tuple-element.55.up_own, ...), custom_call_target="tpu_custom_call" | custom-call | flops 1610612736 | bytes 8388608 | tf_op jit(solution)/shard_map/pallas_call | solution.py:226
  89.7 17.0 %all-gather.2 = bf16[1024,384]{1,0:T(8,128)(2,1)S(1)} all-gather(bf16[256,384]{1,0:T(8,128)(2,1)S(1)} %shard_map.76), channel_id=4, replica_groups=mesh['y'=4,'c'=2,'x'=4,'z'=8] {'y'}, dimensions={0}, use_global_device_ids=true | all-gather | bytes 983040 | tf_op jit(solution)/shard_map/all_gather | solution.py:245
  106.7 3.2 %shard_map.77 = bf16[256,1024]{1,0:T(8,128)(2,1)S(1)} custom-call(s32[2]{0:T(128)S(1)} %pad_add_fusion.pos, bf16[1536,512]{1,0:T(8,128)(2,1)S(1)} %copy-done.1, bf16[1536,512]{1,0:T(8,128)(2,1)} %collective-permute-done.down_other, bf16[4,256,384]{2,1,0:T(8,128)(2,1)S(1)} %bitcast.36), custom_call_target="tpu_custom_call" | custom-call | flops 805306368 | bytes 3670016 | tf_op jit(solution)/shard_map/pallas_call | solution.py:246
  110.7 22.1 %all_to_all.71 = bf16[32,8,1024]{2,1,0:T(8,128)(2,1)} all-to-all(bf16[32,8,1024]{2,1,0:T(8,128)(2,1)} %bitcast.38), channel_id=1, replica_groups=mesh['y'=4,'c'=2,'x'=4,'z'=8] {'x','z'}, dimensions={0} | all-to-all | bytes 1048576 | tf_op jit(solution)/shard_map/all_to_all | solution.py:264
  132.8 2.2 copy-done
  135.0 5.5 %shard_map.78 = bf16[256,384]{1,0:T(8,128)(2,1)S(1)} custom-call(s32[2]{0:T(128)S(1)} %pad_add_fusion.pos, bf16[4,512,1024]{2,1,0:T(8,128)(2,1)S(1)} %bitcast.34, bf16[192,4096]{1,0:T(8,128)(2,1)S(1)} %get-tuple-element.53.gate_own, bf16[192,4096]{1,0:T(8,128)(2,1)} %collective-permute-done.1.gate_other, bf16[192,4096]{1,0:T(8,128)(2,1)S(1)} %get-tuple-element.55.up_own, ...), custom_call_target="tpu_custom_call" | custom-call | flops 1610612736 | bytes 8388608 | tf_op jit(solution)/shard_map/pallas_call | solution.py:226
  140.5 5.5 %shard_map.79 = bf16[256,384]{1,0:T(8,128)(2,1)S(1)} custom-call(s32[2]{0:T(128)S(1)} %pad_add_fusion.pos, bf16[4,512,1024]{2,1,0:T(8,128)(2,1)S(1)} %bitcast.35, bf16[192,4096]{1,0:T(8,128)(2,1)S(1)} %get-tuple-element.53.gate_own, bf16[192,4096]{1,0:T(8,128)(2,1)} %collective-permute-done.1.gate_other, bf16[192,4096]{1,0:T(8,128)(2,1)S(1)} %get-tuple-element.55.up_own, ...), custom_call_target="tpu_custom_call" | custom-call | flops 1610612736 | bytes 8388608 | tf_op jit(solution)/shard_map/pallas_call | solution.py:226
  146.1 15.8 %all-gather.3 = bf16[1024,384]{1,0:T(8,128)(2,1)S(1)} all-gather(bf16[256,384]{1,0:T(8,128)(2,1)S(1)} %shard_map.78), channel_id=5, replica_groups=mesh['y'=4,'c'=2,'x'=4,'z'=8] {'y'}, dimensions={0}, use_global_device_ids=true | all-gather | bytes 983040 | tf_op jit(solution)/shard_map/all_gather | solution.py:245
  161.8 14.5 %all-gather.4 = bf16[1024,384]{1,0:T(8,128)(2,1)S(1)} all-gather(bf16[256,384]{1,0:T(8,128)(2,1)S(1)} %shard_map.79), channel_id=6, replica_groups=mesh['y'=4,'c'=2,'x'=4,'z'=8] {'y'}, dimensions={0}, use_global_device_ids=true | all-gather | bytes 983040 | tf_op jit(solution)/shard_map/all_gather | solution.py:245
  176.4 4.3 %shard_map.80 = bf16[512,1024]{1,0:T(8,128)(2,1)S(1)} custom-call(s32[2]{0:T(128)S(1)} %pad_add_fusion.pos, bf16[1536,512]{1,0:T(8,128)(2,1)S(1)} %copy-done.2, bf16[1536,512]{1,0:T(8,128)(2,1)} %collective-permute-done.down_other, bf16[4,256,384]{2,1,0:T(8,128)(2,1)S(1)} %bitcast.45, bf16[4,256,384]{2,1,0:T(8,128)(2,1)S(1)} %bitcast.46), custom_call_target="tpu_custom_call" | custom-call | flops 1610612736 | bytes 4194304 | tf_op jit(solution)/shard_map/pallas_call | solution.py:246
  181.6 10.3 %all-to-all-start.4 = ((bf16[32,16,1024]{2,1,0:T(8,128)(2,1)}), bf16[32,16,1024]{2,1,0:T(8,128)(2,1)}, u32[]{:S(2)}, u32[]{:S(2)}) async-start(bf16[32,16,1024]{2,1,0:T(8,128)(2,1)} %bitcast.44), calls=%async_computation.4 | async-start | bytes 2097152 | tf_op jit(solution)/shard_map/all_to_all | solution.py:264
  193.6 5.4 %shard_map.82 = bf16[256,384]{1,0:T(8,128)(2,1)S(1)} custom-call(s32[2]{0:T(128)S(1)} %pad_add_fusion.pos, bf16[4,256,1024]{2,1,0:T(8,128)(2,1)S(1)} %bitcast.42, bf16[192,4096]{1,0:T(8,128)(2,1)S(1)} %get-tuple-element.53.gate_own, bf16[192,4096]{1,0:T(8,128)(2,1)} %collective-permute-done.1.gate_other, bf16[192,4096]{1,0:T(8,128)(2,1)S(1)} %get-tuple-element.55.up_own, ...), custom_call_target="tpu_custom_call" | custom-call | flops 1610612736 | bytes 8388608 | tf_op jit(solution)/shard_map/pallas_call | solution.py:226
  199.0 11.6 %all-gather.6 = bf16[1024,384]{1,0:T(8,128)(2,1)S(1)} all-gather(bf16[256,384]{1,0:T(8,128)(2,1)S(1)} %shard_map.82), channel_id=8, replica_groups=mesh['y'=4,'c'=2,'x'=4,'z'=8] {'y'}, dimensions={0}, use_global_device_ids=true | all-gather | bytes 983040 | tf_op jit(solution)/shard_map/all_gather | solution.py:245
  210.6 4.0 %shard_map.83 = bf16[256,1024]{1,0:T(8,128)(2,1)} custom-call(s32[2]{0:T(128)S(1)} %pad_add_fusion.pos, bf16[1536,512]{1,0:T(8,128)(2,1)S(1)} %copy-done.3, bf16[1536,512]{1,0:T(8,128)(2,1)} %collective-permute-done.down_other, bf16[4,256,384]{2,1,0:T(8,128)(2,1)S(1)} %bitcast.37), custom_call_target="tpu_custom_call" | custom-call | flops 805306368 | bytes 3670016 | tf_op jit(solution)/shard_map/pallas_call | solution.py:246
  214.6 9.3 %all-to-all-start.5 = ((bf16[32,8,1024]{2,1,0:T(8,128)(2,1)}), bf16[32,8,1024]{2,1,0:T(8,128)(2,1)S(1)}, u32[]{:S(2)}, u32[]{:S(2)}) async-start(bf16[32,8,1024]{2,1,0:T(8,128)(2,1)} %bitcast.26), calls=%async_computation.5 | async-start | bytes 1048576 | tf_op jit(solution)/shard_map/all_to_all | solution.py:264
  228.9 6.4 %collective-permute-start.3 = (bf16[128,512]{1,0:T(8,128)(2,1)S(1)}, bf16[128,512]{1,0:T(8,128)(2,1)S(1)}, u32[]{:S(2)}, u32[]{:S(2)}) collective-permute-start(bf16[128,512]{1,0:T(8,128)(2,1)S(1)} %get-tuple-element.63), channel_id=1, source_target_pairs={{0,32},{32,0},{1,33},{33,1},{2,34},{34,2},{3,35},{35,3},{4,36},{36... | collective-permute-start | bytes 393224 | tf_op jit(solution)/shard_map/ppermute | solution.py:277
  236.1 7.8 %collective-permute-start.4 = (bf16[128,512]{1,0:T(8,128)(2,1)S(1)}, bf16[128,512]{1,0:T(8,128)(2,1)S(1)}, u32[]{:S(2)}, u32[]{:S(2)}) collective-permute-start(bf16[128,512]{1,0:T(8,128)(2,1)S(1)} %get-tuple-element.68), channel_id=1, source_target_pairs={{0,32},{32,0},{1,33},{33,1},{2,34},{34,2},{3,35},{35,3},{4,36},{36... | collective-permute-start | bytes 393224 | tf_op jit(solution)/shard_map/ppermute | solution.py:277
  (62 shorter events, 23.4 us)
Async XLA Ops:
  7.3 1.2 copy-start.4
  11.2 26.3 %all-to-all-start = ((bf16[32,8,1024]{2,1,0:T(8,128)(2,1)}), bf16[32,8,1024]{2,1,0:T(8,128)(2,1)}, u32[]{:S(2)}, u32[]{:S(2)}) async-start(bf16[32,8,1024]{2,1,0:T(8,128)(2,1)} %bitcast.9), calls=%async_computation | async-start | bytes 1048576 | tf_op jit(solution)/shard_map/all_to_all | solution.py:184
  23.2 48.0 %all-gather.11.cloned.1.call-start = ((), (), s32[]{:S(2)}) async-start(), calls=%async_computation.6 | async-start | bytes 2621440 | tf_op jit(solution)/shard_map/all_gather | solution.py:221
  26.4 3.9 %copy-start.16 = (bf16[2,192,4096]{2,1,0:T(8,128)(2,1)S(1)}, bf16[2,192,4096]{2,1,0:T(8,128)(2,1)}, u32[]{:S(2)}) copy-start(bf16[2,192,4096]{2,1,0:T(8,128)(2,1)} %param.12) | copy-start | bytes 9437188
  26.4 4.9 %copy-start.17 = (bf16[2,192,4096]{2,1,0:T(8,128)(2,1)S(1)}, bf16[2,192,4096]{2,1,0:T(8,128)(2,1)}, u32[]{:S(2)}) copy-start(bf16[2,192,4096]{2,1,0:T(8,128)(2,1)} %param.11) | copy-start | bytes 9437188
  37.5 95.2 %all-gather.13.cloned.1.call-start = ((), (), s32[]{:S(2)}) async-start(), calls=%async_computation.7 | async-start | bytes 5242880 | tf_op jit(solution)/shard_map/all_gather | solution.py:221
  71.2 11.0 %collective-permute-start.1 = (bf16[192,4096]{1,0:T(8,128)(2,1)}, bf16[192,4096]{1,0:T(8,128)(2,1)}, u32[]{:S(2)}, u32[]{:S(2)}) collective-permute-start(bf16[192,4096]{1,0:T(8,128)(2,1)} %get-tuple-element.54), channel_id=1, source_target_pairs={{0,32},{32,0},{1,33},{33,1},{2,34},{34,2},{3,35},{35,3},{4,36},{36... | collective-permute-start | bytes 4718600 | tf_op jit(solution)/shard_map/ppermute | solution.py:200
  75.1 7.2 %collective-permute-start.2 = (bf16[192,4096]{1,0:T(8,128)(2,1)}, bf16[192,4096]{1,0:T(8,128)(2,1)}, u32[]{:S(2)}, u32[]{:S(2)}) collective-permute-start(bf16[192,4096]{1,0:T(8,128)(2,1)} %get-tuple-element.56), channel_id=1, source_target_pairs={{0,32},{32,0},{1,33},{33,1},{2,34},{34,2},{3,35},{35,3},{4,36},{36... | collective-permute-start | bytes 4718600 | tf_op jit(solution)/shard_map/ppermute | solution.py:200
  75.2 31.5 %collective-permute-start = (bf16[1536,512]{1,0:T(8,128)(2,1)}, bf16[1536,512]{1,0:T(8,128)(2,1)}, u32[]{:S(2)}, u32[]{:S(2)}) collective-permute-start(bf16[1536,512]{1,0:T(8,128)(2,1)} %get-tuple-element.52), channel_id=1, source_target_pairs={{0,32},{32,0},{1,33},{33,1},{2,34},{34,2},{3,35},{35,3},{4,36},{36... | collective-permute-start | bytes 4718600 | tf_op jit(solution)/shard_map/ppermute | solution.py:200
  75.6 35.1 %all-to-all-start.2 = ((bf16[32,8,1024]{2,1,0:T(8,128)(2,1)}), bf16[32,8,1024]{2,1,0:T(8,128)(2,1)}, u32[]{:S(2)}, u32[]{:S(2)}) async-start(bf16[32,8,1024]{2,1,0:T(8,128)(2,1)} %bitcast.47), calls=%async_computation.2 | async-start | bytes 1048576 | tf_op jit(solution)/shard_map/all_to_all | solution.py:203
  82.2 109.8 %all-gather.15.cloned.1.call-start = ((), (), s32[]{:S(2)}) async-start(), calls=%async_computation.8 | async-start | bytes 2621440 | tf_op jit(solution)/shard_map/all_gather | solution.py:221
  82.3 1.6 copy-start.8
  83.9 22.8 %copy-start.1 = (bf16[1536,512]{1,0:T(8,128)(2,1)S(1)}, bf16[1536,512]{1,0:T(8,128)(2,1)}, u32[]{:S(2)}) copy-start(bf16[1536,512]{1,0:T(8,128)(2,1)} %get-tuple-element.51.down_own) | copy-start | bytes 4718596
  132.8 2.2 copy-start
  146.0 30.3 %copy-start.2 = (bf16[1536,512]{1,0:T(8,128)(2,1)S(1)}, bf16[1536,512]{1,0:T(8,128)(2,1)}, u32[]{:S(2)}) copy-start(bf16[1536,512]{1,0:T(8,128)(2,1)} %get-tuple-element.51.down_own) | copy-start | bytes 4718596
  181.6 33.0 %all-to-all-start.4 = ((bf16[32,16,1024]{2,1,0:T(8,128)(2,1)}), bf16[32,16,1024]{2,1,0:T(8,128)(2,1)}, u32[]{:S(2)}, u32[]{:S(2)}) async-start(bf16[32,16,1024]{2,1,0:T(8,128)(2,1)} %bitcast.44), calls=%async_computation.4 | async-start | bytes 2097152 | tf_op jit(solution)/shard_map/all_to_all | solution.py:264
  192.0 1.6 copy-start.9
  193.6 17.0 %copy-start.3 = (bf16[1536,512]{1,0:T(8,128)(2,1)S(1)}, bf16[1536,512]{1,0:T(8,128)(2,1)}, u32[]{:S(2)}) copy-start(bf16[1536,512]{1,0:T(8,128)(2,1)} %get-tuple-element.51.down_own) | copy-start | bytes 4718596
  210.6 13.3 %copy-start.15 = (s32[128,8]{0,1:T(8,128)S(1)}, s32[128,8]{0,1:T(8,128)}, u32[]{:S(2)}) copy-start(s32[128,8]{0,1:T(8,128)} %param.10) | copy-start | bytes 12292
  214.6 9.3 %copy-start.5 = (bf16[128,4096]{1,0:T(8,128)(2,1)S(1)}, bf16[128,4096]{1,0:T(8,128)(2,1)}, u32[]{:S(2)}) copy-start(bf16[128,4096]{1,0:T(8,128)(2,1)} %tokens.2) | copy-start | bytes 3145732
  214.6 20.7 %all-to-all-start.5 = ((bf16[32,8,1024]{2,1,0:T(8,128)(2,1)}), bf16[32,8,1024]{2,1,0:T(8,128)(2,1)S(1)}, u32[]{:S(2)}, u32[]{:S(2)}) async-start(bf16[32,8,1024]{2,1,0:T(8,128)(2,1)} %bitcast.26), calls=%async_computation.5 | async-start | bytes 1048576 | tf_op jit(solution)/shard_map/all_to_all | solution.py:264
  223.9 1.0 copy-start.12
  228.9 15.0 %collective-permute-start.3 = (bf16[128,512]{1,0:T(8,128)(2,1)S(1)}, bf16[128,512]{1,0:T(8,128)(2,1)S(1)}, u32[]{:S(2)}, u32[]{:S(2)}) collective-permute-start(bf16[128,512]{1,0:T(8,128)(2,1)S(1)} %get-tuple-element.63), channel_id=1, source_target_pairs={{0,32},{32,0},{1,33},{33,1},{2,34},{34,2},{3,35},{35,3},{4,36},{36... | collective-permute-start | bytes 393224 | tf_op jit(solution)/shard_map/ppermute | solution.py:277
  236.1 8.8 %collective-permute-start.4 = (bf16[128,512]{1,0:T(8,128)(2,1)S(1)}, bf16[128,512]{1,0:T(8,128)(2,1)S(1)}, u32[]{:S(2)}, u32[]{:S(2)}) collective-permute-start(bf16[128,512]{1,0:T(8,128)(2,1)S(1)} %get-tuple-element.68), channel_id=1, source_target_pairs={{0,32},{32,0},{1,33},{33,1},{2,34},{34,2},{3,35},{35,3},{4,36},{36... | collective-permute-start | bytes 393224 | tf_op jit(solution)/shard_map/ppermute | solution.py:277
  (6 other events, 5.3 us)
Sparse Core Ops, SparseCore 0:
  37.6 33.5 all-gather.10
  73.0 57.1 all-gather.12
  132.9 41.6 all-gather.14

commit v5 on v4

--- a/solution.py
+++ b/solution.py
@@ -114,11 +114,12 @@
         out[...] = jnp.transpose(spread(place, dense, first, size)).astype(BF16)
 
 
-def hidden_kernel(pos, blocks, gate_own, gate_other, up_own, up_other, out):
+def hidden_kernel(half, pos, blocks, gate_own, gate_other, up_own, up_other, out):
     quarter = blocks.shape[2]
+    rows = slice(half * PIECE, (half + 1) * PIECE)
     sums = [None] * 4
     for y in range(NY):
-        block = blocks[y]
+        block = blocks[y, rows, :]
         cols = slice(y * quarter, (y + 1) * quarter)
         for which, weight in enumerate((gate_own, up_own, gate_other, up_other)):
             term = by_rows(weight[:, cols], block)
@@ -131,21 +132,39 @@
     out[...] = jnp.transpose(jnp.concatenate([low, high], axis=0)).astype(BF16)
 
 
-def down_kernel(pos, down_own, down_other, *refs):
+def store_columns(pos, out, at, own, other):
+    cols = own.shape[1]
+    for core, total in ((pos[1], own), (1 - pos[1], other)):
+        out[at, pl.ds(pl.multiple_of(core * cols, cols), cols)] = total.astype(BF16)
+
+
+def down_kernel(pos, down_own, down_other, blocks, out):
+    rows, units = blocks.shape[1:]
+    own = other = None
+    for y in range(NY):
+        span = slice(y * units, (y + 1) * units)
+        own_term = times(blocks[y], down_own[span, :])
+        other_term = times(blocks[y], down_other[span, :])
+        own = own_term if y == 0 else own + own_term
+        other = other_term if y == 0 else other + other_term
+    store_columns(pos, out, slice(0, rows), own, other)
+
+
+def down_ring_kernel(pos, down_own, down_other, *refs):
     out = refs[-1]
-    cols = down_other.shape[1]
-    for index, blocks in enumerate(refs[:-1]):
-        rows, units = blocks.shape[1:]
-        at = slice(index * rows, (index + 1) * rows)
-        own = other = None
-        for y in range(NY):
-            span = slice(y * units, (y + 1) * units)
-            own_term = times(blocks[y], down_own[span, :])
-            other_term = times(blocks[y], down_other[span, :])
-            own = own_term if y == 0 else own + own_term
-            other = other_term if y == 0 else other + other_term
-        for core, total in ((pos[1], own), (1 - pos[1], other)):
-            out[at, pl.ds(pl.multiple_of(core * cols, cols), cols)] = total.astype(BF16)
+    for index in range(len(refs) // 5):
+        own, low, high, far_top, far_bottom = refs[5 * index : 5 * index + 5]
+        rows, units = own.shape
+        far = jnp.concatenate([far_top[...], far_bottom[...]], axis=0)
+        mine = theirs = None
+        for block, step in ((own[...], 0), (low[...], 3), (high[...], 1), (far, 2)):
+            at = lax.rem(pos[0] + step, NY)
+            span = pl.ds(pl.multiple_of(at * units, units), units)
+            own_term = times(block, down_own[span, :])
+            other_term = times(block, down_other[span, :])
+            mine = own_term if mine is None else mine + own_term
+            theirs = other_term if theirs is None else theirs + other_term
+        store_columns(pos, out, slice(index * rows, (index + 1) * rows), mine, theirs)
 
 
 def combine_kernel(pos, *refs):
@@ -159,6 +178,17 @@
             step = times(refs[2 * index][...], refs[2 * index + 1][:, at])
             total = step if total is None else total + step
         out[...] = total.astype(out.dtype)
+
+
+def turn(array, step):
+    return lax.ppermute(array, "y", [(i, (i + step) % NY) for i in range(NY)])
+
+
+def ring(block):
+    half = block.shape[0] // 2
+    low = turn(block, 1)
+    high = turn(block, -1)
+    return block, low, high, turn(low[:half], 1), turn(high[half:], -1)
 
 
 def body(tokens, norm_gain, router, routes, w_gate, w_up, w_down):
@@ -224,35 +254,24 @@
         pieces = []
         for half in range(size // PIECE):
             hidden = pl.pallas_call(
-                hidden_kernel,
-                grid_spec=pltpu.PrefetchScalarGridSpec(
-                    num_scalar_prefetch=1,
-                    grid=(1,),
-                    in_specs=[
-                        pl.BlockSpec(
-                            (NY, PIECE, quarter), lambda step, pos, half=half: (0, half, 0)
-                        )
-                    ]
-                    + [pl.BlockSpec((units // 2, width), lambda step, pos: (0, 0))] * 4,
-                    out_specs=pl.BlockSpec((PIECE, units), lambda step, pos: (0, 0)),
-                ),
+                functools.partial(hidden_kernel, half),
                 out_shape=sds((PIECE, units), BF16),
+                in_specs=[SMEM] + [VMEM] * 5,
+                out_specs=VMEM,
                 compiler_params=params(24),
                 cost_estimate=cost(
                     4 * PIECE * width * units, 4 * units * width + 2 * PIECE * width
                 ),
             )(pos, blocks, own[0], others[0], own[1], others[1])
-            pieces.append(lax.all_gather(hidden, "y", axis=0))
+            if size > PIECE:
+                pieces.extend(ring(hidden))
+            else:
+                pieces.append(lax.all_gather(hidden, "y", axis=0))
         result = pl.pallas_call(
-            down_kernel,
-            grid_spec=pltpu.PrefetchScalarGridSpec(
-                num_scalar_prefetch=1,
-                grid=(1,),
-                in_specs=[pl.BlockSpec((ff, cols), lambda step, pos: (0, 0))] * 2
-                + [pl.BlockSpec((NY, PIECE, units), lambda step, pos: (0, 0, 0))] * len(pieces),
-                out_specs=pl.BlockSpec((size, NC * cols), lambda step, pos: (0, 0)),
-            ),
+            down_ring_kernel if size > PIECE else down_kernel,
             out_shape=sds((size, NC * cols), BF16),
+            in_specs=[SMEM] + [VMEM] * (2 + len(pieces)),
+            out_specs=VMEM,
             compiler_params=params(24),
             cost_estimate=cost(
                 2 * size * ff * NC * cols, 2 * ff * NC * cols + 2 * size * NC * cols

time: 253 us -> 241 us (0.953)
  blocking collectives: 113 us -> 83.9 us
  waiting for transfers between devices: 6.48 us -> 18.1 us
  starting transfers between devices: 56.9 us -> 66.2 us
  Pallas kernels: 40.7 us -> 36.9 us
    all_gather x4 -> x2, blocking collectives: 59 us -> 29.2 us  [body(): pieces.append(lax.all_gather(hidden, 'y', axis=0))]
    ppermute x0 -> x8, waiting for transfers between devices: none -> 11.6 us  [turn(): return lax.ppermute(array, 'y', [(i, (i + step) % NY) for i in range(NY)])]
    ppermute x0 -> x8, starting transfers between devices: none -> 11.4 us  [turn(): return lax.ppermute(array, 'y', [(i, (i + step) % NY) for i in range(NY)])]
    pallas_call x7, Pallas kernels: 33.7 us -> 29.9 us  [the longest x4 20 us: body(): pl.pallas_call(functools.partial(hidden_kernel, half), out_shape=sds((PIE...]
  transfers between devices with their start and end apart: 12 -> 20, of which waited for: 3 -> 6; matrix products, arithmetic and copies ran while one was open for 2% -> 3% of each run, Pallas kernels for 15% -> 15%
where the time goes in v5:
time: 241 us; the launch traced here: 240 us
  blocking collectives  83.9 us (35%)
  starting transfers between devices  66.2 us (27%)
  Pallas kernels  36.9 us (15%)
  local copies, waits for them, and re-layouts  20.6 us (9%)
  waiting for transfers between devices  18.1 us (8%)
  between operations  13.4 us (6%)
    all_to_all x1, blocking collectives, body(): received.append(lax.all_to_all(rows, ('x', 'z'), 0, 0, tiled=True))  32.3 us
    all_gather x2, blocking collectives, body(): pieces.append(lax.all_gather(hidden, 'y', axis=0))  29.2 us
    all_to_all x1, blocking collectives, body(): returned.append(lax.all_to_all(result, ('x', 'z'), 0, 0, tiled=True))  22.4 us
    pallas_call x4, Pallas kernels, body(): pl.pallas_call(functools.partial(hidden_kernel, half), out_shape=sds((PIE...  20 us
    all_to_all x2, starting transfers between devices, body(): returned.append(lax.all_to_all(result, ('x', 'z'), 0, 0, tiled=True))  17.2 us
    ppermute x2, starting transfers between devices, body(): give = lax.ppermute(give, 'c', [(0, 1), (1, 0)])  14.5 us
    unnamed x36, local copies, waits for them, and re-layouts  13.9 us
    all_to_all x1, starting transfers between devices, body(): received = [lax.all_to_all(first_rows, ('x', 'z'), 0, 0, tiled=True)]  12 us
  transfers between devices with their start and end apart: 20, of which 6 were waited for; matrix products, arithmetic and copies ran while one was open for 3% of the time, Pallas kernels for 15%

profile of v5, /device:TPU:1, one launch (start us, length us, event | category | flops | bytes accessed | tf_op | source)
XLA Modules:
  0.0 239.9 jit_solution(3926196834251438816)
XLA Ops:
  11.2 12.0 %all-to-all-start = ((bf16[32,8,1024]{2,1,0:T(8,128)(2,1)}), bf16[32,8,1024]{2,1,0:T(8,128)(2,1)}, u32[]{:S(2)}, u32[]{:S(2)}) async-start(bf16[32,8,1024]{2,1,0:T(8,128)(2,1)} %bitcast.9), calls=%async_computation | async-start | bytes 1048576 | tf_op jit(solution)/shard_map/all_to_all | solution.py:214
  26.4 3.9 %dynamic-slice_bitcast_fusion = (bf16[1536,512]{1,0:T(8,128)(2,1)}, bf16[1536,512]{1,0:T(8,128)(2,1)}) fusion(bf16[2,1536,512]{2,1,0:T(8,128)(2,1)} %param.13, s32[]{:T(128)S(6)} %select_n.13, s32[]{:T(128)S(6)} %select_n.12), kind=kLoop, calls=%fused_computation | loop fusion | bytes 6291464 | tf_op jit(solution)/shard_map/jit(dynamic_index_in_dim)/squeeze | solution.py:225
  33.4 4.1 %all-to-all-done = bf16[32,8,1024]{2,1,0:T(8,128)(2,1)} async-done(((bf16[32,8,1024]{2,1,0:T(8,128)(2,1)}), bf16[32,8,1024]{2,1,0:T(8,128)(2,1)}, u32[]{:S(2)}, u32[]{:S(2)}) %all-to-all-start) | async-done | bytes 524320 | tf_op jit(solution)/shard_map/all_to_all | solution.py:214
  37.5 32.3 %all_to_all.70 = bf16[32,16,1024]{2,1,0:T(8,128)(2,1)} all-to-all(bf16[32,16,1024]{2,1,0:T(8,128)(2,1)} %bitcast.41), channel_id=1, replica_groups=mesh['y'=4,'c'=2,'x'=4,'z'=8] {'x','z'}, dimensions={0} | all-to-all | bytes 2097152 | tf_op jit(solution)/shard_map/all_to_all | solution.py:233
  71.2 3.9 %collective-permute-start.1 = (bf16[192,4096]{1,0:T(8,128)(2,1)}, bf16[192,4096]{1,0:T(8,128)(2,1)}, u32[]{:S(2)}, u32[]{:S(2)}) collective-permute-start(bf16[192,4096]{1,0:T(8,128)(2,1)} %get-tuple-element.54), channel_id=1, source_target_pairs={{0,32},{32,0},{1,33},{33,1},{2,34},{34,2},{3,35},{35,3},{4,36},{36... | collective-permute-start | bytes 4718600 | tf_op jit(solution)/shard_map/ppermute | solution.py:230
  75.6 6.6 %all-to-all-start.2 = ((bf16[32,8,1024]{2,1,0:T(8,128)(2,1)}), bf16[32,8,1024]{2,1,0:T(8,128)(2,1)}, u32[]{:S(2)}, u32[]{:S(2)}) async-start(bf16[32,8,1024]{2,1,0:T(8,128)(2,1)} %bitcast.43), calls=%async_computation.2 | async-start | bytes 1048576 | tf_op jit(solution)/shard_map/all_to_all | solution.py:233
  83.8 5.3 %shard_map.76 = bf16[256,384]{1,0:T(8,128)(2,1)S(1)} custom-call(s32[2]{0:T(128)S(1)} %pad_add_fusion.pos, bf16[4,256,1024]{2,1,0:T(8,128)(2,1)S(1)} %bitcast.40, bf16[192,4096]{1,0:T(8,128)(2,1)S(1)} %get-tuple-element.53.gate_own, bf16[192,4096]{1,0:T(8,128)(2,1)} %collective-permute-done.1.gate_other, bf16[192,4096]{1,0:T(8,128)(2,1)S(1)} %get-tuple-element.55.up_own, ...), custom_call_target="tpu_custom_call" | custom-call | flops 1610612736 | bytes 8388608 | tf_op jit(solution)/shard_map/pallas_call | solution.py:256
  89.1 17.0 %all-gather.2 = bf16[1024,384]{1,0:T(8,128)(2,1)S(1)} all-gather(bf16[256,384]{1,0:T(8,128)(2,1)S(1)} %shard_map.76), channel_id=4, replica_groups=mesh['y'=4,'c'=2,'x'=4,'z'=8] {'y'}, dimensions={0}, use_global_device_ids=true | all-gather | bytes 983040 | tf_op jit(solution)/shard_map/all_gather | solution.py:269
  109.6 22.4 %all_to_all.71 = bf16[32,8,1024]{2,1,0:T(8,128)(2,1)} all-to-all(bf16[32,8,1024]{2,1,0:T(8,128)(2,1)} %bitcast.36), channel_id=1, replica_groups=mesh['y'=4,'c'=2,'x'=4,'z'=8] {'x','z'}, dimensions={0} | all-to-all | bytes 1048576 | tf_op jit(solution)/shard_map/all_to_all | solution.py:283
  134.2 4.9 %shard_map.78.refs_0_ = bf16[256,384]{1,0:T(8,128)(2,1)S(1)} custom-call(s32[2]{0:T(128)S(1)} %pad_add_fusion.pos, bf16[4,512,1024]{2,1,0:T(8,128)(2,1)S(1)} %bitcast.32, bf16[192,4096]{1,0:T(8,128)(2,1)S(1)} %get-tuple-element.53.gate_own, bf16[192,4096]{1,0:T(8,128)(2,1)} %collective-permute-done.1.gate_other, ...), custom_call_target="tpu_custom_call" | custom-call | flops 1610612736 | bytes 8388608 | tf_op jit(solution)/shard_map/pallas_call | solution.py:256
  139.1 2.7 %collective-permute-start.4 = (bf16[256,384]{1,0:T(8,128)(2,1)S(1)}, bf16[256,384]{1,0:T(8,128)(2,1)S(1)}, u32[]{:S(2)}, u32[]{:S(2)}) collective-permute-start(bf16[256,384]{1,0:T(8,128)(2,1)S(1)} %shard_map.78.refs_0_), channel_id=1, source_target_pairs={{0,192},{64,0},{128,64},{192,128},{1,193},{65,1},{129,65},{193,129... | collective-permute-start | bytes 589832 | tf_op jit(solution)/shard_map/ppermute | solution.py:184
  141.8 4.9 %shard_map.79.refs_5_ = bf16[256,384]{1,0:T(8,128)(2,1)S(1)} custom-call(s32[2]{0:T(128)S(1)} %pad_add_fusion.pos, bf16[4,512,1024]{2,1,0:T(8,128)(2,1)S(1)} %bitcast.33, bf16[192,4096]{1,0:T(8,128)(2,1)S(1)} %get-tuple-element.53.gate_own, bf16[192,4096]{1,0:T(8,128)(2,1)} %collective-permute-done.1.gate_other, ...), custom_call_target="tpu_custom_call" | custom-call | flops 1610612736 | bytes 8388608 | tf_op jit(solution)/shard_map/pallas_call | solution.py:256
  149.6 2.7 %collective-permute-start.6 = (bf16[128,384]{1,0:T(8,128)(2,1)S(1)}, bf16[128,384]{1,0:T(8,128)(2,1)S(1)}, u32[]{:S(2)}, u32[]{:S(2)}) collective-permute-start(bf16[128,384]{1,0:T(8,128)(2,1)S(1)} %slice.17), channel_id=1, source_target_pairs={{0,192},{64,0},{128,64},{192,128},{1,193},{65,1},{129,65},{193,129... | collective-permute-start | bytes 294920 | tf_op jit(solution)/shard_map/ppermute | solution.py:184
  152.3 6.3 %collective-permute-done.7.refs_6_ = bf16[256,384]{1,0:T(8,128)(2,1)S(1)} collective-permute-done((bf16[256,384]{1,0:T(8,128)(2,1)S(1)}, bf16[256,384]{1,0:T(8,128)(2,1)S(1)}, u32[]{:S(2)}, u32[]{:S(2)}) %collective-permute-start.7) | collective-permute-done | bytes 196640 | tf_op jit(solution)/shard_map/ppermute | solution.py:184
  158.7 3.0 %collective-permute-start.10 = (bf16[128,384]{1,0:T(8,128)(2,1)S(1)}, bf16[128,384]{1,0:T(8,128)(2,1)S(1)}, u32[]{:S(2)}, u32[]{:S(2)}) collective-permute-start(bf16[128,384]{1,0:T(8,128)(2,1)S(1)} %slice.19), channel_id=1, source_target_pairs={{0,192},{64,0},{128,64},{192,128},{1,193},{65,1},{129,65},{193,129... | collective-permute-start | bytes 294920 | tf_op jit(solution)/shard_map/ppermute | solution.py:184
  162.8 4.2 %collective-permute-done.9.refs_8_ = bf16[128,384]{1,0:T(8,128)(2,1)S(1)} collective-permute-done((bf16[128,384]{1,0:T(8,128)(2,1)S(1)}, bf16[128,384]{1,0:T(8,128)(2,1)S(1)}, u32[]{:S(2)}, u32[]{:S(2)}) %collective-permute-start.9) | collective-permute-done | bytes 98336 | tf_op jit(solution)/shard_map/ppermute | solution.py:184
  167.0 3.7 %shard_map.80 = bf16[512,1024]{1,0:T(8,128)(2,1)S(1)} custom-call(s32[2]{0:T(128)S(1)} %pad_add_fusion.pos, bf16[1536,512]{1,0:T(8,128)(2,1)S(1)} %copy-done.2, bf16[1536,512]{1,0:T(8,128)(2,1)} %collective-permute-done.down_other, bf16[256,384]{1,0:T(8,128)(2,1)S(1)} %shard_map.78.refs_0_, bf16[256,384]{1,0:T(8,128)(2,1)S(1)} %collective-permute-done.3.refs_1_, ...), custom_call_target="tpu_custom_call" | custom-call | flops 1610612736 | bytes 4194304 | tf_op jit(solution)/shard_map/pallas_call | solution.py:270
  171.8 8.0 %all-to-all-start.4 = ((bf16[32,16,1024]{2,1,0:T(8,128)(2,1)}), bf16[32,16,1024]{2,1,0:T(8,128)(2,1)}, u32[]{:S(2)}, u32[]{:S(2)}) async-start(bf16[32,16,1024]{2,1,0:T(8,128)(2,1)} %bitcast.42), calls=%async_computation.4 | async-start | bytes 2097152 | tf_op jit(solution)/shard_map/all_to_all | solution.py:283
  181.4 5.0 %shard_map.82 = bf16[256,384]{1,0:T(8,128)(2,1)S(1)} custom-call(s32[2]{0:T(128)S(1)} %pad_add_fusion.pos, bf16[4,256,1024]{2,1,0:T(8,128)(2,1)S(1)} %bitcast.39, bf16[192,4096]{1,0:T(8,128)(2,1)S(1)} %get-tuple-element.53.gate_own, bf16[192,4096]{1,0:T(8,128)(2,1)} %collective-permute-done.1.gate_other, bf16[192,4096]{1,0:T(8,128)(2,1)S(1)} %get-tuple-element.55.up_own, ...), custom_call_target="tpu_custom_call" | custom-call | flops 1610612736 | bytes 8388608 | tf_op jit(solution)/shard_map/pallas_call | solution.py:256
  186.3 12.2 %all-gather.4 = bf16[1024,384]{1,0:T(8,128)(2,1)S(1)} all-gather(bf16[256,384]{1,0:T(8,128)(2,1)S(1)} %shard_map.82), channel_id=6, replica_groups=mesh['y'=4,'c'=2,'x'=4,'z'=8] {'y'}, dimensions={0}, use_global_device_ids=true | all-gather | bytes 983040 | tf_op jit(solution)/shard_map/all_gather | solution.py:269
  198.5 3.5 %shard_map.83 = bf16[256,1024]{1,0:T(8,128)(2,1)} custom-call(s32[2]{0:T(128)S(1)} %pad_add_fusion.pos, bf16[1536,512]{1,0:T(8,128)(2,1)S(1)} %copy-done.3, bf16[1536,512]{1,0:T(8,128)(2,1)} %collective-permute-done.down_other, bf16[4,256,384]{2,1,0:T(8,128)(2,1)S(1)} %bitcast.35), custom_call_target="tpu_custom_call" | custom-call | flops 805306368 | bytes 3670016 | tf_op jit(solution)/shard_map/pallas_call | solution.py:270
  202.1 9.3 %all-to-all-start.5 = ((bf16[32,8,1024]{2,1,0:T(8,128)(2,1)}), bf16[32,8,1024]{2,1,0:T(8,128)(2,1)S(1)}, u32[]{:S(2)}, u32[]{:S(2)}) async-start(bf16[32,8,1024]{2,1,0:T(8,128)(2,1)} %bitcast.24), calls=%async_computation.5 | async-start | bytes 1048576 | tf_op jit(solution)/shard_map/all_to_all | solution.py:283
  216.4 6.7 %collective-permute-start.11 = (bf16[128,512]{1,0:T(8,128)(2,1)S(1)}, bf16[128,512]{1,0:T(8,128)(2,1)S(1)}, u32[]{:S(2)}, u32[]{:S(2)}) collective-permute-start(bf16[128,512]{1,0:T(8,128)(2,1)S(1)} %get-tuple-element.63), channel_id=1, source_target_pairs={{0,32},{32,0},{1,33},{33,1},{2,34},{34,2},{3,35},{35,3},{4,36},{36... | collective-permute-start | bytes 393224 | tf_op jit(solution)/shard_map/ppermute | solution.py:296
  223.9 7.8 %collective-permute-start.12 = (bf16[128,512]{1,0:T(8,128)(2,1)S(1)}, bf16[128,512]{1,0:T(8,128)(2,1)S(1)}, u32[]{:S(2)}, u32[]{:S(2)}) collective-permute-start(bf16[128,512]{1,0:T(8,128)(2,1)S(1)} %get-tuple-element.68), channel_id=1, source_target_pairs={{0,32},{32,0},{1,33},{33,1},{2,34},{34,2},{3,35},{35,3},{4,36},{36... | collective-permute-start | bytes 393224 | tf_op jit(solution)/shard_map/ppermute | solution.py:296
  (80 shorter events, 34.3 us)
Async XLA Ops:
  11.2 26.3 %all-to-all-start = ((bf16[32,8,1024]{2,1,0:T(8,128)(2,1)}), bf16[32,8,1024]{2,1,0:T(8,128)(2,1)}, u32[]{:S(2)}, u32[]{:S(2)}) async-start(bf16[32,8,1024]{2,1,0:T(8,128)(2,1)} %bitcast.9), calls=%async_computation | async-start | bytes 1048576 | tf_op jit(solution)/shard_map/all_to_all | solution.py:214
  23.2 48.0 %all-gather.9.cloned.1.call-start = ((), (), s32[]{:S(2)}) async-start(), calls=%async_computation.6 | async-start | bytes 2621440 | tf_op jit(solution)/shard_map/all_gather | solution.py:251
  37.5 94.5 %all-gather.11.cloned.1.call-start = ((), (), s32[]{:S(2)}) async-start(), calls=%async_computation.7 | async-start | bytes 5242880 | tf_op jit(solution)/shard_map/all_gather | solution.py:251
  71.2 11.0 %collective-permute-start.1 = (bf16[192,4096]{1,0:T(8,128)(2,1)}, bf16[192,4096]{1,0:T(8,128)(2,1)}, u32[]{:S(2)}, u32[]{:S(2)}) collective-permute-start(bf16[192,4096]{1,0:T(8,128)(2,1)} %get-tuple-element.54), channel_id=1, source_target_pairs={{0,32},{32,0},{1,33},{33,1},{2,34},{34,2},{3,35},{35,3},{4,36},{36... | collective-permute-start | bytes 4718600 | tf_op jit(solution)/shard_map/ppermute | solution.py:230
  75.0 7.2 %collective-permute-start.2 = (bf16[192,4096]{1,0:T(8,128)(2,1)}, bf16[192,4096]{1,0:T(8,128)(2,1)}, u32[]{:S(2)}, u32[]{:S(2)}) collective-permute-start(bf16[192,4096]{1,0:T(8,128)(2,1)} %get-tuple-element.56), channel_id=1, source_target_pairs={{0,32},{32,0},{1,33},{33,1},{2,34},{34,2},{3,35},{35,3},{4,36},{36... | collective-permute-start | bytes 4718600 | tf_op jit(solution)/shard_map/ppermute | solution.py:230
  75.1 31.0 %collective-permute-start = (bf16[1536,512]{1,0:T(8,128)(2,1)}, bf16[1536,512]{1,0:T(8,128)(2,1)}, u32[]{:S(2)}, u32[]{:S(2)}) collective-permute-start(bf16[1536,512]{1,0:T(8,128)(2,1)} %get-tuple-element.52), channel_id=1, source_target_pairs={{0,32},{32,0},{1,33},{33,1},{2,34},{34,2},{3,35},{35,3},{4,36},{36... | collective-permute-start | bytes 4718600 | tf_op jit(solution)/shard_map/ppermute | solution.py:230
  75.6 34.0 %all-to-all-start.2 = ((bf16[32,8,1024]{2,1,0:T(8,128)(2,1)}), bf16[32,8,1024]{2,1,0:T(8,128)(2,1)}, u32[]{:S(2)}, u32[]{:S(2)}) async-start(bf16[32,8,1024]{2,1,0:T(8,128)(2,1)} %bitcast.43), calls=%async_computation.2 | async-start | bytes 1048576 | tf_op jit(solution)/shard_map/all_to_all | solution.py:233
  82.2 97.6 %all-gather.13.cloned.1.call-start = ((), (), s32[]{:S(2)}) async-start(), calls=%async_computation.8 | async-start | bytes 2621440 | tf_op jit(solution)/shard_map/all_gather | solution.py:251
  83.8 22.3 %copy-start.1 = (bf16[1536,512]{1,0:T(8,128)(2,1)S(1)}, bf16[1536,512]{1,0:T(8,128)(2,1)}, u32[]{:S(2)}) copy-start(bf16[1536,512]{1,0:T(8,128)(2,1)} %get-tuple-element.51.down_own) | copy-start | bytes 4718596
  139.0 28.0 %copy-start.2 = (bf16[1536,512]{1,0:T(8,128)(2,1)S(1)}, bf16[1536,512]{1,0:T(8,128)(2,1)}, u32[]{:S(2)}) copy-start(bf16[1536,512]{1,0:T(8,128)(2,1)} %get-tuple-element.51.down_own) | copy-start | bytes 4718596
  139.0 10.4 %collective-permute-start.3 = (bf16[256,384]{1,0:T(8,128)(2,1)S(1)}, bf16[256,384]{1,0:T(8,128)(2,1)S(1)}, u32[]{:S(2)}, u32[]{:S(2)}) collective-permute-start(bf16[256,384]{1,0:T(8,128)(2,1)S(1)} %shard_map.78.refs_0_), channel_id=1, source_target_pairs={{0,64},{64,128},{128,192},{192,0},{1,65},{65,129},{129,193},{193,1... | collective-permute-start | bytes 589832 | tf_op jit(solution)/shard_map/ppermute | solution.py:184
  139.1 10.4 %collective-permute-start.4 = (bf16[256,384]{1,0:T(8,128)(2,1)S(1)}, bf16[256,384]{1,0:T(8,128)(2,1)S(1)}, u32[]{:S(2)}, u32[]{:S(2)}) collective-permute-start(bf16[256,384]{1,0:T(8,128)(2,1)S(1)} %shard_map.78.refs_0_), channel_id=1, source_target_pairs={{0,192},{64,0},{128,64},{192,128},{1,193},{65,1},{129,65},{193,129... | collective-permute-start | bytes 589832 | tf_op jit(solution)/shard_map/ppermute | solution.py:184
  146.7 11.9 %collective-permute-start.7 = (bf16[256,384]{1,0:T(8,128)(2,1)S(1)}, bf16[256,384]{1,0:T(8,128)(2,1)S(1)}, u32[]{:S(2)}, u32[]{:S(2)}) collective-permute-start(bf16[256,384]{1,0:T(8,128)(2,1)S(1)} %shard_map.79.refs_5_), channel_id=1, source_target_pairs={{0,64},{64,128},{128,192},{192,0},{1,65},{65,129},{129,193},{193,1... | collective-permute-start | bytes 589832 | tf_op jit(solution)/shard_map/ppermute | solution.py:184
  146.7 12.0 %collective-permute-start.8 = (bf16[256,384]{1,0:T(8,128)(2,1)S(1)}, bf16[256,384]{1,0:T(8,128)(2,1)S(1)}, u32[]{:S(2)}, u32[]{:S(2)}) collective-permute-start(bf16[256,384]{1,0:T(8,128)(2,1)S(1)} %shard_map.79.refs_5_), channel_id=1, source_target_pairs={{0,192},{64,0},{128,64},{192,128},{1,193},{65,1},{129,65},{193,129... | collective-permute-start | bytes 589832 | tf_op jit(solution)/shard_map/ppermute | solution.py:184
  149.4 13.4 %collective-permute-start.5 = (bf16[128,384]{1,0:T(8,128)(2,1)S(1)}, bf16[128,384]{1,0:T(8,128)(2,1)S(1)}, u32[]{:S(2)}, u32[]{:S(2)}) collective-permute-start(bf16[128,384]{1,0:T(8,128)(2,1)S(1)} %slice.16), channel_id=1, source_target_pairs={{0,64},{64,128},{128,192},{192,0},{1,65},{65,129},{129,193},{193,1... | collective-permute-start | bytes 294920 | tf_op jit(solution)/shard_map/ppermute | solution.py:184
  149.6 13.3 %collective-permute-start.6 = (bf16[128,384]{1,0:T(8,128)(2,1)S(1)}, bf16[128,384]{1,0:T(8,128)(2,1)S(1)}, u32[]{:S(2)}, u32[]{:S(2)}) collective-permute-start(bf16[128,384]{1,0:T(8,128)(2,1)S(1)} %slice.17), channel_id=1, source_target_pairs={{0,192},{64,0},{128,64},{192,128},{1,193},{65,1},{129,65},{193,129... | collective-permute-start | bytes 294920 | tf_op jit(solution)/shard_map/ppermute | solution.py:184
  158.6 8.4 %collective-permute-start.9 = (bf16[128,384]{1,0:T(8,128)(2,1)S(1)}, bf16[128,384]{1,0:T(8,128)(2,1)S(1)}, u32[]{:S(2)}, u32[]{:S(2)}) collective-permute-start(bf16[128,384]{1,0:T(8,128)(2,1)S(1)} %slice.18), channel_id=1, source_target_pairs={{0,64},{64,128},{128,192},{192,0},{1,65},{65,129},{129,193},{193,1... | collective-permute-start | bytes 294920 | tf_op jit(solution)/shard_map/ppermute | solution.py:184
  158.7 8.3 %collective-permute-start.10 = (bf16[128,384]{1,0:T(8,128)(2,1)S(1)}, bf16[128,384]{1,0:T(8,128)(2,1)S(1)}, u32[]{:S(2)}, u32[]{:S(2)}) collective-permute-start(bf16[128,384]{1,0:T(8,128)(2,1)S(1)} %slice.19), channel_id=1, source_target_pairs={{0,192},{64,0},{128,64},{192,128},{1,193},{65,1},{129,65},{193,129... | collective-permute-start | bytes 294920 | tf_op jit(solution)/shard_map/ppermute | solution.py:184
  171.8 30.3 %all-to-all-start.4 = ((bf16[32,16,1024]{2,1,0:T(8,128)(2,1)}), bf16[32,16,1024]{2,1,0:T(8,128)(2,1)}, u32[]{:S(2)}, u32[]{:S(2)}) async-start(bf16[32,16,1024]{2,1,0:T(8,128)(2,1)} %bitcast.42), calls=%async_computation.4 | async-start | bytes 2097152 | tf_op jit(solution)/shard_map/all_to_all | solution.py:283
  181.4 17.2 %copy-start.3 = (bf16[1536,512]{1,0:T(8,128)(2,1)S(1)}, bf16[1536,512]{1,0:T(8,128)(2,1)}, u32[]{:S(2)}) copy-start(bf16[1536,512]{1,0:T(8,128)(2,1)} %get-tuple-element.51.down_own) | copy-start | bytes 4718596
  198.5 12.8 %copy-start.15 = (s32[128,8]{0,1:T(8,128)S(1)}, s32[128,8]{0,1:T(8,128)}, u32[]{:S(2)}) copy-start(s32[128,8]{0,1:T(8,128)} %param.10) | copy-start | bytes 12292
  202.1 21.1 %all-to-all-start.5 = ((bf16[32,8,1024]{2,1,0:T(8,128)(2,1)}), bf16[32,8,1024]{2,1,0:T(8,128)(2,1)S(1)}, u32[]{:S(2)}, u32[]{:S(2)}) async-start(bf16[32,8,1024]{2,1,0:T(8,128)(2,1)} %bitcast.24), calls=%async_computation.5 | async-start | bytes 1048576 | tf_op jit(solution)/shard_map/all_to_all | solution.py:283
  216.4 15.3 %collective-permute-start.11 = (bf16[128,512]{1,0:T(8,128)(2,1)S(1)}, bf16[128,512]{1,0:T(8,128)(2,1)S(1)}, u32[]{:S(2)}, u32[]{:S(2)}) collective-permute-start(bf16[128,512]{1,0:T(8,128)(2,1)S(1)} %get-tuple-element.63), channel_id=1, source_target_pairs={{0,32},{32,0},{1,33},{33,1},{2,34},{34,2},{3,35},{35,3},{4,36},{36... | collective-permute-start | bytes 393224 | tf_op jit(solution)/shard_map/ppermute | solution.py:296
  223.9 8.8 %collective-permute-start.12 = (bf16[128,512]{1,0:T(8,128)(2,1)S(1)}, bf16[128,512]{1,0:T(8,128)(2,1)S(1)}, u32[]{:S(2)}, u32[]{:S(2)}) collective-permute-start(bf16[128,512]{1,0:T(8,128)(2,1)S(1)} %get-tuple-element.68), channel_id=1, source_target_pairs={{0,32},{32,0},{1,33},{33,1},{2,34},{34,2},{3,35},{35,3},{4,36},{36... | collective-permute-start | bytes 393224 | tf_op jit(solution)/shard_map/ppermute | solution.py:296
  (14 other events, 31.1 us)
Sparse Core Ops, SparseCore 0:
  37.6 33.5 all-gather.8
  73.0 57.1 all-gather.10
  132.1 43.9 all-gather.12

commit v6 on v5

--- a/solution.py
+++ b/solution.py
@@ -114,22 +114,47 @@
         out[...] = jnp.transpose(spread(place, dense, first, size)).astype(BF16)
 
 
+def activate(pos, sums):
+    units = sums.shape[0] // 4
+    gate_own, up_own, gate_other, up_other = [
+        sums[index * units : (index + 1) * units] for index in range(4)
+    ]
+    own = gate_own / (1.0 + jnp.exp(-gate_own)) * up_own
+    other = gate_other / (1.0 + jnp.exp(-gate_other)) * up_other
+    low = jnp.where(pos[1] == 0, own, other)
+    high = jnp.where(pos[1] == 0, other, own)
+    return jnp.transpose(jnp.concatenate([low, high], axis=0)).astype(BF16)
+
+
 def hidden_kernel(half, pos, blocks, gate_own, gate_other, up_own, up_other, out):
     quarter = blocks.shape[2]
     rows = slice(half * PIECE, (half + 1) * PIECE)
-    sums = [None] * 4
+    total = None
     for y in range(NY):
-        block = blocks[y, rows, :]
         cols = slice(y * quarter, (y + 1) * quarter)
-        for which, weight in enumerate((gate_own, up_own, gate_other, up_other)):
-            term = by_rows(weight[:, cols], block)
-            sums[which] = term if y == 0 else sums[which] + term
-    own, other = [
-        gate / (1.0 + jnp.exp(-gate)) * up for gate, up in (sums[0:2], sums[2:4])
-    ]
-    low = jnp.where(pos[1] == 0, own, other)
-    high = jnp.where(pos[1] == 0, other, own)
-    out[...] = jnp.transpose(jnp.concatenate([low, high], axis=0)).astype(BF16)
+        weights = jnp.concatenate(
+            [weight[:, cols] for weight in (gate_own, up_own, gate_other, up_other)], axis=0
+        )
+        term = by_rows(weights, blocks[y, rows, :])
+        total = term if y == 0 else total + term
+    out[...] = activate(pos, total)
+
+
+def hidden_ring_kernel(
+    pos, own, low, high, far_top, far_bottom, gate_own, gate_other, up_own, up_other, out
+):
+    quarter = own.shape[1]
+    far = jnp.concatenate([far_top[...], far_bottom[...]], axis=0)
+    total = None
+    for block, step in ((own[...], 0), (low[...], 3), (high[...], 1), (far, 2)):
+        at = lax.rem(pos[0] + step, NY)
+        cols = pl.ds(pl.multiple_of(at * quarter, quarter), quarter)
+        weights = jnp.concatenate(
+            [weight[:, cols] for weight in (gate_own, up_own, gate_other, up_other)], axis=0
+        )
+        term = by_rows(weights, block)
+        total = term if total is None else total + term
+    out[...] = activate(pos, total)
 
 
 def store_columns(pos, out, at, own, other):
@@ -245,24 +270,30 @@
     done = []
     for index, size in enumerate(sizes):
         mine = received[index]
-        if index:
-            before = [done[i][j] for i, j in ((index - 1, 0), (index - 2, 1)) if i >= 0]
-            mine, *before = lax.optimization_barrier((mine, *before))
-        blocks = lax.all_gather(mine, "y", axis=0)
-        if index == 1:
-            blocks, returned[0] = lax.optimization_barrier((blocks, returned[0]))
+        if index == 0:
+            inputs = ring(mine)
+        else:
+            if index == 2:
+                mine, *_ = lax.optimization_barrier((mine, *done))
+            blocks = lax.all_gather(mine, "y", axis=0)
+            if index == 1:
+                blocks, returned[0] = lax.optimization_barrier((blocks, returned[0]))
+                done.append(blocks)
+            inputs = (blocks,)
         pieces = []
         for half in range(size // PIECE):
             hidden = pl.pallas_call(
-                functools.partial(hidden_kernel, half),
+                functools.partial(hidden_kernel, half) if index else hidden_ring_kernel,
                 out_shape=sds((PIECE, units), BF16),
-                in_specs=[SMEM] + [VMEM] * 5,
+                in_specs=[SMEM] + [VMEM] * (4 + len(inputs)),
                 out_specs=VMEM,
                 compiler_params=params(24),
                 cost_estimate=cost(
                     4 * PIECE * width * units, 4 * units * width + 2 * PIECE * width
                 ),
-            )(pos, blocks, own[0], others[0], own[1], others[1])
+            )(pos, *inputs, own[0], others[0], own[1], others[1])
+            if index == 0:
+                received[1], hidden = lax.optimization_barrier((received[1], hidden))
             if size > PIECE:
                 pieces.extend(ring(hidden))
             else:
@@ -279,7 +310,7 @@
         )(pos, own[2], others[2], *pieces)
         if index == 0:
             result, received[-1] = lax.optimization_barrier((result, received[-1]))
-        done.append((blocks, result))
+            done.append(result)
         returned.append(lax.all_to_all(result, ("x", "z"), 0, 0, tiled=True))
 
     total = None

time: 241 us -> 242 us (level)
  blocking collectives: 83.9 us -> 49.4 us
  waiting for transfers between devices: 18.1 us -> 40.9 us
  starting transfers between devices: 66.2 us -> 80.4 us
  Pallas kernels: 36.9 us -> 27.2 us
  local copies, waits for them, and re-layouts: 20.6 us -> 28.5 us
    all_to_all x1 -> x0, blocking collectives: 32.3 us -> none  [body(): received.append(lax.all_to_all(rows, ('x', 'z'), 0, 0, tiled=True))]
    ppermute x8 -> x12, waiting for transfers between devices: 11.6 us -> 32.5 us  [turn(): return lax.ppermute(array, 'y', [(i, (i + step) % NY) for i in range(NY)])]
    all_to_all x1 -> x2, starting transfers between devices: 6.59 us -> 17.2 us  [body(): received.append(lax.all_to_all(rows, ('x', 'z'), 0, 0, tiled=True))]
    pallas_call x4, Pallas kernels: 20 us -> 10.3 us  [body(): pl.pallas_call(functools.partial(hidden_kernel, half) if index else hidde...]
    unnamed x36 -> x46, local copies, waits for them, and re-layouts: 13.9 us -> 21.7 us
    ppermute x8 -> x12, starting transfers between devices: 11.4 us -> 15.7 us  [turn(): return lax.ppermute(array, 'y', [(i, (i + step) % NY) for i in range(NY)])]
  transfers between devices with their start and end apart: 20 -> 24, of which waited for: 6 -> 11; matrix products, arithmetic and copies ran while one was open for 3% -> 3% of each run, Pallas kernels for 15% -> 10%
where the time goes in v6:
time: 242 us; the launch traced here: 241 us
  starting transfers between devices  80.4 us (33%)
  blocking collectives  49.4 us (20%)
  waiting for transfers between devices  40.9 us (17%)
  local copies, waits for them, and re-layouts  28.5 us (12%)
  Pallas kernels  27.2 us (11%)
  between operations  13.7 us (6%)
    ppermute x12, waiting for transfers between devices, turn(): return lax.ppermute(array, 'y', [(i, (i + step) % NY) for i in range(NY)])  32.5 us
    all_gather x2, blocking collectives, body(): pieces.append(lax.all_gather(hidden, 'y', axis=0))  27.8 us
    unnamed x46, local copies, waits for them, and re-layouts  21.7 us
    all_to_all x1, blocking collectives, body(): returned.append(lax.all_to_all(result, ('x', 'z'), 0, 0, tiled=True))  21.6 us
    all_to_all x2, starting transfers between devices, body(): received.append(lax.all_to_all(rows, ('x', 'z'), 0, 0, tiled=True))  17.2 us
    all_to_all x2, starting transfers between devices, body(): returned.append(lax.all_to_all(result, ('x', 'z'), 0, 0, tiled=True))  16.4 us
    ppermute x12, starting transfers between devices, turn(): return lax.ppermute(array, 'y', [(i, (i + step) % NY) for i in range(NY)])  15.7 us
    ppermute x2, starting transfers between devices, body(): give = lax.ppermute(give, 'c', [(0, 1), (1, 0)])  14.8 us
  transfers between devices with their start and end apart: 24, of which 11 were waited for; matrix products, arithmetic and copies ran while one was open for 3% of the time, Pallas kernels for 10%

profile of v6, /device:TPU:1, one launch (start us, length us, event | category | flops | bytes accessed | tf_op | source)
XLA Modules:
  0.0 241.0 jit_solution(18192879047757165148)
XLA Ops:
  11.2 12.0 %all-to-all-start = ((bf16[32,8,1024]{2,1,0:T(8,128)(2,1)}), bf16[32,8,1024]{2,1,0:T(8,128)(2,1)}, u32[]{:S(2)}, u32[]{:S(2)}) async-start(bf16[32,8,1024]{2,1,0:T(8,128)(2,1)} %bitcast.9), calls=%async_computation | async-start | bytes 1048576 | tf_op jit(solution)/shard_map/all_to_all | solution.py:239
  26.3 4.0 %dynamic-slice_bitcast_fusion = (bf16[1536,512]{1,0:T(8,128)(2,1)}, bf16[1536,512]{1,0:T(8,128)(2,1)}) fusion(bf16[2,1536,512]{2,1,0:T(8,128)(2,1)} %param.13, s32[]{:T(128)S(6)} %select_n.13, s32[]{:T(128)S(6)} %select_n.12), kind=kLoop, calls=%fused_computation | loop fusion | bytes 6291464 | tf_op jit(solution)/shard_map/jit(dynamic_index_in_dim)/squeeze | solution.py:250
  33.3 4.2 %all-to-all-done = bf16[32,8,1024]{2,1,0:T(8,128)(2,1)} async-done(((bf16[32,8,1024]{2,1,0:T(8,128)(2,1)}), bf16[32,8,1024]{2,1,0:T(8,128)(2,1)}, u32[]{:S(2)}, u32[]{:S(2)}) %all-to-all-start) | async-done | bytes 524320 | tf_op jit(solution)/shard_map/all_to_all | solution.py:239
  37.5 7.6 %all-to-all-start.1 = ((bf16[32,16,1024]{2,1,0:T(8,128)(2,1)}), bf16[32,16,1024]{2,1,0:T(8,128)(2,1)}, u32[]{:S(2)}, u32[]{:S(2)}) async-start(bf16[32,16,1024]{2,1,0:T(8,128)(2,1)} %bitcast.39), calls=%async_computation.1 | async-start | bytes 2097152 | tf_op jit(solution)/shard_map/all_to_all | solution.py:258
  49.7 11.2 %collective-permute-done.1.high = bf16[256,1024]{1,0:T(8,128)(2,1)S(1)} collective-permute-done((bf16[256,1024]{1,0:T(8,128)(2,1)}, bf16[256,1024]{1,0:T(8,128)(2,1)S(1)}, u32[]{:S(2)}, u32[]{:S(2)}) %collective-permute-start.1) | collective-permute-done | bytes 524320 | tf_op jit(solution)/shard_map/ppermute | solution.py:209
  60.9 3.5 %collective-permute-start.3 = (bf16[128,1024]{1,0:T(8,128)(2,1)S(1)}, bf16[128,1024]{1,0:T(8,128)(2,1)S(1)}, u32[]{:S(2)}, u32[]{:S(2)}) collective-permute-start(bf16[128,1024]{1,0:T(8,128)(2,1)S(1)} %slice.25), channel_id=1, source_target_pairs={{0,192},{64,0},{128,64},{192,128},{1,193},{65,1},{129,65},{193,129... | collective-permute-start | bytes 786440 | tf_op jit(solution)/shard_map/ppermute | solution.py:209
  64.5 4.3 %collective-permute-done.3.far_bottom = bf16[128,1024]{1,0:T(8,128)(2,1)S(1)} collective-permute-done((bf16[128,1024]{1,0:T(8,128)(2,1)S(1)}, bf16[128,1024]{1,0:T(8,128)(2,1)S(1)}, u32[]{:S(2)}, u32[]{:S(2)}) %collective-permute-start.3) | collective-permute-done | bytes 262176 | tf_op jit(solution)/shard_map/ppermute | solution.py:209
  68.9 3.2 %collective-permute-done.2.far_top = bf16[128,1024]{1,0:T(8,128)(2,1)S(1)} collective-permute-done((bf16[128,1024]{1,0:T(8,128)(2,1)S(1)}, bf16[128,1024]{1,0:T(8,128)(2,1)S(1)}, u32[]{:S(2)}, u32[]{:S(2)}) %collective-permute-start.2) | collective-permute-done | bytes 262176 | tf_op jit(solution)/shard_map/ppermute | solution.py:209
  72.1 3.0 %shard_map.76 = bf16[256,384]{1,0:T(8,128)(2,1)S(1)} custom-call(s32[2]{0:T(128)S(1)} %pad_add_fusion.pos, bf16[256,1024]{1,0:T(8,128)(2,1)} %bitcast.10.own, bf16[256,1024]{1,0:T(8,128)(2,1)S(1)} %collective-permute-done.low, bf16[256,1024]{1,0:T(8,128)(2,1)S(1)} %collective-permute-done.1.high, bf16[128,1024]{1,0:T(8,128)(2,1)S(1)} %collective-permute-done.2.far_top, ...), custom_call_target="tpu_custom_call" | custom-call | flops 1610612736 | bytes 8388608 | tf_op jit(solution)/shard_map/pallas_call | solution.py:285
  79.9 9.6 %all-to-all-start.2 = ((bf16[32,8,1024]{2,1,0:T(8,128)(2,1)}), bf16[32,8,1024]{2,1,0:T(8,128)(2,1)}, u32[]{:S(2)}, u32[]{:S(2)}) async-start(bf16[32,8,1024]{2,1,0:T(8,128)(2,1)} %bitcast.41), calls=%async_computation.2 | async-start | bytes 1048576 | tf_op jit(solution)/shard_map/all_to_all | solution.py:258
  89.5 15.2 %all-gather.1 = bf16[1024,384]{1,0:T(8,128)(2,1)S(1)} all-gather(bf16[256,384]{1,0:T(8,128)(2,1)S(1)} %shard_map.76), channel_id=3, replica_groups=mesh['y'=4,'c'=2,'x'=4,'z'=8] {'y'}, dimensions={0}, use_global_device_ids=true | all-gather | bytes 983040 | tf_op jit(solution)/shard_map/all_gather | solution.py:300
  109.7 21.6 %all_to_all.70 = bf16[32,8,1024]{2,1,0:T(8,128)(2,1)} all-to-all(bf16[32,8,1024]{2,1,0:T(8,128)(2,1)} %bitcast.35), channel_id=1, replica_groups=mesh['y'=4,'c'=2,'x'=4,'z'=8] {'x','z'}, dimensions={0} | all-to-all | bytes 1048576 | tf_op jit(solution)/shard_map/all_to_all | solution.py:314
  131.3 3.2 %all-gather.7.cloned.1.call-done = bf16[2048,1024]{1,0:T(8,128)(2,1)} async-done(((bf16[512,1024]{1,0:T(8,128)(2,1)}), bf16[2048,1024]{1,0:T(8,128)(2,1)}) %all-gather.7.cloned.1.call-update) | async-done | bytes 4194320 | tf_op jit(solution)/shard_map/all_gather | solution.py:278
  150.2 4.9 %collective-permute-done.12.refs_7_ = bf16[256,384]{1,0:T(8,128)(2,1)S(1)} collective-permute-done((bf16[256,384]{1,0:T(8,128)(2,1)S(1)}, bf16[256,384]{1,0:T(8,128)(2,1)S(1)}, u32[]{:S(2)}, u32[]{:S(2)}) %collective-permute-start.12) | collective-permute-done | bytes 196640 | tf_op jit(solution)/shard_map/ppermute | solution.py:209
  155.1 3.6 %collective-permute-start.14 = (bf16[128,384]{1,0:T(8,128)(2,1)S(1)}, bf16[128,384]{1,0:T(8,128)(2,1)S(1)}, u32[]{:S(2)}, u32[]{:S(2)}) collective-permute-start(bf16[128,384]{1,0:T(8,128)(2,1)S(1)} %slice.29), channel_id=1, source_target_pairs={{0,192},{64,0},{128,64},{192,128},{1,193},{65,1},{129,65},{193,129... | collective-permute-start | bytes 294920 | tf_op jit(solution)/shard_map/ppermute | solution.py:209
  159.3 4.1 %collective-permute-done.9.refs_3_ = bf16[128,384]{1,0:T(8,128)(2,1)S(1)} collective-permute-done((bf16[128,384]{1,0:T(8,128)(2,1)S(1)}, bf16[128,384]{1,0:T(8,128)(2,1)S(1)}, u32[]{:S(2)}, u32[]{:S(2)}) %collective-permute-start.9) | collective-permute-done | bytes 98336 | tf_op jit(solution)/shard_map/ppermute | solution.py:209
  163.5 4.1 %collective-permute-done.13.refs_8_ = bf16[128,384]{1,0:T(8,128)(2,1)S(1)} collective-permute-done((bf16[128,384]{1,0:T(8,128)(2,1)S(1)}, bf16[128,384]{1,0:T(8,128)(2,1)S(1)}, u32[]{:S(2)}, u32[]{:S(2)}) %collective-permute-start.13) | collective-permute-done | bytes 98336 | tf_op jit(solution)/shard_map/ppermute | solution.py:209
  167.7 3.7 %shard_map.80 = bf16[512,1024]{1,0:T(8,128)(2,1)S(1)} custom-call(s32[2]{0:T(128)S(1)} %pad_add_fusion.pos, bf16[1536,512]{1,0:T(8,128)(2,1)S(1)} %copy-done.8, bf16[1536,512]{1,0:T(8,128)(2,1)} %collective-permute-done.6.down_other, bf16[256,384]{1,0:T(8,128)(2,1)S(1)} %shard_map.78.refs_0_, bf16[256,384]{1,0:T(8,128)(2,1)S(1)} %collective-permute-done.7.refs_1_, ...), custom_call_target="tpu_custom_call" | custom-call | flops 1610612736 | bytes 4194304 | tf_op jit(solution)/shard_map/pallas_call | solution.py:301
  172.4 6.8 %all-to-all-start.4 = ((bf16[32,16,1024]{2,1,0:T(8,128)(2,1)}), bf16[32,16,1024]{2,1,0:T(8,128)(2,1)}, u32[]{:S(2)}, u32[]{:S(2)}) async-start(bf16[32,16,1024]{2,1,0:T(8,128)(2,1)} %bitcast.40), calls=%async_computation.4 | async-start | bytes 2097152 | tf_op jit(solution)/shard_map/all_to_all | solution.py:314
  186.1 12.6 %all-gather.3 = bf16[1024,384]{1,0:T(8,128)(2,1)S(1)} all-gather(bf16[256,384]{1,0:T(8,128)(2,1)S(1)} %shard_map.82), channel_id=5, replica_groups=mesh['y'=4,'c'=2,'x'=4,'z'=8] {'y'}, dimensions={0}, use_global_device_ids=true | all-gather | bytes 983040 | tf_op jit(solution)/shard_map/all_gather | solution.py:300
  198.7 3.5 %shard_map.83 = bf16[256,1024]{1,0:T(8,128)(2,1)} custom-call(s32[2]{0:T(128)S(1)} %pad_add_fusion.pos, bf16[1536,512]{1,0:T(8,128)(2,1)S(1)} %copy-done.9, bf16[1536,512]{1,0:T(8,128)(2,1)} %collective-permute-done.6.down_other, bf16[4,256,384]{2,1,0:T(8,128)(2,1)S(1)} %bitcast.34), custom_call_target="tpu_custom_call" | custom-call | flops 805306368 | bytes 3670016 | tf_op jit(solution)/shard_map/pallas_call | solution.py:301
  202.2 9.6 %all-to-all-start.5 = ((bf16[32,8,1024]{2,1,0:T(8,128)(2,1)}), bf16[32,8,1024]{2,1,0:T(8,128)(2,1)S(1)}, u32[]{:S(2)}, u32[]{:S(2)}) async-start(bf16[32,8,1024]{2,1,0:T(8,128)(2,1)} %bitcast.23), calls=%async_computation.5 | async-start | bytes 1048576 | tf_op jit(solution)/shard_map/all_to_all | solution.py:314
  216.8 7.3 %collective-permute-start.15 = (bf16[128,512]{1,0:T(8,128)(2,1)S(1)}, bf16[128,512]{1,0:T(8,128)(2,1)S(1)}, u32[]{:S(2)}, u32[]{:S(2)}) collective-permute-start(bf16[128,512]{1,0:T(8,128)(2,1)S(1)} %get-tuple-element.65), channel_id=1, source_target_pairs={{0,32},{32,0},{1,33},{33,1},{2,34},{34,2},{3,35},{35,3},{4,36},{36... | collective-permute-start | bytes 393224 | tf_op jit(solution)/shard_map/ppermute | solution.py:327
  224.9 7.5 %collective-permute-start.16 = (bf16[128,512]{1,0:T(8,128)(2,1)S(1)}, bf16[128,512]{1,0:T(8,128)(2,1)S(1)}, u32[]{:S(2)}, u32[]{:S(2)}) collective-permute-start(bf16[128,512]{1,0:T(8,128)(2,1)S(1)} %get-tuple-element.70), channel_id=1, source_target_pairs={{0,32},{32,0},{1,33},{33,1},{2,34},{34,2},{3,35},{35,3},{4,36},{36... | collective-permute-start | bytes 393224 | tf_op jit(solution)/shard_map/ppermute | solution.py:327
  (98 shorter events, 57.0 us)
Async XLA Ops:
  11.2 26.3 %all-to-all-start = ((bf16[32,8,1024]{2,1,0:T(8,128)(2,1)}), bf16[32,8,1024]{2,1,0:T(8,128)(2,1)}, u32[]{:S(2)}, u32[]{:S(2)}) async-start(bf16[32,8,1024]{2,1,0:T(8,128)(2,1)} %bitcast.9), calls=%async_computation | async-start | bytes 1048576 | tf_op jit(solution)/shard_map/all_to_all | solution.py:239
  37.5 40.0 %all-to-all-start.1 = ((bf16[32,16,1024]{2,1,0:T(8,128)(2,1)}), bf16[32,16,1024]{2,1,0:T(8,128)(2,1)}, u32[]{:S(2)}, u32[]{:S(2)}) async-start(bf16[32,16,1024]{2,1,0:T(8,128)(2,1)} %bitcast.39), calls=%async_computation.1 | async-start | bytes 2097152 | tf_op jit(solution)/shard_map/all_to_all | solution.py:258
  45.1 89.4 %all-gather.7.cloned.1.call-start = ((), (), s32[]{:S(2)}) async-start(), calls=%async_computation.6 | async-start | bytes 5242880 | tf_op jit(solution)/shard_map/all_gather | solution.py:278
  45.1 27.0 %collective-permute-start.4 = (bf16[192,4096]{1,0:T(8,128)(2,1)}, bf16[192,4096]{1,0:T(8,128)(2,1)S(1)}, u32[]{:S(2)}, u32[]{:S(2)}) collective-permute-start(bf16[192,4096]{1,0:T(8,128)(2,1)} %get-tuple-element.52), channel_id=1, source_target_pairs={{0,32},{32,0},{1,33},{33,1},{2,34},{34,2},{3,35},{35,3},{4,36},{36... | collective-permute-start | bytes 4718600 | tf_op jit(solution)/shard_map/ppermute | solution.py:255
  46.9 25.3 %collective-permute-start.5 = (bf16[192,4096]{1,0:T(8,128)(2,1)}, bf16[192,4096]{1,0:T(8,128)(2,1)S(1)}, u32[]{:S(2)}, u32[]{:S(2)}) collective-permute-start(bf16[192,4096]{1,0:T(8,128)(2,1)} %get-tuple-element.54), channel_id=1, source_target_pairs={{0,32},{32,0},{1,33},{33,1},{2,34},{34,2},{3,35},{35,3},{4,36},{36... | collective-permute-start | bytes 4718600 | tf_op jit(solution)/shard_map/ppermute | solution.py:255
  47.0 13.9 %collective-permute-start.1 = (bf16[256,1024]{1,0:T(8,128)(2,1)}, bf16[256,1024]{1,0:T(8,128)(2,1)S(1)}, u32[]{:S(2)}, u32[]{:S(2)}) collective-permute-start(bf16[256,1024]{1,0:T(8,128)(2,1)} %bitcast.10.own), channel_id=1, source_target_pairs={{0,192},{64,0},{128,64},{192,128},{1,193},{65,1},{129,65},{193,129... | collective-permute-start | bytes 1572872 | tf_op jit(solution)/shard_map/ppermute | solution.py:209
  49.7 14.7 %collective-permute-start = (bf16[256,1024]{1,0:T(8,128)(2,1)}, bf16[256,1024]{1,0:T(8,128)(2,1)S(1)}, u32[]{:S(2)}, u32[]{:S(2)}) collective-permute-start(bf16[256,1024]{1,0:T(8,128)(2,1)} %bitcast.10.own), channel_id=1, source_target_pairs={{0,64},{64,128},{128,192},{192,0},{1,65},{65,129},{129,193},{193,1... | collective-permute-start | bytes 1572872 | tf_op jit(solution)/shard_map/ppermute | solution.py:209
  60.9 7.9 %collective-permute-start.3 = (bf16[128,1024]{1,0:T(8,128)(2,1)S(1)}, bf16[128,1024]{1,0:T(8,128)(2,1)S(1)}, u32[]{:S(2)}, u32[]{:S(2)}) collective-permute-start(bf16[128,1024]{1,0:T(8,128)(2,1)S(1)} %slice.25), channel_id=1, source_target_pairs={{0,192},{64,0},{128,64},{192,128},{1,193},{65,1},{129,65},{193,129... | collective-permute-start | bytes 786440 | tf_op jit(solution)/shard_map/ppermute | solution.py:209
  64.4 7.7 %collective-permute-start.2 = (bf16[128,1024]{1,0:T(8,128)(2,1)S(1)}, bf16[128,1024]{1,0:T(8,128)(2,1)S(1)}, u32[]{:S(2)}, u32[]{:S(2)}) collective-permute-start(bf16[128,1024]{1,0:T(8,128)(2,1)S(1)} %slice.24), channel_id=1, source_target_pairs={{0,64},{64,128},{128,192},{192,0},{1,65},{65,129},{129,193},{193,1... | collective-permute-start | bytes 786440 | tf_op jit(solution)/shard_map/ppermute | solution.py:209
  77.5 27.3 %collective-permute-start.6 = (bf16[1536,512]{1,0:T(8,128)(2,1)}, bf16[1536,512]{1,0:T(8,128)(2,1)}, u32[]{:S(2)}, u32[]{:S(2)}) collective-permute-start(bf16[1536,512]{1,0:T(8,128)(2,1)} %get-tuple-element.57), channel_id=1, source_target_pairs={{0,32},{32,0},{1,33},{33,1},{2,34},{34,2},{3,35},{35,3},{4,36},{36... | collective-permute-start | bytes 4718600 | tf_op jit(solution)/shard_map/ppermute | solution.py:255
  79.9 29.8 %all-to-all-start.2 = ((bf16[32,8,1024]{2,1,0:T(8,128)(2,1)}), bf16[32,8,1024]{2,1,0:T(8,128)(2,1)}, u32[]{:S(2)}, u32[]{:S(2)}) async-start(bf16[32,8,1024]{2,1,0:T(8,128)(2,1)} %bitcast.41), calls=%async_computation.2 | async-start | bytes 1048576 | tf_op jit(solution)/shard_map/all_to_all | solution.py:258
  89.5 89.7 %all-gather.9.cloned.1.call-start = ((), (), s32[]{:S(2)}) async-start(), calls=%async_computation.7 | async-start | bytes 2621440 | tf_op jit(solution)/shard_map/all_gather | solution.py:278
  142.0 5.5 %collective-permute-start.8 = (bf16[256,384]{1,0:T(8,128)(2,1)S(1)}, bf16[256,384]{1,0:T(8,128)(2,1)S(1)}, u32[]{:S(2)}, u32[]{:S(2)}) collective-permute-start(bf16[256,384]{1,0:T(8,128)(2,1)S(1)} %shard_map.78.refs_0_), channel_id=1, source_target_pairs={{0,192},{64,0},{128,64},{192,128},{1,193},{65,1},{129,65},{193,129... | collective-permute-start | bytes 589832 | tf_op jit(solution)/shard_map/ppermute | solution.py:209
  142.1 8.1 %collective-permute-start.7 = (bf16[256,384]{1,0:T(8,128)(2,1)S(1)}, bf16[256,384]{1,0:T(8,128)(2,1)S(1)}, u32[]{:S(2)}, u32[]{:S(2)}) collective-permute-start(bf16[256,384]{1,0:T(8,128)(2,1)S(1)} %shard_map.78.refs_0_), channel_id=1, source_target_pairs={{0,64},{64,128},{128,192},{192,0},{1,65},{65,129},{129,193},{193,1... | collective-permute-start | bytes 589832 | tf_op jit(solution)/shard_map/ppermute | solution.py:209
  146.0 9.1 %collective-permute-start.12 = (bf16[256,384]{1,0:T(8,128)(2,1)S(1)}, bf16[256,384]{1,0:T(8,128)(2,1)S(1)}, u32[]{:S(2)}, u32[]{:S(2)}) collective-permute-start(bf16[256,384]{1,0:T(8,128)(2,1)S(1)} %shard_map.79.refs_5_), channel_id=1, source_target_pairs={{0,192},{64,0},{128,64},{192,128},{1,193},{65,1},{129,65},{193,129... | collective-permute-start | bytes 589832 | tf_op jit(solution)/shard_map/ppermute | solution.py:209
  147.3 11.9 %collective-permute-start.11 = (bf16[256,384]{1,0:T(8,128)(2,1)S(1)}, bf16[256,384]{1,0:T(8,128)(2,1)S(1)}, u32[]{:S(2)}, u32[]{:S(2)}) collective-permute-start(bf16[256,384]{1,0:T(8,128)(2,1)S(1)} %shard_map.79.refs_5_), channel_id=1, source_target_pairs={{0,64},{64,128},{128,192},{192,0},{1,65},{65,129},{129,193},{193,1... | collective-permute-start | bytes 589832 | tf_op jit(solution)/shard_map/ppermute | solution.py:209
  147.5 11.8 %collective-permute-start.10 = (bf16[128,384]{1,0:T(8,128)(2,1)S(1)}, bf16[128,384]{1,0:T(8,128)(2,1)S(1)}, u32[]{:S(2)}, u32[]{:S(2)}) collective-permute-start(bf16[128,384]{1,0:T(8,128)(2,1)S(1)} %slice.27), channel_id=1, source_target_pairs={{0,192},{64,0},{128,64},{192,128},{1,193},{65,1},{129,65},{193,129... | collective-permute-start | bytes 294920 | tf_op jit(solution)/shard_map/ppermute | solution.py:209
  150.1 13.3 %collective-permute-start.9 = (bf16[128,384]{1,0:T(8,128)(2,1)S(1)}, bf16[128,384]{1,0:T(8,128)(2,1)S(1)}, u32[]{:S(2)}, u32[]{:S(2)}) collective-permute-start(bf16[128,384]{1,0:T(8,128)(2,1)S(1)} %slice.26), channel_id=1, source_target_pairs={{0,64},{64,128},{128,192},{192,0},{1,65},{65,129},{129,193},{193,1... | collective-permute-start | bytes 294920 | tf_op jit(solution)/shard_map/ppermute | solution.py:209
  155.1 8.4 %collective-permute-start.14 = (bf16[128,384]{1,0:T(8,128)(2,1)S(1)}, bf16[128,384]{1,0:T(8,128)(2,1)S(1)}, u32[]{:S(2)}, u32[]{:S(2)}) collective-permute-start(bf16[128,384]{1,0:T(8,128)(2,1)S(1)} %slice.29), channel_id=1, source_target_pairs={{0,192},{64,0},{128,64},{192,128},{1,193},{65,1},{129,65},{193,129... | collective-permute-start | bytes 294920 | tf_op jit(solution)/shard_map/ppermute | solution.py:209
  159.2 8.4 %collective-permute-start.13 = (bf16[128,384]{1,0:T(8,128)(2,1)S(1)}, bf16[128,384]{1,0:T(8,128)(2,1)S(1)}, u32[]{:S(2)}, u32[]{:S(2)}) collective-permute-start(bf16[128,384]{1,0:T(8,128)(2,1)S(1)} %slice.28), channel_id=1, source_target_pairs={{0,64},{64,128},{128,192},{192,0},{1,65},{65,129},{129,193},{193,1... | collective-permute-start | bytes 294920 | tf_op jit(solution)/shard_map/ppermute | solution.py:209
  172.4 29.8 %all-to-all-start.4 = ((bf16[32,16,1024]{2,1,0:T(8,128)(2,1)}), bf16[32,16,1024]{2,1,0:T(8,128)(2,1)}, u32[]{:S(2)}, u32[]{:S(2)}) async-start(bf16[32,16,1024]{2,1,0:T(8,128)(2,1)} %bitcast.40), calls=%async_computation.4 | async-start | bytes 2097152 | tf_op jit(solution)/shard_map/all_to_all | solution.py:314
  202.2 22.0 %all-to-all-start.5 = ((bf16[32,8,1024]{2,1,0:T(8,128)(2,1)}), bf16[32,8,1024]{2,1,0:T(8,128)(2,1)S(1)}, u32[]{:S(2)}, u32[]{:S(2)}) async-start(bf16[32,8,1024]{2,1,0:T(8,128)(2,1)} %bitcast.23), calls=%async_computation.5 | async-start | bytes 1048576 | tf_op jit(solution)/shard_map/all_to_all | solution.py:314
  216.8 15.6 %collective-permute-start.15 = (bf16[128,512]{1,0:T(8,128)(2,1)S(1)}, bf16[128,512]{1,0:T(8,128)(2,1)S(1)}, u32[]{:S(2)}, u32[]{:S(2)}) collective-permute-start(bf16[128,512]{1,0:T(8,128)(2,1)S(1)} %get-tuple-element.65), channel_id=1, source_target_pairs={{0,32},{32,0},{1,33},{33,1},{2,34},{34,2},{3,35},{35,3},{4,36},{36... | collective-permute-start | bytes 393224 | tf_op jit(solution)/shard_map/ppermute | solution.py:327
  224.9 8.5 %collective-permute-start.16 = (bf16[128,512]{1,0:T(8,128)(2,1)S(1)}, bf16[128,512]{1,0:T(8,128)(2,1)S(1)}, u32[]{:S(2)}, u32[]{:S(2)}) collective-permute-start(bf16[128,512]{1,0:T(8,128)(2,1)S(1)} %get-tuple-element.70), channel_id=1, source_target_pairs={{0,32},{32,0},{1,33},{33,1},{2,34},{34,2},{3,35},{35,3},{4,36},{36... | collective-permute-start | bytes 393224 | tf_op jit(solution)/shard_map/ppermute | solution.py:327
  (23 other events, 93.2 us)
Sparse Core Ops, SparseCore 0:
  77.6 56.8 all-gather.6
  136.3 42.3 all-gather.8

commit v7 on v6

--- a/solution.py
+++ b/solution.py
@@ -12,8 +12,7 @@
 BF16 = jnp.bfloat16
 NY, NC, NX, NZ = 4, 2, 4, 8
 N_EXP = NX * NZ
-CHUNKS = ((0, 8), (8, 16), (24, 8))
-PIECE = 256
+CHUNKS = ((0, 16), (16, 16))
 
 VMEM = pl.BlockSpec(memory_space=pltpu.VMEM)
 SMEM = pl.BlockSpec(memory_space=pltpu.SMEM)
@@ -126,16 +125,15 @@
     return jnp.transpose(jnp.concatenate([low, high], axis=0)).astype(BF16)
 
 
-def hidden_kernel(half, pos, blocks, gate_own, gate_other, up_own, up_other, out):
+def hidden_kernel(pos, blocks, gate_own, gate_other, up_own, up_other, out):
     quarter = blocks.shape[2]
-    rows = slice(half * PIECE, (half + 1) * PIECE)
     total = None
     for y in range(NY):
         cols = slice(y * quarter, (y + 1) * quarter)
         weights = jnp.concatenate(
             [weight[:, cols] for weight in (gate_own, up_own, gate_other, up_other)], axis=0
         )
-        term = by_rows(weights, blocks[y, rows, :])
+        term = by_rows(weights, blocks[y])
         total = term if y == 0 else total + term
     out[...] = activate(pos, total)
 
@@ -157,39 +155,20 @@
     out[...] = activate(pos, total)
 
 
-def store_columns(pos, out, at, own, other):
-    cols = own.shape[1]
-    for core, total in ((pos[1], own), (1 - pos[1], other)):
-        out[at, pl.ds(pl.multiple_of(core * cols, cols), cols)] = total.astype(BF16)
-
-
-def down_kernel(pos, down_own, down_other, blocks, out):
-    rows, units = blocks.shape[1:]
-    own = other = None
-    for y in range(NY):
-        span = slice(y * units, (y + 1) * units)
-        own_term = times(blocks[y], down_own[span, :])
-        other_term = times(blocks[y], down_other[span, :])
-        own = own_term if y == 0 else own + own_term
-        other = other_term if y == 0 else other + other_term
-    store_columns(pos, out, slice(0, rows), own, other)
-
-
-def down_ring_kernel(pos, down_own, down_other, *refs):
-    out = refs[-1]
-    for index in range(len(refs) // 5):
-        own, low, high, far_top, far_bottom = refs[5 * index : 5 * index + 5]
-        rows, units = own.shape
-        far = jnp.concatenate([far_top[...], far_bottom[...]], axis=0)
-        mine = theirs = None
-        for block, step in ((own[...], 0), (low[...], 3), (high[...], 1), (far, 2)):
-            at = lax.rem(pos[0] + step, NY)
-            span = pl.ds(pl.multiple_of(at * units, units), units)
-            own_term = times(block, down_own[span, :])
-            other_term = times(block, down_other[span, :])
-            mine = own_term if mine is None else mine + own_term
-            theirs = other_term if theirs is None else theirs + other_term
-        store_columns(pos, out, slice(index * rows, (index + 1) * rows), mine, theirs)
+def down_kernel(pos, down_own, down_other, own, low, high, far_top, far_bottom, out):
+    units = own.shape[1]
+    cols = down_own.shape[1]
+    far = jnp.concatenate([far_top[...], far_bottom[...]], axis=0)
+    mine = theirs = None
+    for block, step in ((own[...], 0), (low[...], 3), (high[...], 1), (far, 2)):
+        at = lax.rem(pos[0] + step, NY)
+        span = pl.ds(pl.multiple_of(at * units, units), units)
+        own_term = times(block, down_own[span, :])
+        other_term = times(block, down_other[span, :])
+        mine = own_term if mine is None else mine + own_term
+        theirs = other_term if theirs is None else theirs + other_term
+    for core, total in ((pos[1], mine), (1 - pos[1], theirs)):
+        out[:, pl.ds(pl.multiple_of(core * cols, cols), cols)] = total.astype(BF16)
 
 
 def combine_kernel(pos, *refs):
@@ -209,11 +188,17 @@
     return lax.ppermute(array, "y", [(i, (i + step) % NY) for i in range(NY)])
 
 
+def ring_start(block):
+    return turn(block, 1), turn(block, -1)
+
+
+def ring_end(block, low, high):
+    half = block.shape[0] // 2
+    return block, low, high, turn(low[:half], 1), turn(high[half:], -1)
+
+
 def ring(block):
-    half = block.shape[0] // 2
-    low = turn(block, 1)
-    high = turn(block, -1)
-    return block, low, high, turn(low[:half], 1), turn(high[half:], -1)
+    return ring_end(block, *ring_start(block))
 
 
 def body(tokens, norm_gain, router, routes, w_gate, w_up, w_down):
@@ -267,50 +252,40 @@
     )(pos, tokens, gain, router, turned)
 
     returned = []
-    done = []
+    low, high = ring_start(received[1])
+    gathered = lax.all_gather(received[0], "y", axis=0)
+    gathered, low, high = lax.optimization_barrier((gathered, low, high))
+    later = ring_end(received[1], low, high)
     for index, size in enumerate(sizes):
-        mine = received[index]
+        inputs = later if index else (gathered,)
+        if index:
+            *inputs, first_hidden = lax.optimization_barrier((*inputs, first_hidden))
+        hidden = pl.pallas_call(
+            hidden_ring_kernel if index else hidden_kernel,
+            out_shape=sds((size, units), BF16),
+            in_specs=[SMEM] + [VMEM] * (4 + len(inputs)),
+            out_specs=VMEM,
+            compiler_params=params(16),
+            cost_estimate=cost(4 * size * width * units, 4 * units * width + 2 * size * width),
+        )(pos, *inputs, own[0], others[0], own[1], others[1])
+        first_hidden = hidden
+        pieces = ring(hidden)
         if index == 0:
-            inputs = ring(mine)
+            mixed = lax.optimization_barrier((*pieces, *later))
+            pieces, later = mixed[:5], mixed[5:]
         else:
-            if index == 2:
-                mine, *_ = lax.optimization_barrier((mine, *done))
-            blocks = lax.all_gather(mine, "y", axis=0)
-            if index == 1:
-                blocks, returned[0] = lax.optimization_barrier((blocks, returned[0]))
-                done.append(blocks)
-            inputs = (blocks,)
-        pieces = []
-        for half in range(size // PIECE):
-            hidden = pl.pallas_call(
-                functools.partial(hidden_kernel, half) if index else hidden_ring_kernel,
-                out_shape=sds((PIECE, units), BF16),
-                in_specs=[SMEM] + [VMEM] * (4 + len(inputs)),
-                out_specs=VMEM,
-                compiler_params=params(24),
-                cost_estimate=cost(
-                    4 * PIECE * width * units, 4 * units * width + 2 * PIECE * width
-                ),
-            )(pos, *inputs, own[0], others[0], own[1], others[1])
-            if index == 0:
-                received[1], hidden = lax.optimization_barrier((received[1], hidden))
-            if size > PIECE:
-                pieces.extend(ring(hidden))
-            else:
-                pieces.append(lax.all_gather(hidden, "y", axis=0))
+            *pieces, first_result = lax.optimization_barrier((*pieces, first_result))
         result = pl.pallas_call(
-            down_ring_kernel if size > PIECE else down_kernel,
+            down_kernel,
             out_shape=sds((size, NC * cols), BF16),
-            in_specs=[SMEM] + [VMEM] * (2 + len(pieces)),
+            in_specs=[SMEM] + [VMEM] * 7,
             out_specs=VMEM,
-            compiler_params=params(24),
+            compiler_params=params(16),
             cost_estimate=cost(
                 2 * size * ff * NC * cols, 2 * ff * NC * cols + 2 * size * NC * cols
             ),
         )(pos, own[2], others[2], *pieces)
-        if index == 0:
-            result, received[-1] = lax.optimization_barrier((result, received[-1]))
-            done.append(result)
+        first_result = result
         returned.append(lax.all_to_all(result, ("x", "z"), 0, 0, tiled=True))
 
     total = None

time: 242 us -> 250 us (1.033)
  waiting for transfers between devices: 40.9 us -> 108 us
  blocking collectives: 49.4 us -> 0 us
  local copies, waits for them, and re-layouts: 28.5 us -> 19 us
    all_gather x2 -> x0, blocking collectives: 27.8 us -> none  [body(): pieces.append(lax.all_gather(hidden, 'y', axis=0))]
    ppermute x12, waiting for transfers between devices: 32.5 us -> 56.8 us  [turn(): return lax.ppermute(array, 'y', [(i, (i + step) % NY) for i in range(NY)])]
    all_to_all x2 -> x1, waiting for transfers between devices: 0.01 us -> 23.1 us  [body(): received.append(lax.all_to_all(rows, ('x', 'z'), 0, 0, tiled=True))]
    all_to_all x1 -> x0, blocking collectives: 21.6 us -> none  [body(): returned.append(lax.all_to_all(result, ('x', 'z'), 0, 0, tiled=True))]
    unnamed x46 -> x30, local copies, waits for them, and re-layouts: 21.7 us -> 9.97 us
    all_to_all x2, waiting for transfers between devices: 0.01 us -> 11.7 us  [body(): returned.append(lax.all_to_all(result, ('x', 'z'), 0, 0, tiled=True))]
    all_to_all x1, waiting for transfers between devices: 4.16 us -> 15.3 us  [body(): received = [lax.all_to_all(first_rows, ('x', 'z'), 0, 0, tiled=True)]]
    all_to_all x2 -> x1, starting transfers between devices: 17.2 us -> 8.72 us  [body(): received.append(lax.all_to_all(rows, ('x', 'z'), 0, 0, tiled=True))]
  transfers between devices with their start and end apart: 24 -> 22, of which waited for: 11 -> 11; matrix products, arithmetic and copies ran while one was open for 3% -> 3% of each run, Pallas kernels for 10% -> 8%
where the time goes in v7:
time: 250 us; the launch traced here: 249 us
  waiting for transfers between devices  108 us (43%)
  starting transfers between devices  79.3 us (32%)
  Pallas kernels  27.9 us (11%)
  local copies, waits for them, and re-layouts  19 us (8%)
  between operations  13.7 us (5%)
    ppermute x12, waiting for transfers between devices, turn(): return lax.ppermute(array, 'y', [(i, (i + step) % NY) for i in range(NY)])  56.8 us
    all_to_all x1, waiting for transfers between devices, body(): received.append(lax.all_to_all(rows, ('x', 'z'), 0, 0, tiled=True))  23.1 us
    all_to_all x2, starting transfers between devices, body(): returned.append(lax.all_to_all(result, ('x', 'z'), 0, 0, tiled=True))  20.9 us
    ppermute x12, starting transfers between devices, turn(): return lax.ppermute(array, 'y', [(i, (i + step) % NY) for i in range(NY)])  15.7 us
    all_to_all x1, waiting for transfers between devices, body(): received = [lax.all_to_all(first_rows, ('x', 'z'), 0, 0, tiled=True)]  15.3 us
    ppermute x2, starting transfers between devices, body(): give = lax.ppermute(give, 'c', [(0, 1), (1, 0)])  14.8 us
    pallas_call x2, Pallas kernels, body(): pl.pallas_call(hidden_ring_kernel if index else hidden_kernel, out_shape=...  12 us
    all_to_all x1, starting transfers between devices, body(): received = [lax.all_to_all(first_rows, ('x', 'z'), 0, 0, tiled=True)]  12 us
  transfers between devices with their start and end apart: 22, of which 11 were waited for; matrix products, arithmetic and copies ran while one was open for 3% of the time, Pallas kernels for 8%

profile of v7, /device:TPU:1, one launch (start us, length us, event | category | flops | bytes accessed | tf_op | source)
XLA Modules:
  0.0 248.7 jit_solution(18433845234546893289)
XLA Ops:
  11.5 12.0 %all-to-all-start = ((bf16[32,16,1024]{2,1,0:T(8,128)(2,1)}), bf16[32,16,1024]{2,1,0:T(8,128)(2,1)}, u32[]{:S(2)}, u32[]{:S(2)}) async-start(bf16[32,16,1024]{2,1,0:T(8,128)(2,1)} %bitcast.9), calls=%async_computation | async-start | bytes 2097152 | tf_op jit(solution)/shard_map/all_to_all | solution.py:224
  25.7 3.9 %dynamic-slice_bitcast_fusion = (bf16[1536,512]{1,0:T(8,128)(2,1)}, bf16[1536,512]{1,0:T(8,128)(2,1)}) fusion(bf16[2,1536,512]{2,1,0:T(8,128)(2,1)} %param.13, s32[]{:T(128)S(6)} %select_n.13, s32[]{:T(128)S(6)} %select_n.12), kind=kLoop, calls=%fused_computation | loop fusion | bytes 6291464 | tf_op jit(solution)/shard_map/jit(dynamic_index_in_dim)/squeeze | solution.py:235
  32.8 15.3 %all-to-all-done = bf16[32,16,1024]{2,1,0:T(8,128)(2,1)} async-done(((bf16[32,16,1024]{2,1,0:T(8,128)(2,1)}), bf16[32,16,1024]{2,1,0:T(8,128)(2,1)}, u32[]{:S(2)}, u32[]{:S(2)}) %all-to-all-start) | async-done | bytes 1048608 | tf_op jit(solution)/shard_map/all_to_all | solution.py:224
  48.2 8.7 %all-to-all-start.1 = ((bf16[32,16,1024]{2,1,0:T(8,128)(2,1)}), bf16[32,16,1024]{2,1,0:T(8,128)(2,1)}, u32[]{:S(2)}, u32[]{:S(2)}) async-start(bf16[32,16,1024]{2,1,0:T(8,128)(2,1)} %bitcast.12), calls=%async_computation.1 | async-start | bytes 2097152 | tf_op jit(solution)/shard_map/all_to_all | solution.py:243
  58.6 23.1 %all-to-all-done.1 = bf16[32,16,1024]{2,1,0:T(8,128)(2,1)} async-done(((bf16[32,16,1024]{2,1,0:T(8,128)(2,1)}), bf16[32,16,1024]{2,1,0:T(8,128)(2,1)}, u32[]{:S(2)}, u32[]{:S(2)}) %all-to-all-start.1) | async-done | bytes 1048608 | tf_op jit(solution)/shard_map/all_to_all | solution.py:243
  84.4 5.5 %collective-permute-start = (bf16[1536,512]{1,0:T(8,128)(2,1)}, bf16[1536,512]{1,0:T(8,128)(2,1)}, u32[]{:S(2)}, u32[]{:S(2)}) collective-permute-start(bf16[1536,512]{1,0:T(8,128)(2,1)} %get-tuple-element.58), channel_id=1, source_target_pairs={{0,32},{32,0},{1,33},{33,1},{2,34},{34,2},{3,35},{35,3},{4,36},{36... | collective-permute-start | bytes 4718600 | tf_op jit(solution)/shard_map/ppermute | solution.py:240
  89.9 31.0 %collective-permute-done.1.low = bf16[512,1024]{1,0:T(8,128)(2,1)} collective-permute-done((bf16[512,1024]{1,0:T(8,128)(2,1)}, bf16[512,1024]{1,0:T(8,128)(2,1)}, u32[]{:S(2)}, u32[]{:S(2)}) %collective-permute-start.1) | collective-permute-done | bytes 1048608 | tf_op jit(solution)/shard_map/ppermute | solution.py:188
  123.1 5.5 %shard_map.76.own = bf16[512,384]{1,0:T(8,128)(2,1)S(1)} custom-call(s32[2]{0:T(128)S(1)} %pad_add_fusion.pos, bf16[4,512,1024]{2,1,0:T(8,128)(2,1)S(1)} %bitcast.30, bf16[192,4096]{1,0:T(8,128)(2,1)S(1)} %get-tuple-element.62.gate_own, bf16[192,4096]{1,0:T(8,128)(2,1)} %collective-permute-done.3.gate_other, bf16[192,4096]{1,0:T(8,128)(2,1)S(1)} %get-tuple-element.64.up_own, ...), custom_call_target="tpu_custom_call" | custom-call | flops 3221225472 | bytes 10485760 | tf_op jit(solution)/shard_map/pallas_call | solution.py:263
  135.1 3.2 %collective-permute-done.5.low = bf16[512,384]{1,0:T(8,128)(2,1)S(1)} collective-permute-done((bf16[512,384]{1,0:T(8,128)(2,1)S(1)}, bf16[512,384]{1,0:T(8,128)(2,1)S(1)}, u32[]{:S(2)}, u32[]{:S(2)}) %collective-permute-start.5) | collective-permute-done | bytes 393248 | tf_op jit(solution)/shard_map/ppermute | solution.py:188
  138.6 2.7 %collective-permute-start.8 = (bf16[256,384]{1,0:T(8,128)(2,1)S(1)}, bf16[256,384]{1,0:T(8,128)(2,1)S(1)}, u32[]{:S(2)}, u32[]{:S(2)}) collective-permute-start(bf16[256,384]{1,0:T(8,128)(2,1)S(1)} %slice.25), channel_id=1, source_target_pairs={{0,192},{64,0},{128,64},{192,128},{1,193},{65,1},{129,65},{193,129... | collective-permute-start | bytes 589832 | tf_op jit(solution)/shard_map/ppermute | solution.py:188
  141.4 7.2 %collective-permute-done.10.far_bottom = bf16[256,1024]{1,0:T(8,128)(2,1)S(1)} collective-permute-done((bf16[256,1024]{1,0:T(8,128)(2,1)S(1)}, bf16[256,1024]{1,0:T(8,128)(2,1)S(1)}, u32[]{:S(2)}, u32[]{:S(2)}) %collective-permute-start.10) | collective-permute-done | bytes 524320 | tf_op jit(solution)/shard_map/ppermute | solution.py:188
  149.5 4.2 %collective-permute-done.7.far_top = bf16[256,384]{1,0:T(8,128)(2,1)S(1)} collective-permute-done((bf16[256,384]{1,0:T(8,128)(2,1)S(1)}, bf16[256,384]{1,0:T(8,128)(2,1)S(1)}, u32[]{:S(2)}, u32[]{:S(2)}) %collective-permute-start.7) | collective-permute-done | bytes 196640 | tf_op jit(solution)/shard_map/ppermute | solution.py:188
  153.8 4.8 %shard_map.77 = bf16[512,1024]{1,0:T(8,128)(2,1)} custom-call(s32[2]{0:T(128)S(1)} %pad_add_fusion.pos, bf16[1536,512]{1,0:T(8,128)(2,1)S(1)} %copy-done.6, bf16[1536,512]{1,0:T(8,128)(2,1)} %collective-permute-done.down_other, bf16[512,384]{1,0:T(8,128)(2,1)S(1)} %shard_map.76.own, bf16[512,384]{1,0:T(8,128)(2,1)S(1)} %collective-permute-done.5.low, ...), custom_call_target="tpu_custom_call" | custom-call | flops 1610612736 | bytes 4194304 | tf_op jit(solution)/shard_map/pallas_call | solution.py:278
  158.5 12.1 %all-to-all-start.2 = ((bf16[32,16,1024]{2,1,0:T(8,128)(2,1)}), bf16[32,16,1024]{2,1,0:T(8,128)(2,1)S(1)}, u32[]{:S(2)}, u32[]{:S(2)}) async-start(bf16[32,16,1024]{2,1,0:T(8,128)(2,1)} %bitcast.14), calls=%async_computation.2 | async-start | bytes 2097152 | tf_op jit(solution)/shard_map/all_to_all | solution.py:289
  173.5 6.5 %shard_map.79.own = bf16[512,384]{1,0:T(8,128)(2,1)S(1)} custom-call(s32[2]{0:T(128)S(1)} %pad_add_fusion.pos, bf16[512,1024]{1,0:T(8,128)(2,1)} %bitcast.13.own, bf16[512,1024]{1,0:T(8,128)(2,1)} %collective-permute-done.1.low, bf16[512,1024]{1,0:T(8,128)(2,1)} %collective-permute-done.2.high, bf16[256,1024]{1,0:T(8,128)(2,1)S(1)} %collective-permute-done.9.far_top, ...), custom_call_target="tpu_custom_call" | custom-call | flops 3221225472 | bytes 10485760 | tf_op jit(solution)/shard_map/pallas_call | solution.py:263
  180.1 2.7 %collective-permute-start.13 = (bf16[512,384]{1,0:T(8,128)(2,1)S(1)}, bf16[512,384]{1,0:T(8,128)(2,1)S(1)}, u32[]{:S(2)}, u32[]{:S(2)}) collective-permute-start(bf16[512,384]{1,0:T(8,128)(2,1)S(1)} %shard_map.79.own), channel_id=1, source_target_pairs={{0,192},{64,0},{128,64},{192,128},{1,193},{65,1},{129,65},{193,129... | collective-permute-start | bytes 1179656 | tf_op jit(solution)/shard_map/ppermute | solution.py:188
  182.8 7.1 %collective-permute-done.12.low = bf16[512,384]{1,0:T(8,128)(2,1)S(1)} collective-permute-done((bf16[512,384]{1,0:T(8,128)(2,1)S(1)}, bf16[512,384]{1,0:T(8,128)(2,1)S(1)}, u32[]{:S(2)}, u32[]{:S(2)}) %collective-permute-start.12) | collective-permute-done | bytes 393248 | tf_op jit(solution)/shard_map/ppermute | solution.py:188
  190.0 2.7 %collective-permute-start.15 = (bf16[256,384]{1,0:T(8,128)(2,1)S(1)}, bf16[256,384]{1,0:T(8,128)(2,1)S(1)}, u32[]{:S(2)}, u32[]{:S(2)}) collective-permute-start(bf16[256,384]{1,0:T(8,128)(2,1)S(1)} %slice.27), channel_id=1, source_target_pairs={{0,192},{64,0},{128,64},{192,128},{1,193},{65,1},{129,65},{193,129... | collective-permute-start | bytes 589832 | tf_op jit(solution)/shard_map/ppermute | solution.py:188
  192.7 3.2 %collective-permute-done.14.far_top = bf16[256,384]{1,0:T(8,128)(2,1)S(1)} collective-permute-done((bf16[256,384]{1,0:T(8,128)(2,1)S(1)}, bf16[256,384]{1,0:T(8,128)(2,1)S(1)}, u32[]{:S(2)}, u32[]{:S(2)}) %collective-permute-start.14) | collective-permute-done | bytes 196640 | tf_op jit(solution)/shard_map/ppermute | solution.py:188
  196.0 3.7 %shard_map.80 = bf16[512,1024]{1,0:T(8,128)(2,1)S(1)} custom-call(s32[2]{0:T(128)S(1)} %pad_add_fusion.pos, bf16[1536,512]{1,0:T(8,128)(2,1)S(1)} %copy-done.7, bf16[1536,512]{1,0:T(8,128)(2,1)} %collective-permute-done.down_other, bf16[512,384]{1,0:T(8,128)(2,1)S(1)} %shard_map.79.own, bf16[512,384]{1,0:T(8,128)(2,1)S(1)} %collective-permute-done.12.low, ...), custom_call_target="tpu_custom_call" | custom-call | flops 1610612736 | bytes 4194304 | tf_op jit(solution)/shard_map/pallas_call | solution.py:278
  200.7 8.8 %all-to-all-start.3 = ((bf16[32,16,1024]{2,1,0:T(8,128)(2,1)}), bf16[32,16,1024]{2,1,0:T(8,128)(2,1)S(1)}, u32[]{:S(2)}, u32[]{:S(2)}) async-start(bf16[32,16,1024]{2,1,0:T(8,128)(2,1)} %bitcast.26), calls=%async_computation.3 | async-start | bytes 2097152 | tf_op jit(solution)/shard_map/all_to_all | solution.py:289
  212.8 4.8 %collective-permute-start.11 = (bf16[128,512]{1,0:T(8,128)(2,1)S(1)}, bf16[128,512]{1,0:T(8,128)(2,1)S(1)}, u32[]{:S(2)}, u32[]{:S(2)}) collective-permute-start(bf16[128,512]{1,0:T(8,128)(2,1)S(1)} %get-tuple-element.74), channel_id=1, source_target_pairs={{0,32},{32,0},{1,33},{33,1},{2,34},{34,2},{3,35},{35,3},{4,36},{36... | collective-permute-start | bytes 393224 | tf_op jit(solution)/shard_map/ppermute | solution.py:302
  217.6 11.7 %all-to-all-done.3 = bf16[32,16,1024]{2,1,0:T(8,128)(2,1)S(1)} async-done(((bf16[32,16,1024]{2,1,0:T(8,128)(2,1)}), bf16[32,16,1024]{2,1,0:T(8,128)(2,1)S(1)}, u32[]{:S(2)}, u32[]{:S(2)}) %all-to-all-start.3) | async-done | bytes 1048608 | tf_op jit(solution)/shard_map/all_to_all | solution.py:289
  230.1 10.0 %collective-permute-start.16 = (bf16[128,512]{1,0:T(8,128)(2,1)S(1)}, bf16[128,512]{1,0:T(8,128)(2,1)S(1)}, u32[]{:S(2)}, u32[]{:S(2)}) collective-permute-start(bf16[128,512]{1,0:T(8,128)(2,1)S(1)} %get-tuple-element.92), channel_id=1, source_target_pairs={{0,32},{32,0},{1,33},{33,1},{2,34},{34,2},{3,35},{35,3},{4,36},{36... | collective-permute-start | bytes 393224 | tf_op jit(solution)/shard_map/ppermute | solution.py:302
  (71 shorter events, 34.6 us)
Async XLA Ops:
  11.5 36.6 %all-to-all-start = ((bf16[32,16,1024]{2,1,0:T(8,128)(2,1)}), bf16[32,16,1024]{2,1,0:T(8,128)(2,1)}, u32[]{:S(2)}, u32[]{:S(2)}) async-start(bf16[32,16,1024]{2,1,0:T(8,128)(2,1)} %bitcast.9), calls=%async_computation | async-start | bytes 2097152 | tf_op jit(solution)/shard_map/all_to_all | solution.py:224
  23.5 97.3 %all-gather.3.cloned.1.call-start = ((), (), s32[]{:S(2)}) async-start(), calls=%async_computation.4 | async-start | bytes 5242880 | tf_op jit(solution)/shard_map/all_gather | solution.py:256
  32.8 88.1 %copy-start.2 = (bf16[192,4096]{1,0:T(8,128)(2,1)}, bf16[192,4096]{1,0:T(8,128)(2,1)S(1)}, u32[]{:S(2)}) copy-start(bf16[192,4096]{1,0:T(8,128)(2,1)S(1)} %get-tuple-element.64.up_own) | copy-start | bytes 4718596
  32.8 88.1 %copy-start.4 = (bf16[192,4096]{1,0:T(8,128)(2,1)}, bf16[192,4096]{1,0:T(8,128)(2,1)S(1)}, u32[]{:S(2)}) copy-start(bf16[192,4096]{1,0:T(8,128)(2,1)S(1)} %get-tuple-element.62.gate_own) | copy-start | bytes 4718596
  48.2 33.5 %all-to-all-start.1 = ((bf16[32,16,1024]{2,1,0:T(8,128)(2,1)}), bf16[32,16,1024]{2,1,0:T(8,128)(2,1)}, u32[]{:S(2)}, u32[]{:S(2)}) async-start(bf16[32,16,1024]{2,1,0:T(8,128)(2,1)} %bitcast.12), calls=%async_computation.1 | async-start | bytes 2097152 | tf_op jit(solution)/shard_map/all_to_all | solution.py:243
  56.9 64.0 %collective-permute-start.3 = (bf16[192,4096]{1,0:T(8,128)(2,1)}, bf16[192,4096]{1,0:T(8,128)(2,1)}, u32[]{:S(2)}, u32[]{:S(2)}) collective-permute-start(bf16[192,4096]{1,0:T(8,128)(2,1)} %get-tuple-element.63), channel_id=1, source_target_pairs={{0,32},{32,0},{1,33},{33,1},{2,34},{34,2},{3,35},{35,3},{4,36},{36... | collective-permute-start | bytes 4718600 | tf_op jit(solution)/shard_map/ppermute | solution.py:240
  58.5 62.4 %collective-permute-start.4 = (bf16[192,4096]{1,0:T(8,128)(2,1)}, bf16[192,4096]{1,0:T(8,128)(2,1)}, u32[]{:S(2)}, u32[]{:S(2)}) collective-permute-start(bf16[192,4096]{1,0:T(8,128)(2,1)} %get-tuple-element.65), channel_id=1, source_target_pairs={{0,32},{32,0},{1,33},{33,1},{2,34},{34,2},{3,35},{35,3},{4,36},{36... | collective-permute-start | bytes 4718600 | tf_op jit(solution)/shard_map/ppermute | solution.py:240
  81.7 39.2 %collective-permute-start.1 = (bf16[512,1024]{1,0:T(8,128)(2,1)}, bf16[512,1024]{1,0:T(8,128)(2,1)}, u32[]{:S(2)}, u32[]{:S(2)}) collective-permute-start(bf16[512,1024]{1,0:T(8,128)(2,1)} %bitcast.13.own), channel_id=1, source_target_pairs={{0,64},{64,128},{128,192},{192,0},{1,65},{65,129},{129,193},{193,1... | collective-permute-start | bytes 3145736 | tf_op jit(solution)/shard_map/ppermute | solution.py:188
  82.9 37.9 %collective-permute-start.2 = (bf16[512,1024]{1,0:T(8,128)(2,1)}, bf16[512,1024]{1,0:T(8,128)(2,1)}, u32[]{:S(2)}, u32[]{:S(2)}) collective-permute-start(bf16[512,1024]{1,0:T(8,128)(2,1)} %bitcast.13.own), channel_id=1, source_target_pairs={{0,192},{64,0},{128,64},{192,128},{1,193},{65,1},{129,65},{193,129... | collective-permute-start | bytes 3145736 | tf_op jit(solution)/shard_map/ppermute | solution.py:188
  84.4 69.4 %collective-permute-start = (bf16[1536,512]{1,0:T(8,128)(2,1)}, bf16[1536,512]{1,0:T(8,128)(2,1)}, u32[]{:S(2)}, u32[]{:S(2)}) collective-permute-start(bf16[1536,512]{1,0:T(8,128)(2,1)} %get-tuple-element.58), channel_id=1, source_target_pairs={{0,32},{32,0},{1,33},{33,1},{2,34},{34,2},{3,35},{35,3},{4,36},{36... | collective-permute-start | bytes 4718600 | tf_op jit(solution)/shard_map/ppermute | solution.py:240
  128.6 9.7 %collective-permute-start.5 = (bf16[512,384]{1,0:T(8,128)(2,1)S(1)}, bf16[512,384]{1,0:T(8,128)(2,1)S(1)}, u32[]{:S(2)}, u32[]{:S(2)}) collective-permute-start(bf16[512,384]{1,0:T(8,128)(2,1)S(1)} %shard_map.76.own), channel_id=1, source_target_pairs={{0,64},{64,128},{128,192},{192,0},{1,65},{65,129},{129,193},{193,1... | collective-permute-start | bytes 1179656 | tf_op jit(solution)/shard_map/ppermute | solution.py:188
  129.1 9.5 %collective-permute-start.6 = (bf16[512,384]{1,0:T(8,128)(2,1)S(1)}, bf16[512,384]{1,0:T(8,128)(2,1)S(1)}, u32[]{:S(2)}, u32[]{:S(2)}) collective-permute-start(bf16[512,384]{1,0:T(8,128)(2,1)S(1)} %shard_map.76.own), channel_id=1, source_target_pairs={{0,192},{64,0},{128,64},{192,128},{1,193},{65,1},{129,65},{193,129... | collective-permute-start | bytes 1179656 | tf_op jit(solution)/shard_map/ppermute | solution.py:188
  132.4 16.1 %collective-permute-start.10 = (bf16[256,1024]{1,0:T(8,128)(2,1)S(1)}, bf16[256,1024]{1,0:T(8,128)(2,1)S(1)}, u32[]{:S(2)}, u32[]{:S(2)}) collective-permute-start(bf16[256,1024]{1,0:T(8,128)(2,1)S(1)} %slice.21), channel_id=1, source_target_pairs={{0,192},{64,0},{128,64},{192,128},{1,193},{65,1},{129,65},{193,129... | collective-permute-start | bytes 1572872 | tf_op jit(solution)/shard_map/ppermute | solution.py:188
  133.6 15.9 %collective-permute-start.9 = (bf16[256,1024]{1,0:T(8,128)(2,1)S(1)}, bf16[256,1024]{1,0:T(8,128)(2,1)S(1)}, u32[]{:S(2)}, u32[]{:S(2)}) collective-permute-start(bf16[256,1024]{1,0:T(8,128)(2,1)S(1)} %slice.20), channel_id=1, source_target_pairs={{0,64},{64,128},{128,192},{192,0},{1,65},{65,129},{129,193},{193,1... | collective-permute-start | bytes 1572872 | tf_op jit(solution)/shard_map/ppermute | solution.py:188
  138.3 15.4 %collective-permute-start.7 = (bf16[256,384]{1,0:T(8,128)(2,1)S(1)}, bf16[256,384]{1,0:T(8,128)(2,1)S(1)}, u32[]{:S(2)}, u32[]{:S(2)}) collective-permute-start(bf16[256,384]{1,0:T(8,128)(2,1)S(1)} %slice.24), channel_id=1, source_target_pairs={{0,64},{64,128},{128,192},{192,0},{1,65},{65,129},{129,193},{193,1... | collective-permute-start | bytes 589832 | tf_op jit(solution)/shard_map/ppermute | solution.py:188
  138.6 15.1 %collective-permute-start.8 = (bf16[256,384]{1,0:T(8,128)(2,1)S(1)}, bf16[256,384]{1,0:T(8,128)(2,1)S(1)}, u32[]{:S(2)}, u32[]{:S(2)}) collective-permute-start(bf16[256,384]{1,0:T(8,128)(2,1)S(1)} %slice.25), channel_id=1, source_target_pairs={{0,192},{64,0},{128,64},{192,128},{1,193},{65,1},{129,65},{193,129... | collective-permute-start | bytes 589832 | tf_op jit(solution)/shard_map/ppermute | solution.py:188
  158.5 42.2 %all-to-all-start.2 = ((bf16[32,16,1024]{2,1,0:T(8,128)(2,1)}), bf16[32,16,1024]{2,1,0:T(8,128)(2,1)S(1)}, u32[]{:S(2)}, u32[]{:S(2)}) async-start(bf16[32,16,1024]{2,1,0:T(8,128)(2,1)} %bitcast.14), calls=%async_computation.2 | async-start | bytes 2097152 | tf_op jit(solution)/shard_map/all_to_all | solution.py:289
  180.0 9.8 %collective-permute-start.12 = (bf16[512,384]{1,0:T(8,128)(2,1)S(1)}, bf16[512,384]{1,0:T(8,128)(2,1)S(1)}, u32[]{:S(2)}, u32[]{:S(2)}) collective-permute-start(bf16[512,384]{1,0:T(8,128)(2,1)S(1)} %shard_map.79.own), channel_id=1, source_target_pairs={{0,64},{64,128},{128,192},{192,0},{1,65},{65,129},{129,193},{193,1... | collective-permute-start | bytes 1179656 | tf_op jit(solution)/shard_map/ppermute | solution.py:188
  180.1 9.8 %collective-permute-start.13 = (bf16[512,384]{1,0:T(8,128)(2,1)S(1)}, bf16[512,384]{1,0:T(8,128)(2,1)S(1)}, u32[]{:S(2)}, u32[]{:S(2)}) collective-permute-start(bf16[512,384]{1,0:T(8,128)(2,1)S(1)} %shard_map.79.own), channel_id=1, source_target_pairs={{0,192},{64,0},{128,64},{192,128},{1,193},{65,1},{129,65},{193,129... | collective-permute-start | bytes 1179656 | tf_op jit(solution)/shard_map/ppermute | solution.py:188
  189.9 6.1 %collective-permute-start.14 = (bf16[256,384]{1,0:T(8,128)(2,1)S(1)}, bf16[256,384]{1,0:T(8,128)(2,1)S(1)}, u32[]{:S(2)}, u32[]{:S(2)}) collective-permute-start(bf16[256,384]{1,0:T(8,128)(2,1)S(1)} %slice.26), channel_id=1, source_target_pairs={{0,64},{64,128},{128,192},{192,0},{1,65},{65,129},{129,193},{193,1... | collective-permute-start | bytes 589832 | tf_op jit(solution)/shard_map/ppermute | solution.py:188
  190.0 6.0 %collective-permute-start.15 = (bf16[256,384]{1,0:T(8,128)(2,1)S(1)}, bf16[256,384]{1,0:T(8,128)(2,1)S(1)}, u32[]{:S(2)}, u32[]{:S(2)}) collective-permute-start(bf16[256,384]{1,0:T(8,128)(2,1)S(1)} %slice.27), channel_id=1, source_target_pairs={{0,192},{64,0},{128,64},{192,128},{1,193},{65,1},{129,65},{193,129... | collective-permute-start | bytes 589832 | tf_op jit(solution)/shard_map/ppermute | solution.py:188
  200.7 28.5 %all-to-all-start.3 = ((bf16[32,16,1024]{2,1,0:T(8,128)(2,1)}), bf16[32,16,1024]{2,1,0:T(8,128)(2,1)S(1)}, u32[]{:S(2)}, u32[]{:S(2)}) async-start(bf16[32,16,1024]{2,1,0:T(8,128)(2,1)} %bitcast.26), calls=%async_computation.3 | async-start | bytes 2097152 | tf_op jit(solution)/shard_map/all_to_all | solution.py:289
  212.8 27.4 %collective-permute-start.11 = (bf16[128,512]{1,0:T(8,128)(2,1)S(1)}, bf16[128,512]{1,0:T(8,128)(2,1)S(1)}, u32[]{:S(2)}, u32[]{:S(2)}) collective-permute-start(bf16[128,512]{1,0:T(8,128)(2,1)S(1)} %get-tuple-element.74), channel_id=1, source_target_pairs={{0,32},{32,0},{1,33},{33,1},{2,34},{34,2},{3,35},{35,3},{4,36},{36... | collective-permute-start | bytes 393224 | tf_op jit(solution)/shard_map/ppermute | solution.py:302
  230.1 11.0 %collective-permute-start.16 = (bf16[128,512]{1,0:T(8,128)(2,1)S(1)}, bf16[128,512]{1,0:T(8,128)(2,1)S(1)}, u32[]{:S(2)}, u32[]{:S(2)}) collective-permute-start(bf16[128,512]{1,0:T(8,128)(2,1)S(1)} %get-tuple-element.92), channel_id=1, source_target_pairs={{0,32},{32,0},{1,33},{33,1},{2,34},{34,2},{3,35},{35,3},{4,36},{36... | collective-permute-start | bytes 393224 | tf_op jit(solution)/shard_map/ppermute | solution.py:302
  (13 other events, 88.6 us)
Sparse Core Ops, SparseCore 0:
  48.3 64.0 all-gather.2

commit v8 on v5

--- a/solution.py
+++ b/solution.py
@@ -114,22 +114,30 @@
         out[...] = jnp.transpose(spread(place, dense, first, size)).astype(BF16)
 
 
+def activate(pos, sums):
+    units = sums.shape[0] // 4
+    gate_own, up_own, gate_other, up_other = [
+        sums[index * units : (index + 1) * units] for index in range(4)
+    ]
+    own = gate_own / (1.0 + jnp.exp(-gate_own)) * up_own
+    other = gate_other / (1.0 + jnp.exp(-gate_other)) * up_other
+    low = jnp.where(pos[1] == 0, own, other)
+    high = jnp.where(pos[1] == 0, other, own)
+    return jnp.transpose(jnp.concatenate([low, high], axis=0)).astype(BF16)
+
+
 def hidden_kernel(half, pos, blocks, gate_own, gate_other, up_own, up_other, out):
     quarter = blocks.shape[2]
     rows = slice(half * PIECE, (half + 1) * PIECE)
-    sums = [None] * 4
+    total = None
     for y in range(NY):
-        block = blocks[y, rows, :]
         cols = slice(y * quarter, (y + 1) * quarter)
-        for which, weight in enumerate((gate_own, up_own, gate_other, up_other)):
-            term = by_rows(weight[:, cols], block)
-            sums[which] = term if y == 0 else sums[which] + term
-    own, other = [
-        gate / (1.0 + jnp.exp(-gate)) * up for gate, up in (sums[0:2], sums[2:4])
-    ]
-    low = jnp.where(pos[1] == 0, own, other)
-    high = jnp.where(pos[1] == 0, other, own)
-    out[...] = jnp.transpose(jnp.concatenate([low, high], axis=0)).astype(BF16)
+        weights = jnp.concatenate(
+            [weight[:, cols] for weight in (gate_own, up_own, gate_other, up_other)], axis=0
+        )
+        term = by_rows(weights, blocks[y, rows, :])
+        total = term if y == 0 else total + term
+    out[...] = activate(pos, total)
 
 
 def store_columns(pos, out, at, own, other):
@@ -258,7 +266,7 @@
                 out_shape=sds((PIECE, units), BF16),
                 in_specs=[SMEM] + [VMEM] * 5,
                 out_specs=VMEM,
-                compiler_params=params(24),
+                compiler_params=params(16),
                 cost_estimate=cost(
                     4 * PIECE * width * units, 4 * units * width + 2 * PIECE * width
                 ),
@@ -272,7 +280,7 @@
             out_shape=sds((size, NC * cols), BF16),
             in_specs=[SMEM] + [VMEM] * (2 + len(pieces)),
             out_specs=VMEM,
-            compiler_params=params(24),
+            compiler_params=params(16),
             cost_estimate=cost(
                 2 * size * ff * NC * cols, 2 * ff * NC * cols + 2 * size * NC * cols
             ),

time: 241 us -> 237 us (0.983)
  Pallas kernels: 36.9 us -> 32.7 us
    pallas_call x4, Pallas kernels: 20 us -> 15.7 us  [body(): pl.pallas_call(functools.partial(hidden_kernel, half), out_shape=sds((PIE...]
  transfers between devices with their start and end apart: 20 -> 20, of which waited for: 6 -> 8; matrix products, arithmetic and copies ran while one was open for 3% -> 3% of each run, Pallas kernels for 15% -> 13%
where the time goes in v8:
time: 237 us; the launch traced here: 236 us
  blocking collectives  84.3 us (36%)
  starting transfers between devices  67.2 us (28%)
  Pallas kernels  32.7 us (14%)
  local copies, waits for them, and re-layouts  20.6 us (9%)
  waiting for transfers between devices  16.9 us (7%)
  between operations  13.4 us (6%)
    all_to_all x1, blocking collectives, body(): received.append(lax.all_to_all(rows, ('x', 'z'), 0, 0, tiled=True))  32.3 us
    all_gather x2, blocking collectives, body(): pieces.append(lax.all_gather(hidden, 'y', axis=0))  29.6 us
    all_to_all x1, blocking collectives, body(): returned.append(lax.all_to_all(result, ('x', 'z'), 0, 0, tiled=True))  22.4 us
    all_to_all x2, starting transfers between devices, body(): returned.append(lax.all_to_all(result, ('x', 'z'), 0, 0, tiled=True))  17.9 us
    pallas_call x4, Pallas kernels, body(): pl.pallas_call(functools.partial(hidden_kernel, half), out_shape=sds((PIE...  15.7 us
    ppermute x2, starting transfers between devices, body(): give = lax.ppermute(give, 'c', [(0, 1), (1, 0)])  14.3 us
    unnamed x36, local copies, waits for them, and re-layouts  13.9 us
    all_to_all x1, starting transfers between devices, body(): received = [lax.all_to_all(first_rows, ('x', 'z'), 0, 0, tiled=True)]  12 us
  transfers between devices with their start and end apart: 20, of which 8 were waited for; matrix products, arithmetic and copies ran while one was open for 3% of the time, Pallas kernels for 13%

profile of v8, /device:TPU:1, one launch (start us, length us, event | category | flops | bytes accessed | tf_op | source)
XLA Modules:
  0.0 235.8 jit_solution(8109705178801005450)
XLA Ops:
  11.2 12.0 %all-to-all-start = ((bf16[32,8,1024]{2,1,0:T(8,128)(2,1)}), bf16[32,8,1024]{2,1,0:T(8,128)(2,1)}, u32[]{:S(2)}, u32[]{:S(2)}) async-start(bf16[32,8,1024]{2,1,0:T(8,128)(2,1)} %bitcast.9), calls=%async_computation | async-start | bytes 1048576 | tf_op jit(solution)/shard_map/all_to_all | solution.py:222
  26.4 3.9 %dynamic-slice_bitcast_fusion = (bf16[1536,512]{1,0:T(8,128)(2,1)}, bf16[1536,512]{1,0:T(8,128)(2,1)}) fusion(bf16[2,1536,512]{2,1,0:T(8,128)(2,1)} %param.13, s32[]{:T(128)S(6)} %select_n.13, s32[]{:T(128)S(6)} %select_n.12), kind=kLoop, calls=%fused_computation | loop fusion | bytes 6291464 | tf_op jit(solution)/shard_map/jit(dynamic_index_in_dim)/squeeze | solution.py:233
  33.4 4.1 %all-to-all-done = bf16[32,8,1024]{2,1,0:T(8,128)(2,1)} async-done(((bf16[32,8,1024]{2,1,0:T(8,128)(2,1)}), bf16[32,8,1024]{2,1,0:T(8,128)(2,1)}, u32[]{:S(2)}, u32[]{:S(2)}) %all-to-all-start) | async-done | bytes 524320 | tf_op jit(solution)/shard_map/all_to_all | solution.py:222
  37.5 32.3 %all_to_all.70 = bf16[32,16,1024]{2,1,0:T(8,128)(2,1)} all-to-all(bf16[32,16,1024]{2,1,0:T(8,128)(2,1)} %bitcast.41), channel_id=1, replica_groups=mesh['y'=4,'c'=2,'x'=4,'z'=8] {'x','z'}, dimensions={0} | all-to-all | bytes 2097152 | tf_op jit(solution)/shard_map/all_to_all | solution.py:241
  71.2 3.9 %collective-permute-start.1 = (bf16[192,4096]{1,0:T(8,128)(2,1)}, bf16[192,4096]{1,0:T(8,128)(2,1)}, u32[]{:S(2)}, u32[]{:S(2)}) collective-permute-start(bf16[192,4096]{1,0:T(8,128)(2,1)} %get-tuple-element.54), channel_id=1, source_target_pairs={{0,32},{32,0},{1,33},{33,1},{2,34},{34,2},{3,35},{35,3},{4,36},{36... | collective-permute-start | bytes 4718600 | tf_op jit(solution)/shard_map/ppermute | solution.py:238
  75.6 6.6 %all-to-all-start.2 = ((bf16[32,8,1024]{2,1,0:T(8,128)(2,1)}), bf16[32,8,1024]{2,1,0:T(8,128)(2,1)}, u32[]{:S(2)}, u32[]{:S(2)}) async-start(bf16[32,8,1024]{2,1,0:T(8,128)(2,1)} %bitcast.43), calls=%async_computation.2 | async-start | bytes 1048576 | tf_op jit(solution)/shard_map/all_to_all | solution.py:241
  83.8 4.2 %shard_map.76 = bf16[256,384]{1,0:T(8,128)(2,1)S(1)} custom-call(s32[2]{0:T(128)S(1)} %pad_add_fusion.pos, bf16[4,256,1024]{2,1,0:T(8,128)(2,1)S(1)} %bitcast.40, bf16[192,4096]{1,0:T(8,128)(2,1)S(1)} %get-tuple-element.53.gate_own, bf16[192,4096]{1,0:T(8,128)(2,1)} %collective-permute-done.1.gate_other, bf16[192,4096]{1,0:T(8,128)(2,1)S(1)} %get-tuple-element.55.up_own, ...), custom_call_target="tpu_custom_call" | custom-call | flops 1610612736 | bytes 8388608 | tf_op jit(solution)/shard_map/pallas_call | solution.py:264
  88.0 17.0 %all-gather.2 = bf16[1024,384]{1,0:T(8,128)(2,1)S(1)} all-gather(bf16[256,384]{1,0:T(8,128)(2,1)S(1)} %shard_map.76), channel_id=4, replica_groups=mesh['y'=4,'c'=2,'x'=4,'z'=8] {'y'}, dimensions={0}, use_global_device_ids=true | all-gather | bytes 983040 | tf_op jit(solution)/shard_map/all_gather | solution.py:277
  105.1 2.7 %shard_map.77 = bf16[256,1024]{1,0:T(8,128)(2,1)S(1)} custom-call(s32[2]{0:T(128)S(1)} %pad_add_fusion.pos, bf16[1536,512]{1,0:T(8,128)(2,1)S(1)} %copy-done.1, bf16[1536,512]{1,0:T(8,128)(2,1)} %collective-permute-done.down_other, bf16[4,256,384]{2,1,0:T(8,128)(2,1)S(1)} %bitcast.34), custom_call_target="tpu_custom_call" | custom-call | flops 805306368 | bytes 3670016 | tf_op jit(solution)/shard_map/pallas_call | solution.py:278
  108.5 22.4 %all_to_all.71 = bf16[32,8,1024]{2,1,0:T(8,128)(2,1)} all-to-all(bf16[32,8,1024]{2,1,0:T(8,128)(2,1)} %bitcast.36), channel_id=1, replica_groups=mesh['y'=4,'c'=2,'x'=4,'z'=8] {'x','z'}, dimensions={0} | all-to-all | bytes 1048576 | tf_op jit(solution)/shard_map/all_to_all | solution.py:291
  133.1 3.8 %shard_map.78.refs_0_ = bf16[256,384]{1,0:T(8,128)(2,1)S(1)} custom-call(s32[2]{0:T(128)S(1)} %pad_add_fusion.pos, bf16[4,512,1024]{2,1,0:T(8,128)(2,1)S(1)} %bitcast.32, bf16[192,4096]{1,0:T(8,128)(2,1)S(1)} %get-tuple-element.53.gate_own, bf16[192,4096]{1,0:T(8,128)(2,1)} %collective-permute-done.1.gate_other, ...), custom_call_target="tpu_custom_call" | custom-call | flops 1610612736 | bytes 8388608 | tf_op jit(solution)/shard_map/pallas_call | solution.py:264
  139.7 3.8 %shard_map.79.refs_5_ = bf16[256,384]{1,0:T(8,128)(2,1)S(1)} custom-call(s32[2]{0:T(128)S(1)} %pad_add_fusion.pos, bf16[4,512,1024]{2,1,0:T(8,128)(2,1)S(1)} %bitcast.33, bf16[192,4096]{1,0:T(8,128)(2,1)S(1)} %get-tuple-element.53.gate_own, bf16[192,4096]{1,0:T(8,128)(2,1)} %collective-permute-done.1.gate_other, ...), custom_call_target="tpu_custom_call" | custom-call | flops 1610612736 | bytes 8388608 | tf_op jit(solution)/shard_map/pallas_call | solution.py:264
  146.4 2.7 %collective-permute-start.6 = (bf16[128,384]{1,0:T(8,128)(2,1)S(1)}, bf16[128,384]{1,0:T(8,128)(2,1)S(1)}, u32[]{:S(2)}, u32[]{:S(2)}) collective-permute-start(bf16[128,384]{1,0:T(8,128)(2,1)S(1)} %slice.17), channel_id=1, source_target_pairs={{0,192},{64,0},{128,64},{192,128},{1,193},{65,1},{129,65},{193,129... | collective-permute-start | bytes 294920 | tf_op jit(solution)/shard_map/ppermute | solution.py:192
  149.1 4.4 %collective-permute-done.7.refs_6_ = bf16[256,384]{1,0:T(8,128)(2,1)S(1)} collective-permute-done((bf16[256,384]{1,0:T(8,128)(2,1)S(1)}, bf16[256,384]{1,0:T(8,128)(2,1)S(1)}, u32[]{:S(2)}, u32[]{:S(2)}) %collective-permute-start.7) | collective-permute-done | bytes 196640 | tf_op jit(solution)/shard_map/ppermute | solution.py:192
  154.8 3.6 %collective-permute-start.10 = (bf16[128,384]{1,0:T(8,128)(2,1)S(1)}, bf16[128,384]{1,0:T(8,128)(2,1)S(1)}, u32[]{:S(2)}, u32[]{:S(2)}) collective-permute-start(bf16[128,384]{1,0:T(8,128)(2,1)S(1)} %slice.19), channel_id=1, source_target_pairs={{0,192},{64,0},{128,64},{192,128},{1,193},{65,1},{129,65},{193,129... | collective-permute-start | bytes 294920 | tf_op jit(solution)/shard_map/ppermute | solution.py:192
  159.0 2.8 %collective-permute-done.9.refs_8_ = bf16[128,384]{1,0:T(8,128)(2,1)S(1)} collective-permute-done((bf16[128,384]{1,0:T(8,128)(2,1)S(1)}, bf16[128,384]{1,0:T(8,128)(2,1)S(1)}, u32[]{:S(2)}, u32[]{:S(2)}) %collective-permute-start.9) | collective-permute-done | bytes 98336 | tf_op jit(solution)/shard_map/ppermute | solution.py:192
  163.2 3.7 %shard_map.80 = bf16[512,1024]{1,0:T(8,128)(2,1)S(1)} custom-call(s32[2]{0:T(128)S(1)} %pad_add_fusion.pos, bf16[1536,512]{1,0:T(8,128)(2,1)S(1)} %copy-done.2, bf16[1536,512]{1,0:T(8,128)(2,1)} %collective-permute-done.down_other, bf16[256,384]{1,0:T(8,128)(2,1)S(1)} %shard_map.78.refs_0_, bf16[256,384]{1,0:T(8,128)(2,1)S(1)} %collective-permute-done.3.refs_1_, ...), custom_call_target="tpu_custom_call" | custom-call | flops 1610612736 | bytes 4194304 | tf_op jit(solution)/shard_map/pallas_call | solution.py:278
  168.0 8.2 %all-to-all-start.4 = ((bf16[32,16,1024]{2,1,0:T(8,128)(2,1)}), bf16[32,16,1024]{2,1,0:T(8,128)(2,1)}, u32[]{:S(2)}, u32[]{:S(2)}) async-start(bf16[32,16,1024]{2,1,0:T(8,128)(2,1)} %bitcast.42), calls=%async_computation.4 | async-start | bytes 2097152 | tf_op jit(solution)/shard_map/all_to_all | solution.py:291
  177.8 3.9 %shard_map.82 = bf16[256,384]{1,0:T(8,128)(2,1)S(1)} custom-call(s32[2]{0:T(128)S(1)} %pad_add_fusion.pos, bf16[4,256,1024]{2,1,0:T(8,128)(2,1)S(1)} %bitcast.39, bf16[192,4096]{1,0:T(8,128)(2,1)S(1)} %get-tuple-element.53.gate_own, bf16[192,4096]{1,0:T(8,128)(2,1)} %collective-permute-done.1.gate_other, bf16[192,4096]{1,0:T(8,128)(2,1)S(1)} %get-tuple-element.55.up_own, ...), custom_call_target="tpu_custom_call" | custom-call | flops 1610612736 | bytes 8388608 | tf_op jit(solution)/shard_map/pallas_call | solution.py:264
  181.7 12.6 %all-gather.4 = bf16[1024,384]{1,0:T(8,128)(2,1)S(1)} all-gather(bf16[256,384]{1,0:T(8,128)(2,1)S(1)} %shard_map.82), channel_id=6, replica_groups=mesh['y'=4,'c'=2,'x'=4,'z'=8] {'y'}, dimensions={0}, use_global_device_ids=true | all-gather | bytes 983040 | tf_op jit(solution)/shard_map/all_gather | solution.py:277
  194.3 3.5 %shard_map.83 = bf16[256,1024]{1,0:T(8,128)(2,1)} custom-call(s32[2]{0:T(128)S(1)} %pad_add_fusion.pos, bf16[1536,512]{1,0:T(8,128)(2,1)S(1)} %copy-done.3, bf16[1536,512]{1,0:T(8,128)(2,1)} %collective-permute-done.down_other, bf16[4,256,384]{2,1,0:T(8,128)(2,1)S(1)} %bitcast.35), custom_call_target="tpu_custom_call" | custom-call | flops 805306368 | bytes 3670016 | tf_op jit(solution)/shard_map/pallas_call | solution.py:278
  197.8 9.7 %all-to-all-start.5 = ((bf16[32,8,1024]{2,1,0:T(8,128)(2,1)}), bf16[32,8,1024]{2,1,0:T(8,128)(2,1)S(1)}, u32[]{:S(2)}, u32[]{:S(2)}) async-start(bf16[32,8,1024]{2,1,0:T(8,128)(2,1)} %bitcast.24), calls=%async_computation.5 | async-start | bytes 1048576 | tf_op jit(solution)/shard_map/all_to_all | solution.py:291
  212.5 6.4 %collective-permute-start.11 = (bf16[128,512]{1,0:T(8,128)(2,1)S(1)}, bf16[128,512]{1,0:T(8,128)(2,1)S(1)}, u32[]{:S(2)}, u32[]{:S(2)}) collective-permute-start(bf16[128,512]{1,0:T(8,128)(2,1)S(1)} %get-tuple-element.63), channel_id=1, source_target_pairs={{0,32},{32,0},{1,33},{33,1},{2,34},{34,2},{3,35},{35,3},{4,36},{36... | collective-permute-start | bytes 393224 | tf_op jit(solution)/shard_map/ppermute | solution.py:304
  219.7 7.8 %collective-permute-start.12 = (bf16[128,512]{1,0:T(8,128)(2,1)S(1)}, bf16[128,512]{1,0:T(8,128)(2,1)S(1)}, u32[]{:S(2)}, u32[]{:S(2)}) collective-permute-start(bf16[128,512]{1,0:T(8,128)(2,1)S(1)} %get-tuple-element.68), channel_id=1, source_target_pairs={{0,32},{32,0},{1,33},{33,1},{2,34},{34,2},{3,35},{35,3},{4,36},{36... | collective-permute-start | bytes 393224 | tf_op jit(solution)/shard_map/ppermute | solution.py:304
  (80 shorter events, 36.4 us)
Async XLA Ops:
  11.2 26.3 %all-to-all-start = ((bf16[32,8,1024]{2,1,0:T(8,128)(2,1)}), bf16[32,8,1024]{2,1,0:T(8,128)(2,1)}, u32[]{:S(2)}, u32[]{:S(2)}) async-start(bf16[32,8,1024]{2,1,0:T(8,128)(2,1)} %bitcast.9), calls=%async_computation | async-start | bytes 1048576 | tf_op jit(solution)/shard_map/all_to_all | solution.py:222
  23.2 48.0 %all-gather.9.cloned.1.call-start = ((), (), s32[]{:S(2)}) async-start(), calls=%async_computation.6 | async-start | bytes 2621440 | tf_op jit(solution)/shard_map/all_gather | solution.py:259
  37.5 93.4 %all-gather.11.cloned.1.call-start = ((), (), s32[]{:S(2)}) async-start(), calls=%async_computation.7 | async-start | bytes 5242880 | tf_op jit(solution)/shard_map/all_gather | solution.py:259
  71.2 11.0 %collective-permute-start.1 = (bf16[192,4096]{1,0:T(8,128)(2,1)}, bf16[192,4096]{1,0:T(8,128)(2,1)}, u32[]{:S(2)}, u32[]{:S(2)}) collective-permute-start(bf16[192,4096]{1,0:T(8,128)(2,1)} %get-tuple-element.54), channel_id=1, source_target_pairs={{0,32},{32,0},{1,33},{33,1},{2,34},{34,2},{3,35},{35,3},{4,36},{36... | collective-permute-start | bytes 4718600 | tf_op jit(solution)/shard_map/ppermute | solution.py:238
  75.0 7.2 %collective-permute-start.2 = (bf16[192,4096]{1,0:T(8,128)(2,1)}, bf16[192,4096]{1,0:T(8,128)(2,1)}, u32[]{:S(2)}, u32[]{:S(2)}) collective-permute-start(bf16[192,4096]{1,0:T(8,128)(2,1)} %get-tuple-element.56), channel_id=1, source_target_pairs={{0,32},{32,0},{1,33},{33,1},{2,34},{34,2},{3,35},{35,3},{4,36},{36... | collective-permute-start | bytes 4718600 | tf_op jit(solution)/shard_map/ppermute | solution.py:238
  75.1 29.9 %collective-permute-start = (bf16[1536,512]{1,0:T(8,128)(2,1)}, bf16[1536,512]{1,0:T(8,128)(2,1)}, u32[]{:S(2)}, u32[]{:S(2)}) collective-permute-start(bf16[1536,512]{1,0:T(8,128)(2,1)} %get-tuple-element.52), channel_id=1, source_target_pairs={{0,32},{32,0},{1,33},{33,1},{2,34},{34,2},{3,35},{35,3},{4,36},{36... | collective-permute-start | bytes 4718600 | tf_op jit(solution)/shard_map/ppermute | solution.py:238
  75.6 33.0 %all-to-all-start.2 = ((bf16[32,8,1024]{2,1,0:T(8,128)(2,1)}), bf16[32,8,1024]{2,1,0:T(8,128)(2,1)}, u32[]{:S(2)}, u32[]{:S(2)}) async-start(bf16[32,8,1024]{2,1,0:T(8,128)(2,1)} %bitcast.43), calls=%async_computation.2 | async-start | bytes 1048576 | tf_op jit(solution)/shard_map/all_to_all | solution.py:241
  82.2 94.0 %all-gather.13.cloned.1.call-start = ((), (), s32[]{:S(2)}) async-start(), calls=%async_computation.8 | async-start | bytes 2621440 | tf_op jit(solution)/shard_map/all_gather | solution.py:259
  83.8 21.2 %copy-start.1 = (bf16[1536,512]{1,0:T(8,128)(2,1)S(1)}, bf16[1536,512]{1,0:T(8,128)(2,1)}, u32[]{:S(2)}) copy-start(bf16[1536,512]{1,0:T(8,128)(2,1)} %get-tuple-element.51.down_own) | copy-start | bytes 4718596
  137.0 26.3 %copy-start.2 = (bf16[1536,512]{1,0:T(8,128)(2,1)S(1)}, bf16[1536,512]{1,0:T(8,128)(2,1)}, u32[]{:S(2)}) copy-start(bf16[1536,512]{1,0:T(8,128)(2,1)} %get-tuple-element.51.down_own) | copy-start | bytes 4718596
  137.0 9.3 %collective-permute-start.3 = (bf16[256,384]{1,0:T(8,128)(2,1)S(1)}, bf16[256,384]{1,0:T(8,128)(2,1)S(1)}, u32[]{:S(2)}, u32[]{:S(2)}) collective-permute-start(bf16[256,384]{1,0:T(8,128)(2,1)S(1)} %shard_map.78.refs_0_), channel_id=1, source_target_pairs={{0,64},{64,128},{128,192},{192,0},{1,65},{65,129},{129,193},{193,1... | collective-permute-start | bytes 589832 | tf_op jit(solution)/shard_map/ppermute | solution.py:192
  137.1 9.3 %collective-permute-start.4 = (bf16[256,384]{1,0:T(8,128)(2,1)S(1)}, bf16[256,384]{1,0:T(8,128)(2,1)S(1)}, u32[]{:S(2)}, u32[]{:S(2)}) collective-permute-start(bf16[256,384]{1,0:T(8,128)(2,1)S(1)} %shard_map.78.refs_0_), channel_id=1, source_target_pairs={{0,192},{64,0},{128,64},{192,128},{1,193},{65,1},{129,65},{193,129... | collective-permute-start | bytes 589832 | tf_op jit(solution)/shard_map/ppermute | solution.py:192
  143.5 10.0 %collective-permute-start.7 = (bf16[256,384]{1,0:T(8,128)(2,1)S(1)}, bf16[256,384]{1,0:T(8,128)(2,1)S(1)}, u32[]{:S(2)}, u32[]{:S(2)}) collective-permute-start(bf16[256,384]{1,0:T(8,128)(2,1)S(1)} %shard_map.79.refs_5_), channel_id=1, source_target_pairs={{0,64},{64,128},{128,192},{192,0},{1,65},{65,129},{129,193},{193,1... | collective-permute-start | bytes 589832 | tf_op jit(solution)/shard_map/ppermute | solution.py:192
  143.6 11.2 %collective-permute-start.8 = (bf16[256,384]{1,0:T(8,128)(2,1)S(1)}, bf16[256,384]{1,0:T(8,128)(2,1)S(1)}, u32[]{:S(2)}, u32[]{:S(2)}) collective-permute-start(bf16[256,384]{1,0:T(8,128)(2,1)S(1)} %shard_map.79.refs_5_), channel_id=1, source_target_pairs={{0,192},{64,0},{128,64},{192,128},{1,193},{65,1},{129,65},{193,129... | collective-permute-start | bytes 589832 | tf_op jit(solution)/shard_map/ppermute | solution.py:192
  146.3 12.1 %collective-permute-start.5 = (bf16[128,384]{1,0:T(8,128)(2,1)S(1)}, bf16[128,384]{1,0:T(8,128)(2,1)S(1)}, u32[]{:S(2)}, u32[]{:S(2)}) collective-permute-start(bf16[128,384]{1,0:T(8,128)(2,1)S(1)} %slice.16), channel_id=1, source_target_pairs={{0,64},{64,128},{128,192},{192,0},{1,65},{65,129},{129,193},{193,1... | collective-permute-start | bytes 294920 | tf_op jit(solution)/shard_map/ppermute | solution.py:192
  146.4 12.6 %collective-permute-start.6 = (bf16[128,384]{1,0:T(8,128)(2,1)S(1)}, bf16[128,384]{1,0:T(8,128)(2,1)S(1)}, u32[]{:S(2)}, u32[]{:S(2)}) collective-permute-start(bf16[128,384]{1,0:T(8,128)(2,1)S(1)} %slice.17), channel_id=1, source_target_pairs={{0,192},{64,0},{128,64},{192,128},{1,193},{65,1},{129,65},{193,129... | collective-permute-start | bytes 294920 | tf_op jit(solution)/shard_map/ppermute | solution.py:192
  153.5 8.3 %collective-permute-start.9 = (bf16[128,384]{1,0:T(8,128)(2,1)S(1)}, bf16[128,384]{1,0:T(8,128)(2,1)S(1)}, u32[]{:S(2)}, u32[]{:S(2)}) collective-permute-start(bf16[128,384]{1,0:T(8,128)(2,1)S(1)} %slice.18), channel_id=1, source_target_pairs={{0,64},{64,128},{128,192},{192,0},{1,65},{65,129},{129,193},{193,1... | collective-permute-start | bytes 294920 | tf_op jit(solution)/shard_map/ppermute | solution.py:192
  154.8 8.4 %collective-permute-start.10 = (bf16[128,384]{1,0:T(8,128)(2,1)S(1)}, bf16[128,384]{1,0:T(8,128)(2,1)S(1)}, u32[]{:S(2)}, u32[]{:S(2)}) collective-permute-start(bf16[128,384]{1,0:T(8,128)(2,1)S(1)} %slice.19), channel_id=1, source_target_pairs={{0,192},{64,0},{128,64},{192,128},{1,193},{65,1},{129,65},{193,129... | collective-permute-start | bytes 294920 | tf_op jit(solution)/shard_map/ppermute | solution.py:192
  168.0 29.8 %all-to-all-start.4 = ((bf16[32,16,1024]{2,1,0:T(8,128)(2,1)}), bf16[32,16,1024]{2,1,0:T(8,128)(2,1)}, u32[]{:S(2)}, u32[]{:S(2)}) async-start(bf16[32,16,1024]{2,1,0:T(8,128)(2,1)} %bitcast.42), calls=%async_computation.4 | async-start | bytes 2097152 | tf_op jit(solution)/shard_map/all_to_all | solution.py:291
  177.8 16.5 %copy-start.3 = (bf16[1536,512]{1,0:T(8,128)(2,1)S(1)}, bf16[1536,512]{1,0:T(8,128)(2,1)}, u32[]{:S(2)}) copy-start(bf16[1536,512]{1,0:T(8,128)(2,1)} %get-tuple-element.51.down_own) | copy-start | bytes 4718596
  194.3 13.2 %copy-start.15 = (s32[128,8]{0,1:T(8,128)S(1)}, s32[128,8]{0,1:T(8,128)}, u32[]{:S(2)}) copy-start(s32[128,8]{0,1:T(8,128)} %param.10) | copy-start | bytes 12292
  197.8 21.2 %all-to-all-start.5 = ((bf16[32,8,1024]{2,1,0:T(8,128)(2,1)}), bf16[32,8,1024]{2,1,0:T(8,128)(2,1)S(1)}, u32[]{:S(2)}, u32[]{:S(2)}) async-start(bf16[32,8,1024]{2,1,0:T(8,128)(2,1)} %bitcast.24), calls=%async_computation.5 | async-start | bytes 1048576 | tf_op jit(solution)/shard_map/all_to_all | solution.py:291
  212.5 15.0 %collective-permute-start.11 = (bf16[128,512]{1,0:T(8,128)(2,1)S(1)}, bf16[128,512]{1,0:T(8,128)(2,1)S(1)}, u32[]{:S(2)}, u32[]{:S(2)}) collective-permute-start(bf16[128,512]{1,0:T(8,128)(2,1)S(1)} %get-tuple-element.63), channel_id=1, source_target_pairs={{0,32},{32,0},{1,33},{33,1},{2,34},{34,2},{3,35},{35,3},{4,36},{36... | collective-permute-start | bytes 393224 | tf_op jit(solution)/shard_map/ppermute | solution.py:304
  219.7 8.8 %collective-permute-start.12 = (bf16[128,512]{1,0:T(8,128)(2,1)S(1)}, bf16[128,512]{1,0:T(8,128)(2,1)S(1)}, u32[]{:S(2)}, u32[]{:S(2)}) collective-permute-start(bf16[128,512]{1,0:T(8,128)(2,1)S(1)} %get-tuple-element.68), channel_id=1, source_target_pairs={{0,32},{32,0},{1,33},{33,1},{2,34},{34,2},{3,35},{35,3},{4,36},{36... | collective-permute-start | bytes 393224 | tf_op jit(solution)/shard_map/ppermute | solution.py:304
  (14 other events, 31.5 us)
Sparse Core Ops, SparseCore 0:
  37.6 33.5 all-gather.8
  73.0 57.1 all-gather.10
  132.0 42.0 all-gather.12

commit v9 on v8

--- a/solution.py
+++ b/solution.py
@@ -126,18 +126,30 @@
     return jnp.transpose(jnp.concatenate([low, high], axis=0)).astype(BF16)
 
 
-def hidden_kernel(half, pos, blocks, gate_own, gate_other, up_own, up_other, out):
+def hidden_kernel(
+    half, pos, blocks, gate_own, up_own, gate_other, up_other, out, gate_held, up_held, sems
+):
+    fetches = [
+        pltpu.make_async_copy(gate_other, gate_held, sems.at[0]),
+        pltpu.make_async_copy(up_other, up_held, sems.at[1]),
+    ]
+    for fetch in fetches:
+        fetch.start()
     quarter = blocks.shape[2]
     rows = slice(half * PIECE, (half + 1) * PIECE)
-    total = None
-    for y in range(NY):
-        cols = slice(y * quarter, (y + 1) * quarter)
-        weights = jnp.concatenate(
-            [weight[:, cols] for weight in (gate_own, up_own, gate_other, up_other)], axis=0
-        )
-        term = by_rows(weights, blocks[y, rows, :])
-        total = term if y == 0 else total + term
-    out[...] = activate(pos, total)
+    totals = []
+    for pair in ((gate_own, up_own), (gate_held, up_held)):
+        if totals:
+            for fetch in fetches:
+                fetch.wait()
+        total = None
+        for y in range(NY):
+            cols = slice(y * quarter, (y + 1) * quarter)
+            weights = jnp.concatenate([weight[:, cols] for weight in pair], axis=0)
+            term = by_rows(weights, blocks[y, rows, :])
+            total = term if y == 0 else total + term
+        totals.append(total)
+    out[...] = activate(pos, jnp.concatenate(totals, axis=0))
 
 
 def store_columns(pos, out, at, own, other):
@@ -257,26 +269,28 @@
             before = [done[i][j] for i, j in ((index - 1, 0), (index - 2, 1)) if i >= 0]
             mine, *before = lax.optimization_barrier((mine, *before))
         blocks = lax.all_gather(mine, "y", axis=0)
-        if index == 1:
-            blocks, returned[0] = lax.optimization_barrier((blocks, returned[0]))
         pieces = []
         for half in range(size // PIECE):
+            if index == 1 and half == 0:
+                blocks, returned[0] = lax.optimization_barrier((blocks, returned[0]))
             hidden = pl.pallas_call(
                 functools.partial(hidden_kernel, half),
                 out_shape=sds((PIECE, units), BF16),
-                in_specs=[SMEM] + [VMEM] * 5,
+                in_specs=[SMEM] + [VMEM] * 3 + [pl.BlockSpec(memory_space=pl.ANY)] * 2,
                 out_specs=VMEM,
+                scratch_shapes=[pltpu.VMEM((units // 2, width), BF16)] * 2
+                + [pltpu.SemaphoreType.DMA((2,))],
                 compiler_params=params(16),
                 cost_estimate=cost(
                     4 * PIECE * width * units, 4 * units * width + 2 * PIECE * width
                 ),
-            )(pos, blocks, own[0], others[0], own[1], others[1])
-            if size > PIECE:
+            )(pos, blocks, own[0], own[1], others[0], others[1])
+            if index:
                 pieces.extend(ring(hidden))
             else:
                 pieces.append(lax.all_gather(hidden, "y", axis=0))
         result = pl.pallas_call(
-            down_ring_kernel if size > PIECE else down_kernel,
+            down_ring_kernel if index else down_kernel,
             out_shape=sds((size, NC * cols), BF16),
             in_specs=[SMEM] + [VMEM] * (2 + len(pieces)),
             out_specs=VMEM,

time: 237 us -> 245 us (1.034)
  blocking collectives: 84.3 us -> 72.3 us
  Pallas kernels: 32.7 us -> 40.6 us
  waiting for transfers between devices: 16.9 us -> 24.7 us
  starting transfers between devices: 67.2 us -> 71.3 us
    all_gather x2 -> x1, blocking collectives: 29.6 us -> 17 us  [body(): pieces.append(lax.all_gather(hidden, 'y', axis=0))]
    pallas_call x4, Pallas kernels: 15.7 us -> 23.7 us  [body(): pl.pallas_call(functools.partial(hidden_kernel, half), out_shape=sds((PIE...]
    ppermute x8 -> x12, waiting for transfers between devices: 10.4 us -> 17.4 us  [turn(): return lax.ppermute(array, 'y', [(i, (i + step) % NY) for i in range(NY)])]
    ppermute x8 -> x12, starting transfers between devices: 12 us -> 16.9 us  [turn(): return lax.ppermute(array, 'y', [(i, (i + step) % NY) for i in range(NY)])]
  transfers between devices with their start and end apart: 20 -> 24, of which waited for: 8 -> 9; matrix products, arithmetic and copies ran while one was open for 3% -> 2% of each run, Pallas kernels for 13% -> 16%
where the time goes in v9:
time: 245 us; the launch traced here: 244 us
  blocking collectives  72.3 us (30%)
  starting transfers between devices  71.3 us (29%)
  Pallas kernels  40.6 us (17%)
  waiting for transfers between devices  24.7 us (10%)
  local copies, waits for them, and re-layouts  20.7 us (8%)
  between operations  13.5 us (6%)
    all_to_all x1, blocking collectives, body(): received.append(lax.all_to_all(rows, ('x', 'z'), 0, 0, tiled=True))  32.3 us
    pallas_call x4, Pallas kernels, body(): pl.pallas_call(functools.partial(hidden_kernel, half), out_shape=sds((PIE...  23.7 us
    all_to_all x1, blocking collectives, body(): returned.append(lax.all_to_all(result, ('x', 'z'), 0, 0, tiled=True))  23.1 us
    all_to_all x2, starting transfers between devices, body(): returned.append(lax.all_to_all(result, ('x', 'z'), 0, 0, tiled=True))  17.5 us
    ppermute x12, waiting for transfers between devices, turn(): return lax.ppermute(array, 'y', [(i, (i + step) % NY) for i in range(NY)])  17.4 us
    all_gather x1, blocking collectives, body(): pieces.append(lax.all_gather(hidden, 'y', axis=0))  17 us
    ppermute x12, starting transfers between devices, turn(): return lax.ppermute(array, 'y', [(i, (i + step) % NY) for i in range(NY)])  16.9 us
    unnamed x36, local copies, waits for them, and re-layouts  13.9 us
  transfers between devices with their start and end apart: 24, of which 9 were waited for; matrix products, arithmetic and copies ran while one was open for 2% of the time, Pallas kernels for 16%

profile of v9, /device:TPU:1, one launch (start us, length us, event | category | flops | bytes accessed | tf_op | source)
XLA Modules:
  0.0 244.0 jit_solution(1515535661918408953)
XLA Ops:
  11.2 12.0 %all-to-all-start = ((bf16[32,8,1024]{2,1,0:T(8,128)(2,1)}), bf16[32,8,1024]{2,1,0:T(8,128)(2,1)}, u32[]{:S(2)}, u32[]{:S(2)}) async-start(bf16[32,8,1024]{2,1,0:T(8,128)(2,1)} %bitcast.9), calls=%async_computation | async-start | bytes 1048576 | tf_op jit(solution)/shard_map/all_to_all | solution.py:234
  26.4 4.0 %dynamic-slice_bitcast_fusion = (bf16[1536,512]{1,0:T(8,128)(2,1)}, bf16[1536,512]{1,0:T(8,128)(2,1)}) fusion(bf16[2,1536,512]{2,1,0:T(8,128)(2,1)} %param.13, s32[]{:T(128)S(6)} %select_n.13, s32[]{:T(128)S(6)} %select_n.12), kind=kLoop, calls=%fused_computation | loop fusion | bytes 6291464 | tf_op jit(solution)/shard_map/jit(dynamic_index_in_dim)/squeeze | solution.py:245
  33.4 4.0 %all-to-all-done = bf16[32,8,1024]{2,1,0:T(8,128)(2,1)} async-done(((bf16[32,8,1024]{2,1,0:T(8,128)(2,1)}), bf16[32,8,1024]{2,1,0:T(8,128)(2,1)}, u32[]{:S(2)}, u32[]{:S(2)}) %all-to-all-start) | async-done | bytes 524320 | tf_op jit(solution)/shard_map/all_to_all | solution.py:234
  37.6 32.3 %all_to_all.70 = bf16[32,16,1024]{2,1,0:T(8,128)(2,1)} all-to-all(bf16[32,16,1024]{2,1,0:T(8,128)(2,1)} %bitcast.40), channel_id=1, replica_groups=mesh['y'=4,'c'=2,'x'=4,'z'=8] {'x','z'}, dimensions={0} | all-to-all | bytes 2097152 | tf_op jit(solution)/shard_map/all_to_all | solution.py:253
  71.2 3.9 %collective-permute-start.1 = (bf16[192,4096]{1,0:T(8,128)(2,1)}, bf16[192,4096]{1,0:T(8,128)(2,1)}, u32[]{:S(2)}, u32[]{:S(2)}) collective-permute-start(bf16[192,4096]{1,0:T(8,128)(2,1)} %get-tuple-element.55), channel_id=1, source_target_pairs={{0,32},{32,0},{1,33},{33,1},{2,34},{34,2},{3,35},{35,3},{4,36},{36... | collective-permute-start | bytes 4718600 | tf_op jit(solution)/shard_map/ppermute | solution.py:250
  75.6 6.6 %all-to-all-start.2 = ((bf16[32,8,1024]{2,1,0:T(8,128)(2,1)}), bf16[32,8,1024]{2,1,0:T(8,128)(2,1)}, u32[]{:S(2)}, u32[]{:S(2)}) async-start(bf16[32,8,1024]{2,1,0:T(8,128)(2,1)} %bitcast.41), calls=%async_computation.2 | async-start | bytes 1048576 | tf_op jit(solution)/shard_map/all_to_all | solution.py:253
  83.8 6.0 %shard_map.76 = bf16[256,384]{1,0:T(8,128)(2,1)S(1)} custom-call(s32[2]{0:T(128)S(1)} %pad_add_fusion.pos, bf16[4,256,1024]{2,1,0:T(8,128)(2,1)S(1)} %bitcast.38, bf16[192,4096]{1,0:T(8,128)(2,1)S(1)} %get-tuple-element.53.gate_own, bf16[192,4096]{1,0:T(8,128)(2,1)S(1)} %get-tuple-element.54.up_own, bf16[192,4096]{1,0:T(8,128)(2,1)} %collective-permute-done.1.gate_other, ...), custom_call_target="tpu_custom_call" | custom-call | flops 1610612736 | bytes 8388608 | tf_op jit(solution)/shard_map/pallas_call | solution.py:276
  89.9 17.0 %all-gather.2 = bf16[1024,384]{1,0:T(8,128)(2,1)S(1)} all-gather(bf16[256,384]{1,0:T(8,128)(2,1)S(1)} %shard_map.76), channel_id=4, replica_groups=mesh['y'=4,'c'=2,'x'=4,'z'=8] {'y'}, dimensions={0}, use_global_device_ids=true | all-gather | bytes 983040 | tf_op jit(solution)/shard_map/all_gather | solution.py:291
  110.4 23.1 %all_to_all.71 = bf16[32,8,1024]{2,1,0:T(8,128)(2,1)} all-to-all(bf16[32,8,1024]{2,1,0:T(8,128)(2,1)} %bitcast.34), channel_id=1, replica_groups=mesh['y'=4,'c'=2,'x'=4,'z'=8] {'x','z'}, dimensions={0} | all-to-all | bytes 1048576 | tf_op jit(solution)/shard_map/all_to_all | solution.py:305
  135.6 5.9 %shard_map.78.refs_0_ = bf16[256,384]{1,0:T(8,128)(2,1)S(1)} custom-call(s32[2]{0:T(128)S(1)} %pad_add_fusion.pos, bf16[4,512,1024]{2,1,0:T(8,128)(2,1)S(1)} %bitcast.31, bf16[192,4096]{1,0:T(8,128)(2,1)S(1)} %get-tuple-element.53.gate_own, bf16[192,4096]{1,0:T(8,128)(2,1)S(1)} %get-tuple-element.54.up_own, ...), custom_call_target="tpu_custom_call" | custom-call | flops 1610612736 | bytes 8388608 | tf_op jit(solution)/shard_map/pallas_call | solution.py:276
  144.3 5.9 %shard_map.79.refs_5_ = bf16[256,384]{1,0:T(8,128)(2,1)S(1)} custom-call(s32[2]{0:T(128)S(1)} %pad_add_fusion.pos, bf16[4,512,1024]{2,1,0:T(8,128)(2,1)S(1)} %bitcast.32, bf16[192,4096]{1,0:T(8,128)(2,1)S(1)} %get-tuple-element.53.gate_own, bf16[192,4096]{1,0:T(8,128)(2,1)S(1)} %get-tuple-element.54.up_own, ...), custom_call_target="tpu_custom_call" | custom-call | flops 1610612736 | bytes 8388608 | tf_op jit(solution)/shard_map/pallas_call | solution.py:276
  153.1 2.7 %collective-permute-start.6 = (bf16[128,384]{1,0:T(8,128)(2,1)S(1)}, bf16[128,384]{1,0:T(8,128)(2,1)S(1)}, u32[]{:S(2)}, u32[]{:S(2)}) collective-permute-start(bf16[128,384]{1,0:T(8,128)(2,1)S(1)} %slice.25), channel_id=1, source_target_pairs={{0,192},{64,0},{128,64},{192,128},{1,193},{65,1},{129,65},{193,129... | collective-permute-start | bytes 294920 | tf_op jit(solution)/shard_map/ppermute | solution.py:204
  155.8 6.1 %collective-permute-done.7.refs_6_ = bf16[256,384]{1,0:T(8,128)(2,1)S(1)} collective-permute-done((bf16[256,384]{1,0:T(8,128)(2,1)S(1)}, bf16[256,384]{1,0:T(8,128)(2,1)S(1)}, u32[]{:S(2)}, u32[]{:S(2)}) %collective-permute-start.7) | collective-permute-done | bytes 196640 | tf_op jit(solution)/shard_map/ppermute | solution.py:204
  162.0 2.7 %collective-permute-start.10 = (bf16[128,384]{1,0:T(8,128)(2,1)S(1)}, bf16[128,384]{1,0:T(8,128)(2,1)S(1)}, u32[]{:S(2)}, u32[]{:S(2)}) collective-permute-start(bf16[128,384]{1,0:T(8,128)(2,1)S(1)} %slice.27), channel_id=1, source_target_pairs={{0,192},{64,0},{128,64},{192,128},{1,193},{65,1},{129,65},{193,129... | collective-permute-start | bytes 294920 | tf_op jit(solution)/shard_map/ppermute | solution.py:204
  166.1 4.2 %collective-permute-done.9.refs_8_ = bf16[128,384]{1,0:T(8,128)(2,1)S(1)} collective-permute-done((bf16[128,384]{1,0:T(8,128)(2,1)S(1)}, bf16[128,384]{1,0:T(8,128)(2,1)S(1)}, u32[]{:S(2)}, u32[]{:S(2)}) %collective-permute-start.9) | collective-permute-done | bytes 98336 | tf_op jit(solution)/shard_map/ppermute | solution.py:204
  170.3 3.7 %shard_map.80 = bf16[512,1024]{1,0:T(8,128)(2,1)S(1)} custom-call(s32[2]{0:T(128)S(1)} %pad_add_fusion.pos, bf16[1536,512]{1,0:T(8,128)(2,1)S(1)} %copy-done.2, bf16[1536,512]{1,0:T(8,128)(2,1)} %collective-permute-done.down_other, bf16[256,384]{1,0:T(8,128)(2,1)S(1)} %shard_map.78.refs_0_, bf16[256,384]{1,0:T(8,128)(2,1)S(1)} %collective-permute-done.3.refs_1_, ...), custom_call_target="tpu_custom_call" | custom-call | flops 1610612736 | bytes 4194304 | tf_op jit(solution)/shard_map/pallas_call | solution.py:292
  175.1 8.2 %all-to-all-start.4 = ((bf16[32,16,1024]{2,1,0:T(8,128)(2,1)}), bf16[32,16,1024]{2,1,0:T(8,128)(2,1)}, u32[]{:S(2)}, u32[]{:S(2)}) async-start(bf16[32,16,1024]{2,1,0:T(8,128)(2,1)} %bitcast.39), calls=%async_computation.4 | async-start | bytes 2097152 | tf_op jit(solution)/shard_map/all_to_all | solution.py:305
  184.9 5.9 %shard_map.82.refs_0_ = bf16[256,384]{1,0:T(8,128)(2,1)S(1)} custom-call(s32[2]{0:T(128)S(1)} %pad_add_fusion.pos, bf16[4,256,1024]{2,1,0:T(8,128)(2,1)S(1)} %bitcast.37, bf16[192,4096]{1,0:T(8,128)(2,1)S(1)} %get-tuple-element.53.gate_own, bf16[192,4096]{1,0:T(8,128)(2,1)S(1)} %get-tuple-element.54.up_own, ...), custom_call_target="tpu_custom_call" | custom-call | flops 1610612736 | bytes 8388608 | tf_op jit(solution)/shard_map/pallas_call | solution.py:276
  193.5 3.5 %collective-permute-done.12.refs_1_ = bf16[256,384]{1,0:T(8,128)(2,1)S(1)} collective-permute-done((bf16[256,384]{1,0:T(8,128)(2,1)S(1)}, bf16[256,384]{1,0:T(8,128)(2,1)S(1)}, u32[]{:S(2)}, u32[]{:S(2)}) %collective-permute-start.12) | collective-permute-done | bytes 196640 | tf_op jit(solution)/shard_map/ppermute | solution.py:204
  197.4 2.7 %collective-permute-start.15 = (bf16[128,384]{1,0:T(8,128)(2,1)S(1)}, bf16[128,384]{1,0:T(8,128)(2,1)S(1)}, u32[]{:S(2)}, u32[]{:S(2)}) collective-permute-start(bf16[128,384]{1,0:T(8,128)(2,1)S(1)} %slice.29), channel_id=1, source_target_pairs={{0,192},{64,0},{128,64},{192,128},{1,193},{65,1},{129,65},{193,129... | collective-permute-start | bytes 294920 | tf_op jit(solution)/shard_map/ppermute | solution.py:204
  202.4 3.5 %shard_map.83 = bf16[256,1024]{1,0:T(8,128)(2,1)} custom-call(s32[2]{0:T(128)S(1)} %pad_add_fusion.pos, bf16[1536,512]{1,0:T(8,128)(2,1)S(1)} %copy-done.3, bf16[1536,512]{1,0:T(8,128)(2,1)} %collective-permute-done.down_other, bf16[256,384]{1,0:T(8,128)(2,1)S(1)} %shard_map.82.refs_0_, bf16[256,384]{1,0:T(8,128)(2,1)S(1)} %collective-permute-done.12.refs_1_, ...), custom_call_target="tpu_custom_call" | custom-call | flops 805306368 | bytes 3670016 | tf_op jit(solution)/shard_map/pallas_call | solution.py:292
  205.9 9.3 %all-to-all-start.5 = ((bf16[32,8,1024]{2,1,0:T(8,128)(2,1)}), bf16[32,8,1024]{2,1,0:T(8,128)(2,1)S(1)}, u32[]{:S(2)}, u32[]{:S(2)}) async-start(bf16[32,8,1024]{2,1,0:T(8,128)(2,1)} %bitcast.23), calls=%async_computation.5 | async-start | bytes 1048576 | tf_op jit(solution)/shard_map/all_to_all | solution.py:305
  220.2 5.5 %collective-permute-start.11 = (bf16[128,512]{1,0:T(8,128)(2,1)S(1)}, bf16[128,512]{1,0:T(8,128)(2,1)S(1)}, u32[]{:S(2)}, u32[]{:S(2)}) collective-permute-start(bf16[128,512]{1,0:T(8,128)(2,1)S(1)} %get-tuple-element.63), channel_id=1, source_target_pairs={{0,32},{32,0},{1,33},{33,1},{2,34},{34,2},{3,35},{35,3},{4,36},{36... | collective-permute-start | bytes 393224 | tf_op jit(solution)/shard_map/ppermute | solution.py:318
  227.4 8.4 %collective-permute-start.16 = (bf16[128,512]{1,0:T(8,128)(2,1)S(1)}, bf16[128,512]{1,0:T(8,128)(2,1)S(1)}, u32[]{:S(2)}, u32[]{:S(2)}) collective-permute-start(bf16[128,512]{1,0:T(8,128)(2,1)S(1)} %get-tuple-element.68), channel_id=1, source_target_pairs={{0,32},{32,0},{1,33},{33,1},{2,34},{34,2},{3,35},{35,3},{4,36},{36... | collective-permute-start | bytes 393224 | tf_op jit(solution)/shard_map/ppermute | solution.py:318
  (89 shorter events, 43.5 us)
Async XLA Ops:
  11.2 26.3 %all-to-all-start = ((bf16[32,8,1024]{2,1,0:T(8,128)(2,1)}), bf16[32,8,1024]{2,1,0:T(8,128)(2,1)}, u32[]{:S(2)}, u32[]{:S(2)}) async-start(bf16[32,8,1024]{2,1,0:T(8,128)(2,1)} %bitcast.9), calls=%async_computation | async-start | bytes 1048576 | tf_op jit(solution)/shard_map/all_to_all | solution.py:234
  23.2 48.0 %all-gather.8.cloned.1.call-start = ((), (), s32[]{:S(2)}) async-start(), calls=%async_computation.6 | async-start | bytes 2621440 | tf_op jit(solution)/shard_map/all_gather | solution.py:271
  37.5 95.9 %all-gather.10.cloned.1.call-start = ((), (), s32[]{:S(2)}) async-start(), calls=%async_computation.7 | async-start | bytes 5242880 | tf_op jit(solution)/shard_map/all_gather | solution.py:271
  71.2 11.0 %collective-permute-start.1 = (bf16[192,4096]{1,0:T(8,128)(2,1)}, bf16[192,4096]{1,0:T(8,128)(2,1)}, u32[]{:S(2)}, u32[]{:S(2)}) collective-permute-start(bf16[192,4096]{1,0:T(8,128)(2,1)} %get-tuple-element.55), channel_id=1, source_target_pairs={{0,32},{32,0},{1,33},{33,1},{2,34},{34,2},{3,35},{35,3},{4,36},{36... | collective-permute-start | bytes 4718600 | tf_op jit(solution)/shard_map/ppermute | solution.py:250
  75.1 7.2 %collective-permute-start.2 = (bf16[192,4096]{1,0:T(8,128)(2,1)}, bf16[192,4096]{1,0:T(8,128)(2,1)}, u32[]{:S(2)}, u32[]{:S(2)}) collective-permute-start(bf16[192,4096]{1,0:T(8,128)(2,1)} %get-tuple-element.56), channel_id=1, source_target_pairs={{0,32},{32,0},{1,33},{33,1},{2,34},{34,2},{3,35},{35,3},{4,36},{36... | collective-permute-start | bytes 4718600 | tf_op jit(solution)/shard_map/ppermute | solution.py:250
  75.2 31.7 %collective-permute-start = (bf16[1536,512]{1,0:T(8,128)(2,1)}, bf16[1536,512]{1,0:T(8,128)(2,1)}, u32[]{:S(2)}, u32[]{:S(2)}) collective-permute-start(bf16[1536,512]{1,0:T(8,128)(2,1)} %get-tuple-element.52), channel_id=1, source_target_pairs={{0,32},{32,0},{1,33},{33,1},{2,34},{34,2},{3,35},{35,3},{4,36},{36... | collective-permute-start | bytes 4718600 | tf_op jit(solution)/shard_map/ppermute | solution.py:250
  75.6 34.8 %all-to-all-start.2 = ((bf16[32,8,1024]{2,1,0:T(8,128)(2,1)}), bf16[32,8,1024]{2,1,0:T(8,128)(2,1)}, u32[]{:S(2)}, u32[]{:S(2)}) async-start(bf16[32,8,1024]{2,1,0:T(8,128)(2,1)} %bitcast.41), calls=%async_computation.2 | async-start | bytes 1048576 | tf_op jit(solution)/shard_map/all_to_all | solution.py:253
  82.2 101.1 %all-gather.12.cloned.1.call-start = ((), (), s32[]{:S(2)}) async-start(), calls=%async_computation.8 | async-start | bytes 2621440 | tf_op jit(solution)/shard_map/all_gather | solution.py:271
  141.5 11.4 %collective-permute-start.3 = (bf16[256,384]{1,0:T(8,128)(2,1)S(1)}, bf16[256,384]{1,0:T(8,128)(2,1)S(1)}, u32[]{:S(2)}, u32[]{:S(2)}) collective-permute-start(bf16[256,384]{1,0:T(8,128)(2,1)S(1)} %shard_map.78.refs_0_), channel_id=1, source_target_pairs={{0,64},{64,128},{128,192},{192,0},{1,65},{65,129},{129,193},{193,1... | collective-permute-start | bytes 589832 | tf_op jit(solution)/shard_map/ppermute | solution.py:204
  141.6 11.4 %collective-permute-start.4 = (bf16[256,384]{1,0:T(8,128)(2,1)S(1)}, bf16[256,384]{1,0:T(8,128)(2,1)S(1)}, u32[]{:S(2)}, u32[]{:S(2)}) collective-permute-start(bf16[256,384]{1,0:T(8,128)(2,1)S(1)} %shard_map.78.refs_0_), channel_id=1, source_target_pairs={{0,192},{64,0},{128,64},{192,128},{1,193},{65,1},{129,65},{193,129... | collective-permute-start | bytes 589832 | tf_op jit(solution)/shard_map/ppermute | solution.py:204
  150.2 11.7 %collective-permute-start.7 = (bf16[256,384]{1,0:T(8,128)(2,1)S(1)}, bf16[256,384]{1,0:T(8,128)(2,1)S(1)}, u32[]{:S(2)}, u32[]{:S(2)}) collective-permute-start(bf16[256,384]{1,0:T(8,128)(2,1)S(1)} %shard_map.79.refs_5_), channel_id=1, source_target_pairs={{0,64},{64,128},{128,192},{192,0},{1,65},{65,129},{129,193},{193,1... | collective-permute-start | bytes 589832 | tf_op jit(solution)/shard_map/ppermute | solution.py:204
  150.3 11.7 %collective-permute-start.8 = (bf16[256,384]{1,0:T(8,128)(2,1)S(1)}, bf16[256,384]{1,0:T(8,128)(2,1)S(1)}, u32[]{:S(2)}, u32[]{:S(2)}) collective-permute-start(bf16[256,384]{1,0:T(8,128)(2,1)S(1)} %shard_map.79.refs_5_), channel_id=1, source_target_pairs={{0,192},{64,0},{128,64},{192,128},{1,193},{65,1},{129,65},{193,129... | collective-permute-start | bytes 589832 | tf_op jit(solution)/shard_map/ppermute | solution.py:204
  152.9 13.2 %collective-permute-start.5 = (bf16[128,384]{1,0:T(8,128)(2,1)S(1)}, bf16[128,384]{1,0:T(8,128)(2,1)S(1)}, u32[]{:S(2)}, u32[]{:S(2)}) collective-permute-start(bf16[128,384]{1,0:T(8,128)(2,1)S(1)} %slice.24), channel_id=1, source_target_pairs={{0,64},{64,128},{128,192},{192,0},{1,65},{65,129},{129,193},{193,1... | collective-permute-start | bytes 294920 | tf_op jit(solution)/shard_map/ppermute | solution.py:204
  153.1 13.1 %collective-permute-start.6 = (bf16[128,384]{1,0:T(8,128)(2,1)S(1)}, bf16[128,384]{1,0:T(8,128)(2,1)S(1)}, u32[]{:S(2)}, u32[]{:S(2)}) collective-permute-start(bf16[128,384]{1,0:T(8,128)(2,1)S(1)} %slice.25), channel_id=1, source_target_pairs={{0,192},{64,0},{128,64},{192,128},{1,193},{65,1},{129,65},{193,129... | collective-permute-start | bytes 294920 | tf_op jit(solution)/shard_map/ppermute | solution.py:204
  161.9 8.4 %collective-permute-start.9 = (bf16[128,384]{1,0:T(8,128)(2,1)S(1)}, bf16[128,384]{1,0:T(8,128)(2,1)S(1)}, u32[]{:S(2)}, u32[]{:S(2)}) collective-permute-start(bf16[128,384]{1,0:T(8,128)(2,1)S(1)} %slice.26), channel_id=1, source_target_pairs={{0,64},{64,128},{128,192},{192,0},{1,65},{65,129},{129,193},{193,1... | collective-permute-start | bytes 294920 | tf_op jit(solution)/shard_map/ppermute | solution.py:204
  162.0 8.3 %collective-permute-start.10 = (bf16[128,384]{1,0:T(8,128)(2,1)S(1)}, bf16[128,384]{1,0:T(8,128)(2,1)S(1)}, u32[]{:S(2)}, u32[]{:S(2)}) collective-permute-start(bf16[128,384]{1,0:T(8,128)(2,1)S(1)} %slice.27), channel_id=1, source_target_pairs={{0,192},{64,0},{128,64},{192,128},{1,193},{65,1},{129,65},{193,129... | collective-permute-start | bytes 294920 | tf_op jit(solution)/shard_map/ppermute | solution.py:204
  175.1 30.8 %all-to-all-start.4 = ((bf16[32,16,1024]{2,1,0:T(8,128)(2,1)}), bf16[32,16,1024]{2,1,0:T(8,128)(2,1)}, u32[]{:S(2)}, u32[]{:S(2)}) async-start(bf16[32,16,1024]{2,1,0:T(8,128)(2,1)} %bitcast.39), calls=%async_computation.4 | async-start | bytes 2097152 | tf_op jit(solution)/shard_map/all_to_all | solution.py:305
  190.8 6.2 %collective-permute-start.12 = (bf16[256,384]{1,0:T(8,128)(2,1)S(1)}, bf16[256,384]{1,0:T(8,128)(2,1)S(1)}, u32[]{:S(2)}, u32[]{:S(2)}) collective-permute-start(bf16[256,384]{1,0:T(8,128)(2,1)S(1)} %shard_map.82.refs_0_), channel_id=1, source_target_pairs={{0,64},{64,128},{128,192},{192,0},{1,65},{65,129},{129,193},{193,1... | collective-permute-start | bytes 589832 | tf_op jit(solution)/shard_map/ppermute | solution.py:204
  190.9 6.4 %collective-permute-start.13 = (bf16[256,384]{1,0:T(8,128)(2,1)S(1)}, bf16[256,384]{1,0:T(8,128)(2,1)S(1)}, u32[]{:S(2)}, u32[]{:S(2)}) collective-permute-start(bf16[256,384]{1,0:T(8,128)(2,1)S(1)} %shard_map.82.refs_0_), channel_id=1, source_target_pairs={{0,192},{64,0},{128,64},{192,128},{1,193},{65,1},{129,65},{193,129... | collective-permute-start | bytes 589832 | tf_op jit(solution)/shard_map/ppermute | solution.py:204
  197.0 5.4 %collective-permute-start.14 = (bf16[128,384]{1,0:T(8,128)(2,1)S(1)}, bf16[128,384]{1,0:T(8,128)(2,1)S(1)}, u32[]{:S(2)}, u32[]{:S(2)}) collective-permute-start(bf16[128,384]{1,0:T(8,128)(2,1)S(1)} %slice.28), channel_id=1, source_target_pairs={{0,64},{64,128},{128,192},{192,0},{1,65},{65,129},{129,193},{193,1... | collective-permute-start | bytes 294920 | tf_op jit(solution)/shard_map/ppermute | solution.py:204
  197.4 5.0 %collective-permute-start.15 = (bf16[128,384]{1,0:T(8,128)(2,1)S(1)}, bf16[128,384]{1,0:T(8,128)(2,1)S(1)}, u32[]{:S(2)}, u32[]{:S(2)}) collective-permute-start(bf16[128,384]{1,0:T(8,128)(2,1)S(1)} %slice.29), channel_id=1, source_target_pairs={{0,192},{64,0},{128,64},{192,128},{1,193},{65,1},{129,65},{193,129... | collective-permute-start | bytes 294920 | tf_op jit(solution)/shard_map/ppermute | solution.py:204
  205.9 20.7 %all-to-all-start.5 = ((bf16[32,8,1024]{2,1,0:T(8,128)(2,1)}), bf16[32,8,1024]{2,1,0:T(8,128)(2,1)S(1)}, u32[]{:S(2)}, u32[]{:S(2)}) async-start(bf16[32,8,1024]{2,1,0:T(8,128)(2,1)} %bitcast.23), calls=%async_computation.5 | async-start | bytes 1048576 | tf_op jit(solution)/shard_map/all_to_all | solution.py:305
  220.2 15.5 %collective-permute-start.11 = (bf16[128,512]{1,0:T(8,128)(2,1)S(1)}, bf16[128,512]{1,0:T(8,128)(2,1)S(1)}, u32[]{:S(2)}, u32[]{:S(2)}) collective-permute-start(bf16[128,512]{1,0:T(8,128)(2,1)S(1)} %get-tuple-element.63), channel_id=1, source_target_pairs={{0,32},{32,0},{1,33},{33,1},{2,34},{34,2},{3,35},{35,3},{4,36},{36... | collective-permute-start | bytes 393224 | tf_op jit(solution)/shard_map/ppermute | solution.py:318
  227.4 9.4 %collective-permute-start.16 = (bf16[128,512]{1,0:T(8,128)(2,1)S(1)}, bf16[128,512]{1,0:T(8,128)(2,1)S(1)}, u32[]{:S(2)}, u32[]{:S(2)}) collective-permute-start(bf16[128,512]{1,0:T(8,128)(2,1)S(1)} %get-tuple-element.68), channel_id=1, source_target_pairs={{0,32},{32,0},{1,33},{33,1},{2,34},{34,2},{3,35},{35,3},{4,36},{36... | collective-permute-start | bytes 393224 | tf_op jit(solution)/shard_map/ppermute | solution.py:318
  (18 other events, 118.4 us)
Sparse Core Ops, SparseCore 0:
  37.6 33.5 all-gather.7
  73.0 57.1 all-gather.9
  133.6 42.8 all-gather.11

commit v10 on v8

--- a/solution.py
+++ b/solution.py
@@ -126,16 +126,24 @@
     return jnp.transpose(jnp.concatenate([low, high], axis=0)).astype(BF16)
 
 
-def hidden_kernel(half, pos, blocks, gate_own, gate_other, up_own, up_other, out):
-    quarter = blocks.shape[2]
-    rows = slice(half * PIECE, (half + 1) * PIECE)
+def hidden_kernel(
+    half, pos, blocks, gate_own, gate_other, up_own, up_other, out, held, sems
+):
+    rows = pl.ds(half * PIECE, PIECE)
+    fetches = [
+        pltpu.make_async_copy(blocks.at[y, rows, :], held.at[y], sems.at[y]) for y in range(NY)
+    ]
+    for fetch in fetches:
+        fetch.start()
+    quarter = held.shape[2]
     total = None
     for y in range(NY):
         cols = slice(y * quarter, (y + 1) * quarter)
         weights = jnp.concatenate(
             [weight[:, cols] for weight in (gate_own, up_own, gate_other, up_other)], axis=0
         )
-        term = by_rows(weights, blocks[y, rows, :])
+        fetches[y].wait()
+        term = by_rows(weights, held[y])
         total = term if y == 0 else total + term
     out[...] = activate(pos, total)
 
@@ -144,18 +152,6 @@
     cols = own.shape[1]
     for core, total in ((pos[1], own), (1 - pos[1], other)):
         out[at, pl.ds(pl.multiple_of(core * cols, cols), cols)] = total.astype(BF16)
-
-
-def down_kernel(pos, down_own, down_other, blocks, out):
-    rows, units = blocks.shape[1:]
-    own = other = None
-    for y in range(NY):
-        span = slice(y * units, (y + 1) * units)
-        own_term = times(blocks[y], down_own[span, :])
-        other_term = times(blocks[y], down_other[span, :])
-        own = own_term if y == 0 else own + own_term
-        other = other_term if y == 0 else other + other_term
-    store_columns(pos, out, slice(0, rows), own, other)
 
 
 def down_ring_kernel(pos, down_own, down_other, *refs):
@@ -264,19 +260,20 @@
             hidden = pl.pallas_call(
                 functools.partial(hidden_kernel, half),
                 out_shape=sds((PIECE, units), BF16),
-                in_specs=[SMEM] + [VMEM] * 5,
+                in_specs=[SMEM, pl.BlockSpec(memory_space=pltpu.HBM)] + [VMEM] * 4,
                 out_specs=VMEM,
-                compiler_params=params(16),
+                scratch_shapes=[
+                    pltpu.VMEM((NY, PIECE, quarter), BF16),
+                    pltpu.SemaphoreType.DMA((NY,)),
+                ],
+                compiler_params=params(50),
                 cost_estimate=cost(
                     4 * PIECE * width * units, 4 * units * width + 2 * PIECE * width
                 ),
             )(pos, blocks, own[0], others[0], own[1], others[1])
-            if size > PIECE:
-                pieces.extend(ring(hidden))
-            else:
-                pieces.append(lax.all_gather(hidden, "y", axis=0))
+            pieces.extend(ring(hidden))
         result = pl.pallas_call(
-            down_ring_kernel if size > PIECE else down_kernel,
+            down_ring_kernel,
             out_shape=sds((size, NC * cols), BF16),
             in_specs=[SMEM] + [VMEM] * (2 + len(pieces)),
             out_specs=VMEM,

time: 237 us -> 247 us (1.042)
  blocking collectives: 84.3 us -> 53.5 us
  waiting for transfers between devices: 16.9 us -> 38.9 us
  starting transfers between devices: 67.2 us -> 80.7 us
  Pallas kernels: 32.7 us -> 45.8 us
  local copies, waits for them, and re-layouts: 20.6 us -> 12.5 us
    all_gather x2 -> x0, blocking collectives: 29.6 us -> none  [body(): pieces.append(lax.all_gather(hidden, 'y', axis=0))]
    ppermute x8 -> x16, waiting for transfers between devices: 10.4 us -> 30.8 us  [turn(): return lax.ppermute(array, 'y', [(i, (i + step) % NY) for i in range(NY)])]
    pallas_call x4, Pallas kernels: 15.7 us -> 28.9 us  [body(): pl.pallas_call(functools.partial(hidden_kernel, half), out_shape=sds((PIE...]
    ppermute x8 -> x16, starting transfers between devices: 12 us -> 23.2 us  [turn(): return lax.ppermute(array, 'y', [(i, (i + step) % NY) for i in range(NY)])]
    unnamed x36 -> x28, local copies, waits for them, and re-layouts: 13.9 us -> 5.47 us
    ppermute x2, starting transfers between devices: 14.3 us -> 16.8 us  [body(): give = lax.ppermute(give, 'c', [(0, 1), (1, 0)])]
  transfers between devices with their start and end apart: 20 -> 28, of which waited for: 8 -> 11; matrix products, arithmetic and copies ran while one was open for 3% -> 3% of each run, Pallas kernels for 13% -> 18%
where the time goes in v10:
time: 247 us; the launch traced here: 246 us
  starting transfers between devices  80.7 us (33%)
  blocking collectives  53.5 us (22%)
  Pallas kernels  45.8 us (19%)
  waiting for transfers between devices  38.9 us (16%)
  between operations  13.5 us (5%)
  local copies, waits for them, and re-layouts  12.5 us (5%)
    all_to_all x1, blocking collectives, body(): received.append(lax.all_to_all(rows, ('x', 'z'), 0, 0, tiled=True))  32 us
    ppermute x16, waiting for transfers between devices, turn(): return lax.ppermute(array, 'y', [(i, (i + step) % NY) for i in range(NY)])  30.8 us
    pallas_call x4, Pallas kernels, body(): pl.pallas_call(functools.partial(hidden_kernel, half), out_shape=sds((PIE...  28.9 us
    ppermute x16, starting transfers between devices, turn(): return lax.ppermute(array, 'y', [(i, (i + step) % NY) for i in range(NY)])  23.2 us
    all_to_all x1, blocking collectives, body(): returned.append(lax.all_to_all(result, ('x', 'z'), 0, 0, tiled=True))  21.5 us
    all_to_all x2, starting transfers between devices, body(): returned.append(lax.all_to_all(result, ('x', 'z'), 0, 0, tiled=True))  17.7 us
    ppermute x2, starting transfers between devices, body(): give = lax.ppermute(give, 'c', [(0, 1), (1, 0)])  16.8 us
    all_to_all x1, starting transfers between devices, body(): received = [lax.all_to_all(first_rows, ('x', 'z'), 0, 0, tiled=True)]  12 us
  transfers between devices with their start and end apart: 28, of which 11 were waited for; matrix products, arithmetic and copies ran while one was open for 3% of the time, Pallas kernels for 18%

profile of v10, /device:TPU:1, one launch (start us, length us, event | category | flops | bytes accessed | tf_op | source)
XLA Modules:
  0.0 245.7 jit_solution(16920240424506163)
XLA Ops:
  11.2 12.0 %all-to-all-start = ((bf16[32,8,1024]{2,1,0:T(8,128)(2,1)}), bf16[32,8,1024]{2,1,0:T(8,128)(2,1)}, u32[]{:S(2)}, u32[]{:S(2)}) async-start(bf16[32,8,1024]{2,1,0:T(8,128)(2,1)} %bitcast.9), calls=%async_computation | async-start | bytes 1048576 | tf_op jit(solution)/shard_map/all_to_all | solution.py:218
  25.4 4.0 %dynamic-slice_bitcast_fusion = (bf16[1536,512]{1,0:T(8,128)(2,1)}, bf16[1536,512]{1,0:T(8,128)(2,1)}) fusion(bf16[2,1536,512]{2,1,0:T(8,128)(2,1)} %param.13, s32[]{:T(128)S(6)} %select_n.13, s32[]{:T(128)S(6)} %select_n.12), kind=kLoop, calls=%fused_computation | loop fusion | bytes 6291464 | tf_op jit(solution)/shard_map/jit(dynamic_index_in_dim)/squeeze | solution.py:229
  32.6 4.9 %all-to-all-done = bf16[32,8,1024]{2,1,0:T(8,128)(2,1)} async-done(((bf16[32,8,1024]{2,1,0:T(8,128)(2,1)}), bf16[32,8,1024]{2,1,0:T(8,128)(2,1)}, u32[]{:S(2)}, u32[]{:S(2)}) %all-to-all-start) | async-done | bytes 524320 | tf_op jit(solution)/shard_map/all_to_all | solution.py:218
  37.6 32.0 %all_to_all.70 = bf16[32,16,1024]{2,1,0:T(8,128)(2,1)} all-to-all(bf16[32,16,1024]{2,1,0:T(8,128)(2,1)S(1)} %bitcast.34), channel_id=1, replica_groups=mesh['y'=4,'c'=2,'x'=4,'z'=8] {'x','z'}, dimensions={0} | all-to-all | bytes 2097152 | tf_op jit(solution)/shard_map/all_to_all | solution.py:237
  71.2 3.6 %collective-permute-start.1 = (bf16[192,4096]{1,0:T(8,128)(2,1)}, bf16[192,4096]{1,0:T(8,128)(2,1)S(1)}, u32[]{:S(2)}, u32[]{:S(2)}) collective-permute-start(bf16[192,4096]{1,0:T(8,128)(2,1)} %get-tuple-element.54), channel_id=1, source_target_pairs={{0,32},{32,0},{1,33},{33,1},{2,34},{34,2},{3,35},{35,3},{4,36},{36... | collective-permute-start | bytes 4718600 | tf_op jit(solution)/shard_map/ppermute | solution.py:234
  75.4 6.8 %all-to-all-start.2 = ((bf16[32,8,1024]{2,1,0:T(8,128)(2,1)}), bf16[32,8,1024]{2,1,0:T(8,128)(2,1)}, u32[]{:S(2)}, u32[]{:S(2)}) async-start(bf16[32,8,1024]{2,1,0:T(8,128)(2,1)} %bitcast.35), calls=%async_computation.2 | async-start | bytes 1048576 | tf_op jit(solution)/shard_map/all_to_all | solution.py:237
  82.3 7.3 %shard_map.76.refs_0_ = bf16[256,384]{1,0:T(8,128)(2,1)S(1)} custom-call(s32[2]{0:T(128)S(1)} %pad_add_fusion.pos, bf16[4,256,1024]{2,1,0:T(8,128)(2,1)} %bitcast.43, bf16[192,4096]{1,0:T(8,128)(2,1)S(1)} %get-tuple-element.53.gate_own, bf16[192,4096]{1,0:T(8,128)(2,1)S(1)} %collective-permute-done.1.gate_other, bf16[192,4096]{1,0:T(8,128)(2,1)} %get-tuple-element.55.up_own, ...), custom_call_target="tpu_custom_call" | custom-call | flops 1610612736 | bytes 8388608 | tf_op jit(solution)/shard_map/pallas_call | solution.py:260
  92.4 9.5 %collective-permute-done.3.refs_1_ = bf16[256,384]{1,0:T(8,128)(2,1)S(1)} collective-permute-done((bf16[256,384]{1,0:T(8,128)(2,1)S(1)}, bf16[256,384]{1,0:T(8,128)(2,1)S(1)}, u32[]{:S(2)}, u32[]{:S(2)}) %collective-permute-start.3) | collective-permute-done | bytes 196640 | tf_op jit(solution)/shard_map/ppermute | solution.py:188
  104.7 4.9 %collective-permute-done.5.refs_3_ = bf16[128,384]{1,0:T(8,128)(2,1)S(1)} collective-permute-done((bf16[128,384]{1,0:T(8,128)(2,1)S(1)}, bf16[128,384]{1,0:T(8,128)(2,1)S(1)}, u32[]{:S(2)}, u32[]{:S(2)}) %collective-permute-start.5) | collective-permute-done | bytes 98336 | tf_op jit(solution)/shard_map/ppermute | solution.py:188
  113.1 21.5 %all_to_all.71 = bf16[32,8,1024]{2,1,0:T(8,128)(2,1)} all-to-all(bf16[32,8,1024]{2,1,0:T(8,128)(2,1)} %bitcast.30), channel_id=1, replica_groups=mesh['y'=4,'c'=2,'x'=4,'z'=8] {'x','z'}, dimensions={0} | all-to-all | bytes 1048576 | tf_op jit(solution)/shard_map/all_to_all | solution.py:288
  134.6 7.1 %shard_map.78.refs_0_ = bf16[256,384]{1,0:T(8,128)(2,1)S(1)} custom-call(s32[2]{0:T(128)S(1)} %pad_add_fusion.pos, bf16[4,512,1024]{2,1,0:T(8,128)(2,1)} %bitcast.39, bf16[192,4096]{1,0:T(8,128)(2,1)S(1)} %get-tuple-element.53.gate_own, bf16[192,4096]{1,0:T(8,128)(2,1)S(1)} %collective-permute-done.1.gate_other, bf16[192,4096]{1,0:T(8,128)(2,1)} %get-tuple-element.55.up_own, ...), custom_call_target="tpu_custom_call" | custom-call | flops 1610612736 | bytes 8388608 | tf_op jit(solution)/shard_map/pallas_call | solution.py:260
  144.7 7.1 %shard_map.79.refs_5_ = bf16[256,384]{1,0:T(8,128)(2,1)S(1)} custom-call(s32[2]{0:T(128)S(1)} %pad_add_fusion.pos, bf16[4,512,1024]{2,1,0:T(8,128)(2,1)} %bitcast.40, bf16[192,4096]{1,0:T(8,128)(2,1)S(1)} %get-tuple-element.53.gate_own, bf16[192,4096]{1,0:T(8,128)(2,1)S(1)} %collective-permute-done.1.gate_other, bf16[192,4096]{1,0:T(8,128)(2,1)} %get-tuple-element.55.up_own, ...), custom_call_target="tpu_custom_call" | custom-call | flops 1610612736 | bytes 8388608 | tf_op jit(solution)/shard_map/pallas_call | solution.py:260
  157.5 4.8 %collective-permute-done.11.refs_6_ = bf16[256,384]{1,0:T(8,128)(2,1)S(1)} collective-permute-done((bf16[256,384]{1,0:T(8,128)(2,1)S(1)}, bf16[256,384]{1,0:T(8,128)(2,1)S(1)}, u32[]{:S(2)}, u32[]{:S(2)}) %collective-permute-start.11) | collective-permute-done | bytes 196640 | tf_op jit(solution)/shard_map/ppermute | solution.py:188
  162.4 3.4 %collective-permute-start.14 = (bf16[128,384]{1,0:T(8,128)(2,1)S(1)}, bf16[128,384]{1,0:T(8,128)(2,1)S(1)}, u32[]{:S(2)}, u32[]{:S(2)}) collective-permute-start(bf16[128,384]{1,0:T(8,128)(2,1)S(1)} %slice.37), channel_id=1, source_target_pairs={{0,192},{64,0},{128,64},{192,128},{1,193},{65,1},{129,65},{193,129... | collective-permute-start | bytes 294920 | tf_op jit(solution)/shard_map/ppermute | solution.py:188
  166.4 4.2 %collective-permute-done.13.refs_8_ = bf16[128,384]{1,0:T(8,128)(2,1)S(1)} collective-permute-done((bf16[128,384]{1,0:T(8,128)(2,1)S(1)}, bf16[128,384]{1,0:T(8,128)(2,1)S(1)}, u32[]{:S(2)}, u32[]{:S(2)}) %collective-permute-start.13) | collective-permute-done | bytes 98336 | tf_op jit(solution)/shard_map/ppermute | solution.py:188
  170.6 3.7 %shard_map.80 = bf16[512,1024]{1,0:T(8,128)(2,1)S(1)} custom-call(s32[2]{0:T(128)S(1)} %pad_add_fusion.pos, bf16[1536,512]{1,0:T(8,128)(2,1)S(1)} %copy-done.1, bf16[1536,512]{1,0:T(8,128)(2,1)} %collective-permute-done.down_other, bf16[256,384]{1,0:T(8,128)(2,1)S(1)} %shard_map.78.refs_0_, bf16[256,384]{1,0:T(8,128)(2,1)S(1)} %collective-permute-done.7.refs_1_, ...), custom_call_target="tpu_custom_call" | custom-call | flops 1610612736 | bytes 4194304 | tf_op jit(solution)/shard_map/pallas_call | solution.py:275
  175.4 8.9 %all-to-all-start.4 = ((bf16[32,16,1024]{2,1,0:T(8,128)(2,1)}), bf16[32,16,1024]{2,1,0:T(8,128)(2,1)}, u32[]{:S(2)}, u32[]{:S(2)}) async-start(bf16[32,16,1024]{2,1,0:T(8,128)(2,1)} %bitcast.33), calls=%async_computation.4 | async-start | bytes 2097152 | tf_op jit(solution)/shard_map/all_to_all | solution.py:288
  184.3 7.3 %shard_map.82.refs_0_ = bf16[256,384]{1,0:T(8,128)(2,1)S(1)} custom-call(s32[2]{0:T(128)S(1)} %pad_add_fusion.pos, bf16[4,256,1024]{2,1,0:T(8,128)(2,1)} %bitcast.42, bf16[192,4096]{1,0:T(8,128)(2,1)S(1)} %get-tuple-element.53.gate_own, bf16[192,4096]{1,0:T(8,128)(2,1)S(1)} %collective-permute-done.1.gate_other, bf16[192,4096]{1,0:T(8,128)(2,1)} %get-tuple-element.55.up_own, ...), custom_call_target="tpu_custom_call" | custom-call | flops 1610612736 | bytes 8388608 | tf_op jit(solution)/shard_map/pallas_call | solution.py:260
  194.4 3.4 %collective-permute-done.16.refs_1_ = bf16[256,384]{1,0:T(8,128)(2,1)S(1)} collective-permute-done((bf16[256,384]{1,0:T(8,128)(2,1)S(1)}, bf16[256,384]{1,0:T(8,128)(2,1)S(1)}, u32[]{:S(2)}, u32[]{:S(2)}) %collective-permute-start.16) | collective-permute-done | bytes 196640 | tf_op jit(solution)/shard_map/ppermute | solution.py:188
  200.6 3.3 %collective-permute-done.18.refs_3_ = bf16[128,384]{1,0:T(8,128)(2,1)S(1)} collective-permute-done((bf16[128,384]{1,0:T(8,128)(2,1)S(1)}, bf16[128,384]{1,0:T(8,128)(2,1)S(1)}, u32[]{:S(2)}, u32[]{:S(2)}) %collective-permute-start.18) | collective-permute-done | bytes 98336 | tf_op jit(solution)/shard_map/ppermute | solution.py:188
  204.0 3.5 %shard_map.83 = bf16[256,1024]{1,0:T(8,128)(2,1)} custom-call(s32[2]{0:T(128)S(1)} %pad_add_fusion.pos, bf16[1536,512]{1,0:T(8,128)(2,1)S(1)} %copy-done.2, bf16[1536,512]{1,0:T(8,128)(2,1)} %collective-permute-done.down_other, bf16[256,384]{1,0:T(8,128)(2,1)S(1)} %shard_map.82.refs_0_, bf16[256,384]{1,0:T(8,128)(2,1)S(1)} %collective-permute-done.16.refs_1_, ...), custom_call_target="tpu_custom_call" | custom-call | flops 805306368 | bytes 3670016 | tf_op jit(solution)/shard_map/pallas_call | solution.py:275
  207.5 8.9 %all-to-all-start.5 = ((bf16[32,8,1024]{2,1,0:T(8,128)(2,1)}), bf16[32,8,1024]{2,1,0:T(8,128)(2,1)S(1)}, u32[]{:S(2)}, u32[]{:S(2)}) async-start(bf16[32,8,1024]{2,1,0:T(8,128)(2,1)} %bitcast.22), calls=%async_computation.5 | async-start | bytes 1048576 | tf_op jit(solution)/shard_map/all_to_all | solution.py:288
  219.3 7.8 %collective-permute-start.15 = (bf16[128,512]{1,0:T(8,128)(2,1)S(1)}, bf16[128,512]{1,0:T(8,128)(2,1)S(1)}, u32[]{:S(2)}, u32[]{:S(2)}) collective-permute-start(bf16[128,512]{1,0:T(8,128)(2,1)S(1)} %get-tuple-element.63), channel_id=1, source_target_pairs={{0,32},{32,0},{1,33},{33,1},{2,34},{34,2},{3,35},{35,3},{4,36},{36... | collective-permute-start | bytes 393224 | tf_op jit(solution)/shard_map/ppermute | solution.py:301
  228.5 9.0 %collective-permute-start.20 = (bf16[128,512]{1,0:T(8,128)(2,1)S(1)}, bf16[128,512]{1,0:T(8,128)(2,1)S(1)}, u32[]{:S(2)}, u32[]{:S(2)}) collective-permute-start(bf16[128,512]{1,0:T(8,128)(2,1)S(1)} %get-tuple-element.68), channel_id=1, source_target_pairs={{0,32},{32,0},{1,33},{33,1},{2,34},{34,2},{3,35},{35,3},{4,36},{36... | collective-permute-start | bytes 393224 | tf_op jit(solution)/shard_map/ppermute | solution.py:301
  (90 shorter events, 43.3 us)
Async XLA Ops:
  11.2 26.3 %all-to-all-start = ((bf16[32,8,1024]{2,1,0:T(8,128)(2,1)}), bf16[32,8,1024]{2,1,0:T(8,128)(2,1)}, u32[]{:S(2)}, u32[]{:S(2)}) async-start(bf16[32,8,1024]{2,1,0:T(8,128)(2,1)} %bitcast.9), calls=%async_computation | async-start | bytes 1048576 | tf_op jit(solution)/shard_map/all_to_all | solution.py:218
  23.2 48.0 %all-gather.7.cloned.1.call-start = ((), (), s32[]{:S(2)}) async-start(), calls=%async_computation.6 | async-start | bytes 2621440 | tf_op jit(solution)/shard_map/all_gather | solution.py:255
  37.5 97.0 %all-gather.9.cloned.1.call-start = ((), (), s32[]{:S(2)}) async-start(), calls=%async_computation.7 | async-start | bytes 5242880 | tf_op jit(solution)/shard_map/all_gather | solution.py:255
  71.2 11.0 %collective-permute-start.1 = (bf16[192,4096]{1,0:T(8,128)(2,1)}, bf16[192,4096]{1,0:T(8,128)(2,1)S(1)}, u32[]{:S(2)}, u32[]{:S(2)}) collective-permute-start(bf16[192,4096]{1,0:T(8,128)(2,1)} %get-tuple-element.54), channel_id=1, source_target_pairs={{0,32},{32,0},{1,33},{33,1},{2,34},{34,2},{3,35},{35,3},{4,36},{36... | collective-permute-start | bytes 4718600 | tf_op jit(solution)/shard_map/ppermute | solution.py:234
  74.9 7.4 %collective-permute-start.2 = (bf16[192,4096]{1,0:T(8,128)(2,1)}, bf16[192,4096]{1,0:T(8,128)(2,1)}, u32[]{:S(2)}, u32[]{:S(2)}) collective-permute-start(bf16[192,4096]{1,0:T(8,128)(2,1)} %get-tuple-element.56), channel_id=1, source_target_pairs={{0,32},{32,0},{1,33},{33,1},{2,34},{34,2},{3,35},{35,3},{4,36},{36... | collective-permute-start | bytes 4718600 | tf_op jit(solution)/shard_map/ppermute | solution.py:234
  75.0 29.8 %collective-permute-start = (bf16[1536,512]{1,0:T(8,128)(2,1)}, bf16[1536,512]{1,0:T(8,128)(2,1)}, u32[]{:S(2)}, u32[]{:S(2)}) collective-permute-start(bf16[1536,512]{1,0:T(8,128)(2,1)} %get-tuple-element.52), channel_id=1, source_target_pairs={{0,32},{32,0},{1,33},{33,1},{2,34},{34,2},{3,35},{35,3},{4,36},{36... | collective-permute-start | bytes 4718600 | tf_op jit(solution)/shard_map/ppermute | solution.py:234
  75.4 37.7 %all-to-all-start.2 = ((bf16[32,8,1024]{2,1,0:T(8,128)(2,1)}), bf16[32,8,1024]{2,1,0:T(8,128)(2,1)}, u32[]{:S(2)}, u32[]{:S(2)}) async-start(bf16[32,8,1024]{2,1,0:T(8,128)(2,1)} %bitcast.35), calls=%async_computation.2 | async-start | bytes 1048576 | tf_op jit(solution)/shard_map/all_to_all | solution.py:237
  82.2 102.1 %all-gather.11.cloned.1.call-start = ((), (), s32[]{:S(2)}) async-start(), calls=%async_computation.8 | async-start | bytes 2621440 | tf_op jit(solution)/shard_map/all_gather | solution.py:255
  89.6 12.2 %collective-permute-start.3 = (bf16[256,384]{1,0:T(8,128)(2,1)S(1)}, bf16[256,384]{1,0:T(8,128)(2,1)S(1)}, u32[]{:S(2)}, u32[]{:S(2)}) collective-permute-start(bf16[256,384]{1,0:T(8,128)(2,1)S(1)} %shard_map.76.refs_0_), channel_id=1, source_target_pairs={{0,64},{64,128},{128,192},{192,0},{1,65},{65,129},{129,193},{193,1... | collective-permute-start | bytes 589832 | tf_op jit(solution)/shard_map/ppermute | solution.py:188
  89.9 12.1 %collective-permute-start.4 = (bf16[256,384]{1,0:T(8,128)(2,1)S(1)}, bf16[256,384]{1,0:T(8,128)(2,1)S(1)}, u32[]{:S(2)}, u32[]{:S(2)}) collective-permute-start(bf16[256,384]{1,0:T(8,128)(2,1)S(1)} %shard_map.76.refs_0_), channel_id=1, source_target_pairs={{0,192},{64,0},{128,64},{192,128},{1,193},{65,1},{129,65},{193,129... | collective-permute-start | bytes 589832 | tf_op jit(solution)/shard_map/ppermute | solution.py:188
  101.9 7.8 %collective-permute-start.5 = (bf16[128,384]{1,0:T(8,128)(2,1)S(1)}, bf16[128,384]{1,0:T(8,128)(2,1)S(1)}, u32[]{:S(2)}, u32[]{:S(2)}) collective-permute-start(bf16[128,384]{1,0:T(8,128)(2,1)S(1)} %slice.32), channel_id=1, source_target_pairs={{0,64},{64,128},{128,192},{192,0},{1,65},{65,129},{129,193},{193,1... | collective-permute-start | bytes 294920 | tf_op jit(solution)/shard_map/ppermute | solution.py:188
  102.0 7.6 %collective-permute-start.6 = (bf16[128,384]{1,0:T(8,128)(2,1)S(1)}, bf16[128,384]{1,0:T(8,128)(2,1)S(1)}, u32[]{:S(2)}, u32[]{:S(2)}) collective-permute-start(bf16[128,384]{1,0:T(8,128)(2,1)S(1)} %slice.33), channel_id=1, source_target_pairs={{0,192},{64,0},{128,64},{192,128},{1,193},{65,1},{129,65},{193,129... | collective-permute-start | bytes 294920 | tf_op jit(solution)/shard_map/ppermute | solution.py:188
  141.8 12.8 %collective-permute-start.7 = (bf16[256,384]{1,0:T(8,128)(2,1)S(1)}, bf16[256,384]{1,0:T(8,128)(2,1)S(1)}, u32[]{:S(2)}, u32[]{:S(2)}) collective-permute-start(bf16[256,384]{1,0:T(8,128)(2,1)S(1)} %shard_map.78.refs_0_), channel_id=1, source_target_pairs={{0,64},{64,128},{128,192},{192,0},{1,65},{65,129},{129,193},{193,1... | collective-permute-start | bytes 589832 | tf_op jit(solution)/shard_map/ppermute | solution.py:188
  141.9 12.9 %collective-permute-start.8 = (bf16[256,384]{1,0:T(8,128)(2,1)S(1)}, bf16[256,384]{1,0:T(8,128)(2,1)S(1)}, u32[]{:S(2)}, u32[]{:S(2)}) collective-permute-start(bf16[256,384]{1,0:T(8,128)(2,1)S(1)} %shard_map.78.refs_0_), channel_id=1, source_target_pairs={{0,192},{64,0},{128,64},{192,128},{1,193},{65,1},{129,65},{193,129... | collective-permute-start | bytes 589832 | tf_op jit(solution)/shard_map/ppermute | solution.py:188
  151.8 10.4 %collective-permute-start.11 = (bf16[256,384]{1,0:T(8,128)(2,1)S(1)}, bf16[256,384]{1,0:T(8,128)(2,1)S(1)}, u32[]{:S(2)}, u32[]{:S(2)}) collective-permute-start(bf16[256,384]{1,0:T(8,128)(2,1)S(1)} %shard_map.79.refs_5_), channel_id=1, source_target_pairs={{0,64},{64,128},{128,192},{192,0},{1,65},{65,129},{129,193},{193,1... | collective-permute-start | bytes 589832 | tf_op jit(solution)/shard_map/ppermute | solution.py:188
  151.9 10.4 %collective-permute-start.12 = (bf16[256,384]{1,0:T(8,128)(2,1)S(1)}, bf16[256,384]{1,0:T(8,128)(2,1)S(1)}, u32[]{:S(2)}, u32[]{:S(2)}) collective-permute-start(bf16[256,384]{1,0:T(8,128)(2,1)S(1)} %shard_map.79.refs_5_), channel_id=1, source_target_pairs={{0,192},{64,0},{128,64},{192,128},{1,193},{65,1},{129,65},{193,129... | collective-permute-start | bytes 589832 | tf_op jit(solution)/shard_map/ppermute | solution.py:188
  154.6 11.8 %collective-permute-start.9 = (bf16[128,384]{1,0:T(8,128)(2,1)S(1)}, bf16[128,384]{1,0:T(8,128)(2,1)S(1)}, u32[]{:S(2)}, u32[]{:S(2)}) collective-permute-start(bf16[128,384]{1,0:T(8,128)(2,1)S(1)} %slice.34), channel_id=1, source_target_pairs={{0,64},{64,128},{128,192},{192,0},{1,65},{65,129},{129,193},{193,1... | collective-permute-start | bytes 294920 | tf_op jit(solution)/shard_map/ppermute | solution.py:188
  154.7 11.7 %collective-permute-start.10 = (bf16[128,384]{1,0:T(8,128)(2,1)S(1)}, bf16[128,384]{1,0:T(8,128)(2,1)S(1)}, u32[]{:S(2)}, u32[]{:S(2)}) collective-permute-start(bf16[128,384]{1,0:T(8,128)(2,1)S(1)} %slice.35), channel_id=1, source_target_pairs={{0,192},{64,0},{128,64},{192,128},{1,193},{65,1},{129,65},{193,129... | collective-permute-start | bytes 294920 | tf_op jit(solution)/shard_map/ppermute | solution.py:188
  162.2 8.4 %collective-permute-start.13 = (bf16[128,384]{1,0:T(8,128)(2,1)S(1)}, bf16[128,384]{1,0:T(8,128)(2,1)S(1)}, u32[]{:S(2)}, u32[]{:S(2)}) collective-permute-start(bf16[128,384]{1,0:T(8,128)(2,1)S(1)} %slice.36), channel_id=1, source_target_pairs={{0,64},{64,128},{128,192},{192,0},{1,65},{65,129},{129,193},{193,1... | collective-permute-start | bytes 294920 | tf_op jit(solution)/shard_map/ppermute | solution.py:188
  162.4 8.3 %collective-permute-start.14 = (bf16[128,384]{1,0:T(8,128)(2,1)S(1)}, bf16[128,384]{1,0:T(8,128)(2,1)S(1)}, u32[]{:S(2)}, u32[]{:S(2)}) collective-permute-start(bf16[128,384]{1,0:T(8,128)(2,1)S(1)} %slice.37), channel_id=1, source_target_pairs={{0,192},{64,0},{128,64},{192,128},{1,193},{65,1},{129,65},{193,129... | collective-permute-start | bytes 294920 | tf_op jit(solution)/shard_map/ppermute | solution.py:188
  175.4 32.1 %all-to-all-start.4 = ((bf16[32,16,1024]{2,1,0:T(8,128)(2,1)}), bf16[32,16,1024]{2,1,0:T(8,128)(2,1)}, u32[]{:S(2)}, u32[]{:S(2)}) async-start(bf16[32,16,1024]{2,1,0:T(8,128)(2,1)} %bitcast.33), calls=%async_computation.4 | async-start | bytes 2097152 | tf_op jit(solution)/shard_map/all_to_all | solution.py:288
  207.5 20.2 %all-to-all-start.5 = ((bf16[32,8,1024]{2,1,0:T(8,128)(2,1)}), bf16[32,8,1024]{2,1,0:T(8,128)(2,1)S(1)}, u32[]{:S(2)}, u32[]{:S(2)}) async-start(bf16[32,8,1024]{2,1,0:T(8,128)(2,1)} %bitcast.22), calls=%async_computation.5 | async-start | bytes 1048576 | tf_op jit(solution)/shard_map/all_to_all | solution.py:288
  219.3 18.2 %collective-permute-start.15 = (bf16[128,512]{1,0:T(8,128)(2,1)S(1)}, bf16[128,512]{1,0:T(8,128)(2,1)S(1)}, u32[]{:S(2)}, u32[]{:S(2)}) collective-permute-start(bf16[128,512]{1,0:T(8,128)(2,1)S(1)} %get-tuple-element.63), channel_id=1, source_target_pairs={{0,32},{32,0},{1,33},{33,1},{2,34},{34,2},{3,35},{35,3},{4,36},{36... | collective-permute-start | bytes 393224 | tf_op jit(solution)/shard_map/ppermute | solution.py:301
  228.5 10.0 %collective-permute-start.20 = (bf16[128,512]{1,0:T(8,128)(2,1)S(1)}, bf16[128,512]{1,0:T(8,128)(2,1)S(1)}, u32[]{:S(2)}, u32[]{:S(2)}) collective-permute-start(bf16[128,512]{1,0:T(8,128)(2,1)S(1)} %get-tuple-element.68), channel_id=1, source_target_pairs={{0,32},{32,0},{1,33},{33,1},{2,34},{34,2},{3,35},{35,3},{4,36},{36... | collective-permute-start | bytes 393224 | tf_op jit(solution)/shard_map/ppermute | solution.py:301
  (18 other events, 168.4 us)
Sparse Core Ops, SparseCore 0:
  37.6 33.5 all-gather.6
  73.0 57.1 all-gather.8
  134.7 44.5 all-gather.10
